TPU v7x, 32 devices: a whole 2x2x4 slice. The times are simulated.
32 devices in a mesh: dp: 4 (over y, x), seq: 8 (over z, core).
Axes of the slice: x: 2, y: 2, z: 4, core: 2. Of those that a mesh axis runs over, the one named last changes fastest.
Arguments:
- target: bfloat16 [1024, 16, 1024], P('seq', 'dp'), may hold values from -6 to 6
- source: bfloat16 [1024, 16, 1024], P('seq', 'dp'), may hold values from -6 to 6
- target_len: int32 [16], P('dp'), may hold values from 256 to 1024, as said below
- source_len: int32 [16], P('dp'), may hold values from 256 to 1024, as said below
- self_query: bfloat16 [1024, 1024], P('dp'), may hold values from -0.1875 to 0.1875
- self_key: bfloat16 [1024, 1024], P('dp'), may hold values from -0.1875 to 0.1875
- self_value: bfloat16 [1024, 1024], P('dp'), may hold values from -0.1875 to 0.1875
- self_output: bfloat16 [1024, 1024], P('dp'), may hold values from -3 to 3
- cross_query: bfloat16 [1024, 1024], P('dp'), may hold values from -0.1875 to 0.1875
- cross_key: bfloat16 [1024, 1024], P('dp'), may hold values from -0.1875 to 0.1875
- cross_value: bfloat16 [1024, 1024], P('dp'), may hold values from -0.1875 to 0.1875
- cross_output: bfloat16 [1024, 1024], P('dp'), may hold values from -3 to 3
- feed_in: bfloat16 [1024, 4096], P('dp'), may hold values from -0.1875 to 0.1875
- feed_out: bfloat16 [4096, 1024], P('dp'), may hold values from -0.09375 to 0.09375
- adapter_down: bfloat16 [1024, 512], P('dp'), may hold values from -0.1875 to 0.1875
- adapter_up: bfloat16 [512, 1024], P('dp'), may hold values from -0.0625 to 0.0625
- self_gain: bfloat16 [1024], P('dp'), may hold values from 0.5 to 1.5
- self_shift: bfloat16 [1024], P('dp'), may hold values from -1 to 1
- cross_gain: bfloat16 [1024], P('dp'), may hold values from 0.5 to 1.5
- cross_shift: bfloat16 [1024], P('dp'), may hold values from -1 to 1
- final_gain: bfloat16 [1024], P('dp'), may hold values from 0.5 to 1.5
- final_shift: bfloat16 [1024], P('dp'), may hold values from -1 to 1
- cotangent: bfloat16 [1024, 16, 1024], P('seq', 'dp'), may hold values from -6 to 6
Outputs:
- output: bfloat16 [1024, 16, 1024], P('seq', 'dp')
- grad_target: bfloat16 [1024, 16, 1024], P('seq', 'dp')
- grad_source: bfloat16 [1024, 16, 1024], P('seq', 'dp')
- self_query_grad: float32 [1024, 1024], P(('dp', 'seq'))
- self_key_grad: float32 [1024, 1024], P(('dp', 'seq'))
- self_value_grad: float32 [1024, 1024], P(('dp', 'seq'))
- self_output_grad: float32 [1024, 1024], P(('dp', 'seq'))
- cross_query_grad: float32 [1024, 1024], P(('dp', 'seq'))
- cross_key_grad: float32 [1024, 1024], P(('dp', 'seq'))
- cross_value_grad: float32 [1024, 1024], P(('dp', 'seq'))
- cross_output_grad: float32 [1024, 1024], P(('dp', 'seq'))
- adapter_down_grad: float32 [1024, 512], P(('dp', 'seq'))
- adapter_up_grad: float32 [512, 1024], P(('dp', 'seq'))
- self_gain_grad: float32 [1024], P(('dp', 'seq'))
- self_shift_grad: float32 [1024], P(('dp', 'seq'))
- cross_gain_grad: float32 [1024], P(('dp', 'seq'))
- cross_shift_grad: float32 [1024], P(('dp', 'seq'))
- final_gain_grad: float32 [1024], P(('dp', 'seq'))
- final_shift_grad: float32 [1024], P(('dp', 'seq'))
Inputs may be any that keep to these rules, and one draw needn't show every extreme that they name: `target_len`: of the 4 sequences on each index of dp, one has all 1024 positions. `source_len`: of the 4 sequences on each index of dp, one has all 1024 positions.
All inputs are finite; a program needn't handle non-finite values.
Results may differ from a plain program's by a relative error of at most 0.028.
Values may be sent and summed in bfloat16 or wider, within the bound.
No kernel may reach another device: no remote copies, remote signals or barrier semaphores. Data moves between devices by JAX's collectives and lax.ppermute only.
A program may use at most 576 MiB of HBM per device.

v0:
```python
import jax
import jax.numpy as jnp
from jax import lax
from jax.sharding import PartitionSpec as P

H = 16
HEAD = 64
SEQ_MB = 1


MASKED_SCORE = -1e30


def layer_norm(inputs, gain, shift):
    centre = jnp.mean(inputs, axis=-1, keepdims=True)
    centred = inputs - centre
    spread = jnp.mean(centred * centred, axis=-1, keepdims=True)
    return centred * lax.rsqrt(spread + 1e-05) * gain + shift


def gelu_exact(inputs):
    return jax.nn.gelu(inputs, approximate=False)


def product(left, right):
    return jnp.dot(left, right, preferred_element_type=jnp.float32)


def product_tn(left, right):
    return lax.dot_general(
        left, right, (((0,), (0,)), ((), ())), preferred_element_type=jnp.float32
    )


def product_nt(left, right):
    return lax.dot_general(
        left, right, (((1,), (1,)), ((), ())), preferred_element_type=jnp.float32
    )


def masked_scores(query_one, key_one, allowed, softmax_scale):
    scores = (
        jnp.einsum("bhe,lhe->hbl", query_one, key_one, preferred_element_type=jnp.float32)
        * softmax_scale
    )
    return jnp.where(allowed[None], scores, MASKED_SCORE)


def attend_forward(queries, keys_all, values_all, allowed_list, softmax_scale):
    block_rows, batch_seqs, model_width = queries.shape
    key_count = keys_all.shape[0]
    query_heads = queries.reshape(block_rows, batch_seqs, H, HEAD)
    key_heads = keys_all.reshape(key_count, batch_seqs, H, HEAD)
    value_heads = values_all.reshape(key_count, batch_seqs, H, HEAD)
    scores = masked_scores(query_heads[:, 0], key_heads[:, 0], allowed_list[0], softmax_scale)
    highest = jnp.max(scores, axis=-1, keepdims=True)
    raised = jnp.exp(scores - highest)
    summed = jnp.sum(raised, axis=-1, keepdims=True)
    weights_low = (raised / summed).astype(jnp.bfloat16)
    mixed_rows = jnp.einsum(
        "hbl,lhe->bhe", weights_low, value_heads[:, 0], preferred_element_type=jnp.float32
    )
    mixed_list = [mixed_rows.reshape(block_rows, model_width).astype(jnp.bfloat16)]
    total_list = [highest + jnp.log(summed)]
    return (jnp.stack(mixed_list, axis=1), total_list)


def attend_backward(
    queries, keys_all, values_all, total_list, grad_mixed, allowed_list, softmax_scale
):
    block_rows, batch_seqs, model_width = queries.shape
    key_count = keys_all.shape[0]
    query_heads = queries.reshape(block_rows, batch_seqs, H, HEAD)
    key_heads = keys_all.reshape(key_count, batch_seqs, H, HEAD)
    value_heads = values_all.reshape(key_count, batch_seqs, H, HEAD)
    grad_heads = grad_mixed.reshape(block_rows, batch_seqs, H, HEAD)
    scores = masked_scores(query_heads[:, 0], key_heads[:, 0], allowed_list[0], softmax_scale)
    probs_now = jnp.exp(scores - total_list[0])
    dprob = jnp.einsum(
        "bhe,lhe->hbl", grad_heads[:, 0], value_heads[:, 0], preferred_element_type=jnp.float32
    )
    centre = jnp.sum(probs_now * dprob, axis=-1, keepdims=True)
    dscore = (probs_now * (dprob - centre)).astype(jnp.bfloat16)
    dquery = (
        jnp.einsum("hbl,lhe->bhe", dscore, key_heads[:, 0], preferred_element_type=jnp.float32)
        * softmax_scale
    )
    dquery_list = [dquery.reshape(block_rows, model_width).astype(jnp.bfloat16)]
    centre_list = [centre]
    return (jnp.stack(dquery_list, axis=1), centre_list)


def row_stats(total_list, centre_list):
    totals_all = jnp.stack([item[..., 0] for item in total_list], axis=0)
    centres_all = jnp.stack([item[..., 0] for item in centre_list], axis=0)
    return jnp.stack([totals_all, centres_all], axis=0)


def key_side(keys_own, values_own, queries_all, grads_all, stats_all, allowed_list, softmax_scale):
    block_rows, batch_seqs, model_width = keys_own.shape
    query_count = queries_all.shape[0]
    query_heads = queries_all.reshape(query_count, batch_seqs, H, HEAD)
    grad_heads = grads_all.reshape(query_count, batch_seqs, H, HEAD)
    key_heads = keys_own.reshape(block_rows, batch_seqs, H, HEAD)
    value_heads = values_own.reshape(block_rows, batch_seqs, H, HEAD)
    scores = masked_scores(query_heads[:, 0], key_heads[:, 0], allowed_list[0], softmax_scale)
    probs_now = jnp.exp(scores - stats_all[0, 0][..., None])
    dprob = jnp.einsum(
        "bhe,lhe->hbl", grad_heads[:, 0], value_heads[:, 0], preferred_element_type=jnp.float32
    )
    dscore = (probs_now * (dprob - stats_all[1, 0][..., None])).astype(jnp.bfloat16)
    grad_keys = (
        jnp.einsum("hbl,bhe->lhe", dscore, query_heads[:, 0], preferred_element_type=jnp.float32)
        * softmax_scale
    )
    grad_values = jnp.einsum(
        "hbl,bhe->lhe",
        probs_now.astype(jnp.bfloat16),
        grad_heads[:, 0],
        preferred_element_type=jnp.float32,
    )
    key_list = [grad_keys.reshape(block_rows, model_width).astype(jnp.bfloat16)]
    value_list = [grad_values.reshape(block_rows, model_width).astype(jnp.bfloat16)]
    row_count = block_rows * batch_seqs
    return (
        jnp.stack(key_list, axis=1).reshape(row_count, model_width),
        jnp.stack(value_list, axis=1).reshape(row_count, model_width),
    )


def joined(collected, which):
    return jnp.concatenate([entry[which] for entry in collected], axis=0)


def body(
    target,
    source,
    target_len,
    source_len,
    self_query,
    self_key,
    self_value,
    self_output,
    cross_query,
    cross_key,
    cross_value,
    cross_output,
    feed_in,
    feed_out,
    adapter_down,
    adapter_up,
    self_gain,
    self_shift,
    cross_gain,
    cross_shift,
    final_gain,
    final_shift,
    cotangent,
):
    block_rows, seqs_here, model_width = target.shape
    batch_seqs = SEQ_MB
    micro_count = seqs_here // batch_seqs
    length = block_rows * lax.axis_size("seq")
    softmax_scale = HEAD ** (-0.5)
    key_pos = jnp.arange(length, dtype=jnp.int32)
    query_pos = lax.axis_index("seq") * block_rows + jnp.arange(block_rows, dtype=jnp.int32)
    row_count = block_rows * batch_seqs
    norm_totals = None
    left_list = []
    right_list = []
    output_list = []
    target_grads = []
    source_grads = []
    for micro_step in range(micro_count):
        gathered = (
            lax.all_gather(self_query, "dp", axis=0, tiled=True),
            lax.all_gather(self_key, "dp", axis=0, tiled=True),
            lax.all_gather(self_value, "dp", axis=0, tiled=True),
            lax.all_gather(self_output, "dp", axis=0, tiled=True),
            lax.all_gather(cross_query, "dp", axis=0, tiled=True),
            lax.all_gather(cross_key, "dp", axis=0, tiled=True),
            lax.all_gather(cross_value, "dp", axis=0, tiled=True),
            lax.all_gather(cross_output, "dp", axis=0, tiled=True),
            lax.all_gather(feed_in, "dp", axis=0, tiled=True),
            lax.all_gather(feed_out, "dp", axis=0, tiled=True),
            lax.all_gather(adapter_down, "dp", axis=0, tiled=True),
            lax.all_gather(adapter_up, "dp", axis=0, tiled=True),
            lax.all_gather(self_gain, "dp", axis=0, tiled=True),
            lax.all_gather(self_shift, "dp", axis=0, tiled=True),
            lax.all_gather(cross_gain, "dp", axis=0, tiled=True),
            lax.all_gather(cross_shift, "dp", axis=0, tiled=True),
            lax.all_gather(final_gain, "dp", axis=0, tiled=True),
            lax.all_gather(final_shift, "dp", axis=0, tiled=True),
        )
        (
            full_sq,
            full_sk,
            full_sv,
            full_so,
            full_cq,
            full_ck,
            full_cv,
            full_co,
            full_fin,
            full_fout,
            full_adown,
            full_aup,
            gain_first,
            shift_first,
            gain_second,
            shift_second,
            gain_final,
            shift_final,
        ) = gathered
        gain_first = gain_first.astype(jnp.float32)
        shift_first = shift_first.astype(jnp.float32)
        gain_second = gain_second.astype(jnp.float32)
        shift_second = shift_second.astype(jnp.float32)
        gain_final = gain_final.astype(jnp.float32)
        shift_final = shift_final.astype(jnp.float32)
        lower = micro_step * batch_seqs
        target_now = target[:, lower : lower + batch_seqs]
        source_now = source[:, lower : lower + batch_seqs]
        grad_out = (
            cotangent[:, lower : lower + batch_seqs]
            .reshape(row_count, model_width)
            .astype(jnp.float32)
        )
        target_limit = target_len[lower : lower + batch_seqs]
        source_limit = source_len[lower : lower + batch_seqs]
        self_allowed = [
            (key_pos[None, :] <= query_pos[:, None]) & (key_pos[None, :] < target_limit[0])
        ]
        cross_allowed = [(key_pos < source_limit[0])[None, :]]
        target_flat = target_now.reshape(row_count, model_width)
        source_flat = source_now.reshape(row_count, model_width)
        shape_three = (block_rows, batch_seqs, model_width)
        queries = product(target_flat, full_sq).astype(jnp.bfloat16).reshape(shape_three)
        keys_now = product(target_flat, full_sk).astype(jnp.bfloat16).reshape(shape_three)
        values_now = product(target_flat, full_sv).astype(jnp.bfloat16).reshape(shape_three)
        self_keys_all, self_values_all = (
            lax.all_gather(keys_now, "seq", axis=0, tiled=True),
            lax.all_gather(values_now, "seq", axis=0, tiled=True),
        )
        self_mixed, self_totals = attend_forward(
            queries, self_keys_all, self_values_all, self_allowed, softmax_scale
        )
        self_mixed_flat = self_mixed.reshape(row_count, model_width)
        resid_one = target_flat.astype(jnp.float32) + product(self_mixed_flat, full_so)
        first_norm = layer_norm(resid_one, gain_first, shift_first)
        first_low = first_norm.astype(jnp.bfloat16)
        cross_queries = product(first_low, full_cq).astype(jnp.bfloat16).reshape(shape_three)
        cross_keys = product(source_flat, full_ck).astype(jnp.bfloat16).reshape(shape_three)
        cross_values = product(source_flat, full_cv).astype(jnp.bfloat16).reshape(shape_three)
        cross_keys_all, cross_values_all = (
            lax.all_gather(cross_keys, "seq", axis=0, tiled=True),
            lax.all_gather(cross_values, "seq", axis=0, tiled=True),
        )
        cross_mixed, cross_totals = attend_forward(
            cross_queries, cross_keys_all, cross_values_all, cross_allowed, softmax_scale
        )
        cross_mixed_flat = cross_mixed.reshape(row_count, model_width)
        resid_two = first_norm + product(cross_mixed_flat, full_co)
        second_norm = layer_norm(resid_two, gain_second, shift_second)
        second_low = second_norm.astype(jnp.bfloat16)
        pre_ffn = product(second_low, full_fin)
        hidden_ffn = gelu_exact(pre_ffn).astype(jnp.bfloat16)
        pre_adapter = product(second_low, full_adown)
        hidden_adapter = gelu_exact(pre_adapter).astype(jnp.bfloat16)
        branch = product(hidden_ffn, full_fout) + 4.0 * product(hidden_adapter, full_aup)
        resid_three = second_norm + branch
        output_list.append(
            layer_norm(resid_three, gain_final, shift_final)
            .astype(jnp.bfloat16)
            .reshape(shape_three)
        )
        _, norm_back_three = jax.vjp(layer_norm, resid_three, gain_final, shift_final)
        grad_resid_three, grad_gain_final, grad_shift_final = norm_back_three(grad_out)
        grad_branch = grad_resid_three.astype(jnp.bfloat16)
        _, gelu_back_adapter = jax.vjp(gelu_exact, pre_adapter)
        grad_pre_adapter = gelu_back_adapter(4.0 * product_nt(grad_branch, full_aup))[0].astype(
            jnp.bfloat16
        )
        _, gelu_back_ffn = jax.vjp(gelu_exact, pre_ffn)
        grad_pre_ffn = gelu_back_ffn(product_nt(grad_branch, full_fout))[0].astype(jnp.bfloat16)
        grad_second = (
            grad_resid_three
            + product_nt(grad_pre_ffn, full_fin)
            + product_nt(grad_pre_adapter, full_adown)
        )
        _, norm_back_two = jax.vjp(layer_norm, resid_two, gain_second, shift_second)
        grad_resid_two, grad_gain_second, grad_shift_second = norm_back_two(grad_second)
        grad_resid_two_low = grad_resid_two.astype(jnp.bfloat16)
        grad_cross_mixed = (
            product_nt(grad_resid_two_low, full_co).astype(jnp.bfloat16).reshape(shape_three)
        )
        cross_keys_back, cross_values_back = (
            lax.all_gather(cross_keys, "seq", axis=0, tiled=True),
            lax.all_gather(cross_values, "seq", axis=0, tiled=True),
        )
        grad_cross_queries, cross_centres = attend_backward(
            cross_queries,
            cross_keys_back,
            cross_values_back,
            cross_totals,
            grad_cross_mixed,
            cross_allowed,
            softmax_scale,
        )
        cross_q_all, cross_g_all = (
            lax.all_gather(cross_queries, "seq", axis=0, tiled=True),
            lax.all_gather(grad_cross_mixed, "seq", axis=0, tiled=True),
        )
        cross_stats_all = lax.all_gather(
            row_stats(cross_totals, cross_centres), "seq", axis=3, tiled=True
        )
        cross_key_allowed = [(query_pos < source_limit[0])[None, :]]
        grad_cross_keys, grad_cross_values = key_side(
            cross_keys,
            cross_values,
            cross_q_all,
            cross_g_all,
            cross_stats_all,
            cross_key_allowed,
            softmax_scale,
        )
        source_grads.append(
            (product_nt(grad_cross_keys, full_ck) + product_nt(grad_cross_values, full_cv))
            .astype(jnp.bfloat16)
            .reshape(shape_three)
        )
        grad_cross_queries_flat = grad_cross_queries.reshape(row_count, model_width)
        grad_first = grad_resid_two + product_nt(grad_cross_queries_flat, full_cq)
        _, norm_back_one = jax.vjp(layer_norm, resid_one, gain_first, shift_first)
        grad_resid_one, grad_gain_first, grad_shift_first = norm_back_one(grad_first)
        grad_resid_one_low = grad_resid_one.astype(jnp.bfloat16)
        grad_self_mixed = (
            product_nt(grad_resid_one_low, full_so).astype(jnp.bfloat16).reshape(shape_three)
        )
        self_keys_back, self_values_back = (
            lax.all_gather(keys_now, "seq", axis=0, tiled=True),
            lax.all_gather(values_now, "seq", axis=0, tiled=True),
        )
        grad_queries, self_centres = attend_backward(
            queries,
            self_keys_back,
            self_values_back,
            self_totals,
            grad_self_mixed,
            self_allowed,
            softmax_scale,
        )
        self_q_all, self_g_all = (
            lax.all_gather(queries, "seq", axis=0, tiled=True),
            lax.all_gather(grad_self_mixed, "seq", axis=0, tiled=True),
        )
        self_stats_all = lax.all_gather(
            row_stats(self_totals, self_centres), "seq", axis=3, tiled=True
        )
        self_key_allowed = [
            (query_pos[None, :] <= key_pos[:, None]) & (query_pos[None, :] < target_limit[0])
        ]
        grad_keys_now, grad_values_now = key_side(
            keys_now,
            values_now,
            self_q_all,
            self_g_all,
            self_stats_all,
            self_key_allowed,
            softmax_scale,
        )
        grad_queries_flat = grad_queries.reshape(row_count, model_width)
        target_grads.append(
            (
                grad_resid_one
                + product_nt(grad_queries_flat, full_sq)
                + product_nt(grad_keys_now, full_sk)
                + product_nt(grad_values_now, full_sv)
            )
            .astype(jnp.bfloat16)
            .reshape(shape_three)
        )
        left_list.append(
            (
                target_flat,
                self_mixed_flat,
                first_low,
                source_flat,
                cross_mixed_flat,
                second_low,
                hidden_adapter,
            )
        )
        right_list.append(
            (
                grad_queries_flat,
                grad_keys_now,
                grad_values_now,
                grad_resid_one_low,
                grad_cross_queries_flat,
                grad_cross_keys,
                grad_cross_values,
                grad_resid_two_low,
                grad_pre_adapter,
                grad_branch,
            )
        )
        norm_now = (
            grad_gain_first,
            grad_shift_first,
            grad_gain_second,
            grad_shift_second,
            grad_gain_final,
            grad_shift_final,
        )
        if norm_totals is None:
            norm_totals = norm_now
        else:
            norm_totals = tuple(jax.tree.map(jnp.add, norm_totals, norm_now))
    inputs_ex, mixed_ex, first_ex, source_ex, cross_ex, second_ex, adapter_ex = (
        lax.all_to_all(joined(left_list, 0), "dp", split_axis=1, concat_axis=0, tiled=True),
        lax.all_to_all(joined(left_list, 1), "dp", split_axis=1, concat_axis=0, tiled=True),
        lax.all_to_all(joined(left_list, 2), "dp", split_axis=1, concat_axis=0, tiled=True),
        lax.all_to_all(joined(left_list, 3), "dp", split_axis=1, concat_axis=0, tiled=True),
        lax.all_to_all(joined(left_list, 4), "dp", split_axis=1, concat_axis=0, tiled=True),
        lax.all_to_all(joined(left_list, 5), "dp", split_axis=1, concat_axis=0, tiled=True),
        lax.all_to_all(joined(left_list, 6), "dp", split_axis=1, concat_axis=0, tiled=True),
    )
    (
        dq_all,
        dk_all,
        dv_all,
        dres_one_all,
        dqc_all,
        dkc_all,
        dvc_all,
        dres_two_all,
        dpre_all,
        dbranch_all,
    ) = (
        lax.all_gather(joined(right_list, 0), "dp", axis=0, tiled=True),
        lax.all_gather(joined(right_list, 1), "dp", axis=0, tiled=True),
        lax.all_gather(joined(right_list, 2), "dp", axis=0, tiled=True),
        lax.all_gather(joined(right_list, 3), "dp", axis=0, tiled=True),
        lax.all_gather(joined(right_list, 4), "dp", axis=0, tiled=True),
        lax.all_gather(joined(right_list, 5), "dp", axis=0, tiled=True),
        lax.all_gather(joined(right_list, 6), "dp", axis=0, tiled=True),
        lax.all_gather(joined(right_list, 7), "dp", axis=0, tiled=True),
        lax.all_gather(joined(right_list, 8), "dp", axis=0, tiled=True),
        lax.all_gather(joined(right_list, 9), "dp", axis=0, tiled=True),
    )
    weight_sums = (
        lax.psum_scatter(
            product_tn(inputs_ex, dq_all).astype(jnp.bfloat16),
            "seq",
            scatter_dimension=0,
            tiled=True,
        ).astype(jnp.float32),
        lax.psum_scatter(
            product_tn(inputs_ex, dk_all).astype(jnp.bfloat16),
            "seq",
            scatter_dimension=0,
            tiled=True,
        ).astype(jnp.float32),
        lax.psum_scatter(
            product_tn(inputs_ex, dv_all).astype(jnp.bfloat16),
            "seq",
            scatter_dimension=0,
            tiled=True,
        ).astype(jnp.float32),
        lax.psum_scatter(
            product_tn(mixed_ex, dres_one_all).astype(jnp.bfloat16),
            "seq",
            scatter_dimension=0,
            tiled=True,
        ).astype(jnp.float32),
        lax.psum_scatter(
            product_tn(first_ex, dqc_all).astype(jnp.bfloat16),
            "seq",
            scatter_dimension=0,
            tiled=True,
        ).astype(jnp.float32),
        lax.psum_scatter(
            product_tn(source_ex, dkc_all).astype(jnp.bfloat16),
            "seq",
            scatter_dimension=0,
            tiled=True,
        ).astype(jnp.float32),
        lax.psum_scatter(
            product_tn(source_ex, dvc_all).astype(jnp.bfloat16),
            "seq",
            scatter_dimension=0,
            tiled=True,
        ).astype(jnp.float32),
        lax.psum_scatter(
            product_tn(cross_ex, dres_two_all).astype(jnp.bfloat16),
            "seq",
            scatter_dimension=0,
            tiled=True,
        ).astype(jnp.float32),
        lax.psum_scatter(
            product_tn(second_ex, dpre_all).astype(jnp.bfloat16),
            "seq",
            scatter_dimension=0,
            tiled=True,
        ).astype(jnp.float32),
        lax.psum_scatter(
            (4.0 * product_tn(adapter_ex, dbranch_all)).astype(jnp.bfloat16),
            "seq",
            scatter_dimension=0,
            tiled=True,
        ).astype(jnp.float32),
    )
    norm_sums = (
        lax.psum_scatter(norm_totals[0], ("dp", "seq"), scatter_dimension=0, tiled=True),
        lax.psum_scatter(norm_totals[1], ("dp", "seq"), scatter_dimension=0, tiled=True),
        lax.psum_scatter(norm_totals[2], ("dp", "seq"), scatter_dimension=0, tiled=True),
        lax.psum_scatter(norm_totals[3], ("dp", "seq"), scatter_dimension=0, tiled=True),
        lax.psum_scatter(norm_totals[4], ("dp", "seq"), scatter_dimension=0, tiled=True),
        lax.psum_scatter(norm_totals[5], ("dp", "seq"), scatter_dimension=0, tiled=True),
    )
    output_all = jnp.concatenate(output_list, axis=1)
    target_grad_all = jnp.concatenate(target_grads, axis=1)
    source_grad_all = jnp.concatenate(source_grads, axis=1)
    return (
        output_all,
        target_grad_all,
        source_grad_all,
        weight_sums[0],
        weight_sums[1],
        weight_sums[2],
        weight_sums[3],
        weight_sums[4],
        weight_sums[5],
        weight_sums[6],
        weight_sums[7],
        weight_sums[8],
        weight_sums[9],
        norm_sums[0],
        norm_sums[1],
        norm_sums[2],
        norm_sums[3],
        norm_sums[4],
        norm_sums[5],
    )


def solution(mesh):
    return jax.shard_map(
        body,
        mesh=mesh,
        in_specs=(
            P("seq", "dp", None),
            P("seq", "dp", None),
            P("dp"),
            P("dp"),
            P("dp", None),
            P("dp", None),
            P("dp", None),
            P("dp", None),
            P("dp", None),
            P("dp", None),
            P("dp", None),
            P("dp", None),
            P("dp", None),
            P("dp", None),
            P("dp", None),
            P("dp", None),
            P("dp"),
            P("dp"),
            P("dp"),
            P("dp"),
            P("dp"),
            P("dp"),
            P("seq", "dp", None),
        ),
        out_specs=(
            P("seq", "dp", None),
            P("seq", "dp", None),
            P("seq", "dp", None),
            P(("dp", "seq"), None),
            P(("dp", "seq"), None),
            P(("dp", "seq"), None),
            P(("dp", "seq"), None),
            P(("dp", "seq"), None),
            P(("dp", "seq"), None),
            P(("dp", "seq"), None),
            P(("dp", "seq"), None),
            P(("dp", "seq"), None),
            P(("dp", "seq"), None),
            P(("dp", "seq")),
            P(("dp", "seq")),
            P(("dp", "seq")),
            P(("dp", "seq")),
            P(("dp", "seq")),
            P(("dp", "seq")),
        ),
        check_vma=False,
    )
```

profile of v0, /device:TPU:0, one launch (start us, length us, event | category | flops | bytes accessed | tf_op | source)
XLA Modules:
  0.0 2409.5 jit_solution(13050917351921281214)
XLA Ops:
  13.1 34.9 %all-gather.97.cloned.1.call-done = bf16[1024,1024]{1,0:T(8,128)(2,1)} async-done(((bf16[256,1024]{1,0:T(8,128)(2,1)}), bf16[1024,1024]{1,0:T(8,128)(2,1)}) %all-gather.97.cloned.1.call-update) | async-done | bytes 2097168 | tf_op jit(solution)/shard_map/all_gather | solution.py:177
  50.7 34.4 %all-gather.93.cloned.1.call-done = bf16[1024,1024]{1,0:T(8,128)(2,1)} async-done(((bf16[256,1024]{1,0:T(8,128)(2,1)}), bf16[1024,1024]{1,0:T(8,128)(2,1)}) %all-gather.93.cloned.1.call-update) | async-done | bytes 2097168 | tf_op jit(solution)/shard_map/all_gather | solution.py:178
  127.8 31.6 %all-gather.101.cloned.1.call-done = bf16[1024,1024]{1,0:T(8,128)(2,1)} async-done(((bf16[256,1024]{1,0:T(8,128)(2,1)}), bf16[1024,1024]{1,0:T(8,128)(2,1)}) %all-gather.101.cloned.1.call-update) | async-done | bytes 2097168 | tf_op jit(solution)/shard_map/all_gather | solution.py:182
  297.5 27.3 %all-gather.155.cloned.1.call-done = bf16[1024,1024]{1,0:T(8,128)(2,1)} async-done(((bf16[128,1024]{1,0:T(8,128)(2,1)}), bf16[1024,1024]{1,0:T(8,128)(2,1)}) %all-gather.155.cloned.1.call-update) | async-done | bytes 2097168 | tf_op jit(solution)/shard_map/all_gather | solution.py:242
  606.7 26.3 %all-gather.157.cloned.1.call-done = bf16[1024,1024]{1,0:T(8,128)(2,1)} async-done(((bf16[128,1024]{1,0:T(8,128)(2,1)}), bf16[1024,1024]{1,0:T(8,128)(2,1)}) %all-gather.157.cloned.1.call-update) | async-done | bytes 2097168 | tf_op jit(solution)/shard_map/all_gather | solution.py:257
  673.5 26.8 %all-gather.151.cloned.1.call-done = bf16[1024,1024]{1,0:T(8,128)(2,1)} async-done(((bf16[128,1024]{1,0:T(8,128)(2,1)}), bf16[1024,1024]{1,0:T(8,128)(2,1)}) %all-gather.151.cloned.1.call-update) | async-done | bytes 2097168 | tf_op jit(solution)/shard_map/all_gather | solution.py:256
  704.2 26.3 %all-gather.149.cloned.1.call-done = bf16[1024,1024]{1,0:T(8,128)(2,1)} async-done(((bf16[128,1024]{1,0:T(8,128)(2,1)}), bf16[1024,1024]{1,0:T(8,128)(2,1)}) %all-gather.149.cloned.1.call-update) | async-done | bytes 2097168 | tf_op jit(solution)/shard_map/all_gather | solution.py:257
  826.0 82.3 %all-gather.109.cloned.1.call-done = bf16[1024,4096]{1,0:T(8,128)(2,1)} async-done(((bf16[256,4096]{1,0:T(8,128)(2,1)}), bf16[1024,4096]{1,0:T(8,128)(2,1)}) %all-gather.109.cloned.1.call-update) | async-done | bytes 8388624 | tf_op jit(solution)/shard_map/all_gather | solution.py:184
  914.2 83.3 %all-gather.111.cloned.1.call-done = bf16[4096,1024]{1,0:T(8,128)(2,1)} async-done(((bf16[1024,1024]{1,0:T(8,128)(2,1)}), bf16[4096,1024]{1,0:T(8,128)(2,1)}) %all-gather.111.cloned.1.call-update) | async-done | bytes 8388624 | tf_op jit(solution)/shard_map/all_gather | solution.py:185
  1694.9 23.9 all-to-all-done.3
  1840.3 41.6 %all-reduce.6 = (f32[1024]{0:T(1024)S(1)}, f32[1024]{0:T(1024)S(1)}, f32[1024]{0:T(1024)S(1)}, f32[1024]{0:T(1024)S(1)}, f32[1024]{0:T(1024)S(1)}, /*index=5*/f32[1024]{0:T(1024)S(1)}) all-reduce(f32[1024]{0:T(1024)S(1)} %add_add_fusion.17, f32[1024]{0:T(1024)S(1)} %add_add_fusion.16, ...), channel_id=44, replica_groups=mesh['dp'=4,'seq'=8] {'dp','seq'}, use_global_device_ids=true, to_apply=%region_86.87.clone | all-reduce | flops 6144 | bytes 49152
  1898.7 24.3 %all-gather.129.cloned.1.call-done = bf16[2048,1024]{0,1:T(8,128)(2,1)} async-done(((bf16[512,1024]{0,1:T(8,128)(2,1)}), bf16[2048,1024]{0,1:T(8,128)(2,1)}) %all-gather.129.cloned.1.call-update) | async-done | bytes 4194320 | tf_op jit(solution)/shard_map/all_gather | solution.py:447
  1931.8 45.6 %all-gather.127.cloned.1.call-done = bf16[2048,1024]{0,1:T(8,128)(2,1)} async-done(((bf16[512,1024]{0,1:T(8,128)(2,1)}), bf16[2048,1024]{0,1:T(8,128)(2,1)}) %all-gather.127.cloned.1.call-update) | async-done | bytes 4194320 | tf_op jit(solution)/shard_map/all_gather | solution.py:446
  1985.7 46.0 %all-gather.121.cloned.1.call-done = bf16[2048,1024]{0,1:T(8,128)(2,1)} async-done(((bf16[512,1024]{0,1:T(8,128)(2,1)}), bf16[2048,1024]{0,1:T(8,128)(2,1)}) %all-gather.121.cloned.1.call-update) | async-done | bytes 4194320 | tf_op jit(solution)/shard_map/all_gather | solution.py:443
  2042.0 44.2 %all-gather.119.cloned.1.call-done = bf16[2048,1024]{0,1:T(8,128)(2,1)} async-done(((bf16[512,1024]{0,1:T(8,128)(2,1)}), bf16[2048,1024]{0,1:T(8,128)(2,1)}) %all-gather.119.cloned.1.call-update) | async-done | bytes 4194320 | tf_op jit(solution)/shard_map/all_gather | solution.py:442
  2120.3 29.5 %reduce-scatter.29.cloned.1.call-done = bf16[16,1024]{1,0:T(8,128)(2,1)} async-done(((bf16[128,1024]{1,0:T(8,128)(2,1)}), bf16[16,1024]{1,0:T(8,128)(2,1)}) %reduce-scatter.29.cloned.1.call-update) | async-done | bytes 32784 | tf_op jit(solution)/shard_map/reduce_scatter | solution.py:507
  2151.1 30.0 %reduce-scatter.25.cloned.1.call-done = bf16[32,1024]{1,0:T(8,128)(2,1)} async-done(((bf16[256,1024]{1,0:T(8,128)(2,1)}), bf16[32,1024]{1,0:T(8,128)(2,1)}) %reduce-scatter.25.cloned.1.call-update) | async-done | bytes 65552 | tf_op jit(solution)/shard_map/reduce_scatter | solution.py:495
  2182.6 29.8 %reduce-scatter.19.cloned.1.call-done = bf16[32,1024]{1,0:T(8,128)(2,1)} async-done(((bf16[256,1024]{1,0:T(8,128)(2,1)}), bf16[32,1024]{1,0:T(8,128)(2,1)}) %reduce-scatter.19.cloned.1.call-update) | async-done | bytes 65552 | tf_op jit(solution)/shard_map/reduce_scatter | solution.py:477
  2213.9 29.8 %reduce-scatter.17.cloned.1.call-done = bf16[32,1024]{1,0:T(8,128)(2,1)} async-done(((bf16[256,1024]{1,0:T(8,128)(2,1)}), bf16[32,1024]{1,0:T(8,128)(2,1)}) %reduce-scatter.17.cloned.1.call-update) | async-done | bytes 65552 | tf_op jit(solution)/shard_map/reduce_scatter | solution.py:471
  2245.2 30.0 %reduce-scatter.11.cloned.1.call-done = bf16[32,1024]{1,0:T(8,128)(2,1)} async-done(((bf16[256,1024]{1,0:T(8,128)(2,1)}), bf16[32,1024]{1,0:T(8,128)(2,1)}) %reduce-scatter.11.cloned.1.call-update) | async-done | bytes 65552 | tf_op jit(solution)/shard_map/reduce_scatter | solution.py:453
  2276.7 29.9 %reduce-scatter.23.cloned.1.call-done = bf16[32,1024]{1,0:T(8,128)(2,1)} async-done(((bf16[256,1024]{1,0:T(8,128)(2,1)}), bf16[32,1024]{1,0:T(8,128)(2,1)}) %reduce-scatter.23.cloned.1.call-update) | async-done | bytes 65552 | tf_op jit(solution)/shard_map/reduce_scatter | solution.py:489
  2308.1 30.0 %reduce-scatter.21.cloned.1.call-done = bf16[32,1024]{1,0:T(8,128)(2,1)} async-done(((bf16[256,1024]{1,0:T(8,128)(2,1)}), bf16[32,1024]{1,0:T(8,128)(2,1)}) %reduce-scatter.21.cloned.1.call-update) | async-done | bytes 65552 | tf_op jit(solution)/shard_map/reduce_scatter | solution.py:483
  2339.6 29.8 %reduce-scatter.15.cloned.1.call-done = bf16[32,1024]{1,0:T(8,128)(2,1)} async-done(((bf16[256,1024]{1,0:T(8,128)(2,1)}), bf16[32,1024]{1,0:T(8,128)(2,1)}) %reduce-scatter.15.cloned.1.call-update) | async-done | bytes 65552 | tf_op jit(solution)/shard_map/reduce_scatter | solution.py:465
  2370.9 29.8 %reduce-scatter.13.cloned.1.call-done = bf16[32,1024]{1,0:T(8,128)(2,1)} async-done(((bf16[256,1024]{1,0:T(8,128)(2,1)}), bf16[32,1024]{1,0:T(8,128)(2,1)}) %reduce-scatter.13.cloned.1.call-update) | async-done | bytes 65552 | tf_op jit(solution)/shard_map/reduce_scatter | solution.py:459
  (1658 shorter events, 1520.6 us)
Async XLA Ops:
  127.8 475.0 %all-gather.165.cloned.1.call-start = ((), (), s32[]{:S(2)}) async-start(), calls=%async_computation.63 | async-start | bytes 2359296 | tf_op jit(solution)/shard_map/all_gather | solution.py:257
  164.8 504.7 %all-gather.107.cloned.1.call-start = ((), (), s32[]{:S(2)}) async-start(), calls=%async_computation.24 | async-start | bytes 2621440 | tf_op jit(solution)/shard_map/all_gather | solution.py:183
  165.4 534.9 %all-gather.151.cloned.1.call-start = ((), (), s32[]{:S(2)}) async-start(), calls=%async_computation.56 | async-start | bytes 2359296 | tf_op jit(solution)/shard_map/all_gather | solution.py:256
  168.4 562.1 %all-gather.149.cloned.1.call-start = ((), (), s32[]{:S(2)}) async-start(), calls=%async_computation.55 | async-start | bytes 2359296 | tf_op jit(solution)/shard_map/all_gather | solution.py:257
  170.7 590.0 %all-gather.143.cloned.1.call-start = ((), (), s32[]{:S(2)}) async-start(), calls=%async_computation.52 | async-start | bytes 2359296 | tf_op jit(solution)/shard_map/all_gather | solution.py:256
  173.7 617.1 %all-gather.141.cloned.1.call-start = ((), (), s32[]{:S(2)}) async-start(), calls=%async_computation.51 | async-start | bytes 2359296 | tf_op jit(solution)/shard_map/all_gather | solution.py:257
  176.0 642.8 %all-gather.113.cloned.1.call-start = ((), (), s32[]{:S(2)}) async-start(), calls=%async_computation.27 | async-start | bytes 1310720 | tf_op jit(solution)/shard_map/all_gather | solution.py:186
  176.9 731.4 %all-gather.109.cloned.1.call-start = ((), (), s32[]{:S(2)}) async-start(), calls=%async_computation.25 | async-start | bytes 10485760 | tf_op jit(solution)/shard_map/all_gather | solution.py:184
  177.4 820.1 %all-gather.111.cloned.1.call-start = ((), (), s32[]{:S(2)}) async-start(), calls=%async_computation.26 | async-start | bytes 10485760 | tf_op jit(solution)/shard_map/all_gather | solution.py:185
  178.0 848.0 %all-gather.115.cloned.1.call-start = ((), (), s32[]{:S(2)}) async-start(), calls=%async_computation.28 | async-start | bytes 1310720 | tf_op jit(solution)/shard_map/all_gather | solution.py:187
  178.8 1078.0 %all-gather.185.cloned.1.call-start = ((), (), s32[]{:S(2)}) async-start(), calls=%async_computation.73 | async-start | bytes 2359296 | tf_op jit(solution)/shard_map/all_gather | solution.py:311
  557.0 769.6 %all-gather.189.cloned.1.call-start = ((), (), s32[]{:S(2)}) async-start(), calls=%async_computation.75 | async-start | bytes 2359296 | tf_op jit(solution)/shard_map/all_gather | solution.py:311
  652.3 678.3 %all-gather.193.cloned.1.call-start = ((), (), s32[]{:S(2)}) async-start(), calls=%async_computation.77 | async-start | bytes 2359296 | tf_op jit(solution)/shard_map/all_gather | solution.py:311
  746.5 588.1 %all-gather.197.cloned.1.call-start = ((), (), s32[]{:S(2)}) async-start(), calls=%async_computation.79 | async-start | bytes 2359296 | tf_op jit(solution)/shard_map/all_gather | solution.py:311
  806.5 607.2 %all-gather.187.cloned.1.call-start = ((), (), s32[]{:S(2)}) async-start(), calls=%async_computation.74 | async-start | bytes 2359296 | tf_op jit(solution)/shard_map/all_gather | solution.py:312
  1242.4 503.9 %all-gather.133.cloned.1.call-start = ((), (), s32[]{:S(2)}) async-start(), calls=%async_computation.45 | async-start | bytes 2621440 | tf_op jit(solution)/shard_map/all_gather | solution.py:449
  1244.3 514.5 %all-gather.135.cloned.1.call-start = ((), (), s32[]{:S(2)}) async-start(), calls=%async_computation.47 | async-start | bytes 5242880 | tf_op jit(solution)/shard_map/all_gather | solution.py:450
  1246.5 541.0 %all-gather.131.cloned.1.call-start = ((), (), s32[]{:S(2)}) async-start(), calls=%async_computation.43 | async-start | bytes 5242880 | tf_op jit(solution)/shard_map/all_gather | solution.py:448
  1247.7 562.1 %all-gather.125.cloned.1.call-start = ((), (), s32[]{:S(2)}) async-start(), calls=%async_computation.37 | async-start | bytes 5242880 | tf_op jit(solution)/shard_map/all_gather | solution.py:445
  1249.0 585.0 %all-gather.123.cloned.1.call-start = ((), (), s32[]{:S(2)}) async-start(), calls=%async_computation.35 | async-start | bytes 5242880 | tf_op jit(solution)/shard_map/all_gather | solution.py:444
  1265.7 623.2 %all-gather.117.cloned.1.call-start = ((), (), s32[]{:S(2)}) async-start(), calls=%async_computation.29 | async-start | bytes 5242880 | tf_op jit(solution)/shard_map/all_gather | solution.py:441
  1320.2 602.9 %all-gather.129.cloned.1.call-start = ((), (), s32[]{:S(2)}) async-start(), calls=%async_computation.41 | async-start | bytes 5242880 | tf_op jit(solution)/shard_map/all_gather | solution.py:447
  1452.8 524.6 %all-gather.127.cloned.1.call-start = ((), (), s32[]{:S(2)}) async-start(), calls=%async_computation.39 | async-start | bytes 5242880 | tf_op jit(solution)/shard_map/all_gather | solution.py:446
  1511.1 520.7 %all-gather.121.cloned.1.call-start = ((), (), s32[]{:S(2)}) async-start(), calls=%async_computation.33 | async-start | bytes 5242880 | tf_op jit(solution)/shard_map/all_gather | solution.py:443
  (552 other events, 23853.8 us)
Sparse Core Ops, SparseCore 0:
  9.9 38.0 all-gather.96
  49.8 35.2 all-gather.92
  87.0 35.3 all-gather.104
  124.1 35.2 all-gather.100
  161.1 35.3 all-gather.94
  259.2 34.7 all-gather.98
  477.2 34.7 all-gather.102
  634.7 34.8 all-gather.106
  820.5 87.6 all-gather.108
  909.9 87.5 all-gather.110
  1148.8 29.2 all-gather.186
  1360.7 29.9 all-gather.180
  1392.4 29.2 all-gather.170
  1514.1 34.7 all-gather.132
  1550.6 52.6 all-gather.134
  1605.0 52.6 all-gather.130
  1659.5 63.8 all-gather.124
  1725.0 80.4 all-gather.122
  1807.9 60.3 all-gather.116
  1870.0 52.9 all-gather.128
  1924.8 52.5 all-gather.126
  1979.1 52.5 all-gather.120
  2033.6 52.5 all-gather.118
  2088.4 30.4 reduce-scatter.26
  (40 shorter events, 1143.5 us)
where the time goes:
time: 2420 us; the launch traced here: 2410 us
  waiting for transfers between devices  1180 us (49%)
  matrix products  616 us (25%)
  local copies, waits for them, and re-layouts  254 us (10%)
  blocking collectives  200 us (8%)
  other arithmetic  107 us (4%)
  starting transfers between devices  30.9 us (1%)
    dot_general x44, matrix products, product_nt(): lax.dot_general(left, right, (((1,), (1,)), ((), ())), preferred_element_...  126 us
    dot_general x48, matrix products, product(): return jnp.dot(left, right, preferred_element_type=jnp.float32)  111 us
    all_gather x4, waiting for transfers between devices, body(): lax.all_gather(cross_values, 'seq', axis=0, tiled=True)  91.8 us
    all_gather x1, waiting for transfers between devices, body(): lax.all_gather(feed_out, 'dp', axis=0, tiled=True)  83.3 us
    all_gather x1, waiting for transfers between devices, body(): lax.all_gather(feed_in, 'dp', axis=0, tiled=True)  82.3 us
    all_gather x4, waiting for transfers between devices, body(): lax.all_gather(cross_keys, 'seq', axis=0, tiled=True)  79.6 us
    dot_general x8, matrix products, key_side(): jnp.einsum('hbl,bhe->lhe', dscore, query_heads[:, 0], preferred_element_t...  78.6 us
    dot_general x16, matrix products, masked_scores(): jnp.einsum('bhe,lhe->hbl', query_one, key_one, preferred_element_type=jnp...  69.5 us
  transfers between devices with their start and end apart: 71, of which 45 were waited for; matrix products, arithmetic and copies ran while one was open for 39% of the time, Pallas kernels for 0%

commit v1 on v0

v1 whole, which is shorter than its diff:
```python
import functools

import jax
import jax.numpy as jnp
from jax import lax
from jax.experimental import pallas as pl
from jax.experimental.pallas import tpu as pltpu
from jax.sharding import PartitionSpec as P

HEAD = 64
PAIR = 2 * HEAD
SCALE = HEAD ** (-0.5)
MASKED_SCORE = -1e30
NEVER = 2**30
ALWAYS = 2**29
F32 = jnp.float32
BF16 = jnp.bfloat16
VMEM_LIMIT = 56 * 1024 * 1024


def dot(left, right):
    return jnp.dot(left, right, preferred_element_type=F32)


def dot_tn(left, right):
    return lax.dot_general(left, right, (((0,), (0,)), ((), ())), preferred_element_type=F32)


def dot_nt(left, right):
    return lax.dot_general(left, right, (((1,), (1,)), ((), ())), preferred_element_type=F32)


def gelu_exact(inputs):
    return jax.nn.gelu(inputs, approximate=False)


def norm_forward(inputs, gain, shift):
    centre = jnp.mean(inputs, axis=-1, keepdims=True)
    centred = inputs - centre
    spread = jnp.mean(centred * centred, axis=-1, keepdims=True)
    rstd = lax.rsqrt(spread + 1e-05)
    return centred * rstd * gain + shift, centre, rstd


def norm_backward(inputs, centre, rstd, gain, grad):
    normed = (inputs - centre) * rstd
    grad_gain = jnp.sum(grad * normed, axis=0)
    grad_shift = jnp.sum(grad, axis=0)
    inner = grad * gain
    mean_one = jnp.mean(inner, axis=-1, keepdims=True)
    mean_two = jnp.mean(inner * normed, axis=-1, keepdims=True)
    return rstd * (inner - mean_one - normed * mean_two), grad_gain, grad_shift


def tile_of(rows):
    return 128 if rows % 128 == 0 else rows


def key_rows(tile_end, rows, block, causal):
    if not causal:
        return rows
    return min(rows, ((tile_end - 1) // block + 1) * block)


def beside(top):
    row = lax.broadcasted_iota(jnp.int32, top.shape, 0)
    zero = jnp.zeros_like(top)
    return jnp.concatenate(
        [jnp.where(row < HEAD, top, zero), jnp.where(row < HEAD, zero, top)], axis=1
    )


def below(side):
    lane = lax.broadcasted_iota(jnp.int32, side.shape, 1)
    zero = jnp.zeros_like(side)
    return jnp.concatenate(
        [jnp.where(lane < HEAD, side, zero), jnp.where(lane < HEAD, zero, side)], axis=0
    )


def heads_back(wide, tile):
    return jnp.concatenate([wide[:HEAD, :tile], wide[HEAD:, tile:]], axis=0).T


def forward_kernel(pieces, block, causal, *refs):
    query_ref, key_pos_ref, query_pos_ref = refs[:3]
    key_refs = refs[3 : 3 + pieces]
    value_refs = refs[3 + pieces : 3 + 2 * pieces]
    out_ref, total_ref = refs[3 + 2 * pieces :]
    rows = query_ref.shape[0]
    tile = tile_of(rows)
    scaled = query_ref[...].astype(F32) * SCALE
    query_up = scaled.T.astype(BF16)
    values_up = [ref[...].astype(F32).T.astype(BF16) for ref in value_refs]
    for start in range(0, rows, tile):
        keys = key_rows(start + tile, rows, block, causal)
        wide = beside(query_up[:, start : start + tile])
        query_pos = query_pos_ref[:, start : start + tile]
        limit = jnp.concatenate([query_pos, query_pos], axis=1)
        scores = []
        for piece in range(pieces):
            score = dot(key_refs[piece][:keys, :], wide)
            allowed = key_pos_ref[piece, :keys, :] <= limit
            scores.append(jnp.where(allowed, score, MASKED_SCORE))
        highest = functools.reduce(
            jnp.maximum, [jnp.max(score, axis=0, keepdims=True) for score in scores]
        )
        summed = jnp.zeros_like(highest)
        mixed = jnp.zeros((PAIR, 2 * tile), F32)
        for piece in range(pieces):
            raised = jnp.exp(scores[piece] - highest)
            summed = summed + jnp.sum(raised, axis=0, keepdims=True)
            mixed = mixed + dot(values_up[piece][:, :keys], raised.astype(BF16))
        mixed = mixed / summed
        out_ref[start : start + tile, :] = heads_back(mixed, tile).astype(BF16)
        total = highest + jnp.log(summed)
        total_ref[0, 0:1, start : start + tile] = total[:, :tile]
        total_ref[0, 1:2, start : start + tile] = total[:, tile:]


def attend_forward(queries, keys_values, key_pos, query_pos, block, causal):
    rows, width = queries.shape
    pieces = len(keys_values)
    pairs = width // PAIR
    column = pl.BlockSpec((rows, PAIR), lambda p: (0, p))
    second = pl.BlockSpec((rows, PAIR), lambda p: (0, p + pairs))
    whole_pos = pl.BlockSpec((pieces, rows, 1), lambda p: (0, 0, 0))
    row_pos = pl.BlockSpec((1, rows), lambda p: (0, 0))
    return pl.pallas_call(
        functools.partial(forward_kernel, pieces, block, causal),
        grid=(pairs,),
        in_specs=[column, whole_pos, row_pos] + [column] * pieces + [second] * pieces,
        out_specs=[column, pl.BlockSpec((1, 2, rows), lambda p: (p, 0, 0))],
        out_shape=[
            jax.ShapeDtypeStruct((rows, width), BF16),
            jax.ShapeDtypeStruct((pairs, 2, rows), F32),
        ],
        compiler_params=pltpu.CompilerParams(vmem_limit_bytes=VMEM_LIMIT),
        cost_estimate=pl.CostEstimate(
            flops=8 * rows * rows * pieces * width,
            bytes_accessed=2 * rows * width * (2 + 2 * pieces),
            transcendentals=rows * rows * pieces * width // HEAD,
        ),
    )(queries, key_pos, query_pos, *keys_values, *keys_values)


def backward_kernel(pieces, block, causal, *refs):
    query_ref, out_ref, grad_ref, total_ref, key_pos_ref, query_pos_ref = refs[:6]
    key_refs = refs[6 : 6 + pieces]
    value_refs = refs[6 + pieces : 6 + 2 * pieces]
    dquery_ref, down_ref = refs[6 + 2 * pieces : 8 + 2 * pieces]
    dother_refs = refs[8 + 2 * pieces : 7 + 3 * pieces]
    dkey_ref, dvalue_ref = refs[7 + 3 * pieces :]
    rows = query_ref.shape[0]
    tile = tile_of(rows)
    scaled = query_ref[...].astype(F32) * SCALE
    query_up = scaled.T
    scaled = scaled.astype(BF16)
    grad_up = grad_ref[...].astype(F32).T
    out_up = out_ref[...].astype(F32).T
    keys_up = [ref[...].astype(F32).T.astype(BF16) for ref in key_refs]
    product_up = grad_up * out_up
    query_up = query_up.astype(BF16)
    grad_up = grad_up.astype(BF16)
    dkey_ref[...] = jnp.zeros_like(dkey_ref)
    dvalue_ref[...] = jnp.zeros_like(dvalue_ref)
    for start in range(0, rows, tile):
        stop = start + tile
        keys = key_rows(stop, rows, block, causal)
        query_wide = beside(query_up[:, start:stop])
        grad_wide = beside(grad_up[:, start:stop])
        query_tall = below(scaled[start:stop, :])
        grad_tall = below(grad_ref[start:stop, :])
        product = product_up[:, start:stop]
        centre = jnp.concatenate(
            [
                jnp.sum(product[:HEAD], axis=0, keepdims=True),
                jnp.sum(product[HEAD:], axis=0, keepdims=True),
            ],
            axis=1,
        )
        total = jnp.concatenate(
            [total_ref[0, 0:1, start:stop], total_ref[0, 1:2, start:stop]], axis=1
        )
        query_pos = query_pos_ref[:, start:stop]
        limit = jnp.concatenate([query_pos, query_pos], axis=1)
        dquery = jnp.zeros((PAIR, 2 * tile), F32)
        for piece in range(pieces):
            score = dot(key_refs[piece][:keys, :], query_wide)
            allowed = key_pos_ref[piece, :keys, :] <= limit
            probs = jnp.exp(jnp.where(allowed, score, MASKED_SCORE) - total)
            dprob = dot(value_refs[piece][:keys, :], grad_wide)
            dscore = (probs * (dprob - centre)).astype(BF16)
            dvalue_ref[piece, :keys, :] += dot(probs.astype(BF16), grad_tall)
            dkey_ref[piece, :keys, :] += dot(dscore, query_tall)
            dquery = dquery + dot(keys_up[piece][:, :keys], dscore)
        dquery_ref[start:stop, :] = (heads_back(dquery, tile) * SCALE).astype(BF16)
    down_ref[0] = dkey_ref[0]
    down_ref[1] = dvalue_ref[0]
    for piece in range(1, pieces):
        dother_refs[piece - 1][0] = dkey_ref[piece].astype(BF16)
        dother_refs[piece - 1][1] = dvalue_ref[piece].astype(BF16)


def attend_backward(
    queries, keys_values, outputs, grads, totals, key_pos, query_pos, block, causal
):
    rows, width = queries.shape
    pieces = len(keys_values)
    pairs = width // PAIR
    column = pl.BlockSpec((rows, PAIR), lambda p: (0, p))
    second = pl.BlockSpec((rows, PAIR), lambda p: (0, p + pairs))
    whole_pos = pl.BlockSpec((pieces, rows, 1), lambda p: (0, 0, 0))
    row_pos = pl.BlockSpec((1, rows), lambda p: (0, 0))
    both = pl.BlockSpec((2, rows, PAIR), lambda p: (0, 0, p))
    return pl.pallas_call(
        functools.partial(backward_kernel, pieces, block, causal),
        grid=(pairs,),
        in_specs=[
            column,
            column,
            column,
            pl.BlockSpec((1, 2, rows), lambda p: (p, 0, 0)),
            whole_pos,
            row_pos,
        ]
        + [column] * pieces
        + [second] * pieces,
        out_specs=[column, both] + [both] * (pieces - 1),
        out_shape=[
            jax.ShapeDtypeStruct((rows, width), BF16),
            jax.ShapeDtypeStruct((2, rows, width), F32),
        ]
        + [jax.ShapeDtypeStruct((2, rows, width), BF16)] * (pieces - 1),
        scratch_shapes=[pltpu.VMEM((pieces, rows, PAIR), F32)] * 2,
        compiler_params=pltpu.CompilerParams(vmem_limit_bytes=VMEM_LIMIT),
        cost_estimate=pl.CostEstimate(
            flops=20 * rows * rows * pieces * width,
            bytes_accessed=2 * rows * width * (6 + 4 * pieces),
            transcendentals=rows * rows * pieces * width // HEAD,
        ),
    )(queries, outputs, grads, totals, key_pos, query_pos, *keys_values, *keys_values)


def place_kernel(place_ref, *refs):
    out_ref = refs[8]
    here, core = place_ref[0], place_ref[1]
    half = refs[0].shape[1]
    for which in range(2):
        side = core if which == 0 else 1 - core
        columns = pl.ds(pl.multiple_of(side * half, 128), half)
        for step in range(4):
            out_ref[here ^ step, :, columns] = refs[which * 4 + step][...]


def placed(place, parts, first, count):
    rows = parts[0].shape[0]
    half = 512
    steps = 2
    chunk = rows // steps
    out = pl.pallas_call(
        place_kernel,
        grid_spec=pltpu.PrefetchScalarGridSpec(
            num_scalar_prefetch=1,
            grid=(count, steps),
            in_specs=[pl.BlockSpec((chunk, half), lambda w, r, s: (r, first + w))] * 8,
            out_specs=pl.BlockSpec((4, chunk, 2 * half), lambda w, r, s: (0, r, w)),
        ),
        out_shape=jax.ShapeDtypeStruct((4, rows, count * 2 * half), BF16),
        compiler_params=pltpu.CompilerParams(vmem_limit_bytes=VMEM_LIMIT),
        cost_estimate=pl.CostEstimate(
            flops=0, bytes_accessed=4 * 4 * rows * count * 2 * half, transcendentals=0
        ),
    )(place, *parts)
    return out.reshape(4 * rows, count * 2 * half)


def swap_pairs(size, bit):
    return [(index, index ^ bit) for index in range(size)]


def gather_group(weights, core):
    seq = lax.axis_size("seq")
    half = weights[0].shape[1] // 2
    mine = jnp.concatenate(
        [lax.dynamic_slice_in_dim(item, core * half, half, 1) for item in weights], axis=1
    )
    other = jnp.concatenate(
        [lax.dynamic_slice_in_dim(item, (1 - core) * half, half, 1) for item in weights], axis=1
    )
    along_x, along_y, cores = swap_pairs(4, 1), swap_pairs(4, 2), swap_pairs(seq, 1)
    from_x = lax.ppermute(mine, "dp", along_x)
    from_y = lax.ppermute(mine, "dp", along_y)
    rows = mine.shape[0] // 2
    diagonal = jnp.concatenate(
        [
            lax.ppermute(from_y[:rows], "dp", along_x),
            lax.ppermute(from_x[rows:], "dp", along_y),
        ],
        axis=0,
    )
    return [mine, from_x, from_y, diagonal, other] + [
        lax.ppermute(item, "seq", cores) for item in (from_x, from_y, diagonal)
    ]


def gather_dp(item):
    return lax.all_gather(item, "dp", axis=0, tiled=True)


def gather_all(item):
    count = lax.axis_size("seq")
    rows = item.shape[0] // count
    mine = lax.dynamic_slice_in_dim(item, lax.axis_index("seq") * rows, rows, 0)
    return lax.all_gather(mine, ("dp", "seq"), axis=0, tiled=True)


def take(item, index, axis):
    return lax.dynamic_index_in_dim(item, index, axis, keepdims=False)


def halve(item, axis, bit, name, mask, kind):
    size = lax.axis_size(name)
    received = lax.ppermute(take(item, 1 - bit, axis), name, swap_pairs(size, mask))
    return (take(item, bit, axis).astype(F32) + received.astype(F32)).astype(kind)


def scatter_sum(partial):
    rows, columns = partial.shape
    dp, seq = lax.axis_size("dp"), lax.axis_size("seq")
    if dp != 4 or seq != 8:
        return lax.psum_scatter(
            partial.astype(BF16), ("dp", "seq"), scatter_dimension=0, tiled=True
        ).astype(F32)
    here, there = lax.axis_index("dp"), lax.axis_index("seq")
    along_x, along_y = here % 2, here // 2
    core, z_low, z_high = there % 2, (there // 2) % 2, there // 4
    own = rows // 32
    kind = partial.dtype
    item = partial.reshape(2, 2, 4, 2, own, columns)
    item = halve(item, 3, core, "seq", 1, kind)
    one = halve(item[..., : columns // 2], 1, along_x, "dp", 1, kind)
    two = halve(item[..., columns // 2 :], 0, along_y, "dp", 2, kind)
    one = halve(one, 0, along_y, "dp", 2, kind)
    two = halve(two, 0, along_x, "dp", 1, kind)
    item = jnp.concatenate([one, two], axis=-1).reshape(2, 2, own, columns)
    item = halve(item, 1, z_low, "seq", 2, kind)
    return halve(item, 0, z_high, "seq", 4, F32)


def scatter_norms(norms):
    dp, seq = lax.axis_size("dp"), lax.axis_size("seq")
    width = norms[0].shape[0]
    own = width // (dp * seq)
    stacked = jnp.stack(norms, axis=0)
    if dp != 4 or seq != 8:
        return lax.psum_scatter(stacked, ("dp", "seq"), scatter_dimension=1, tiled=True)
    here, there = lax.axis_index("dp"), lax.axis_index("seq")
    item = stacked.reshape(6, 32, own).swapaxes(0, 1).reshape(2, 2, 2, 2, 2, 6, own)
    item = halve(item, 4, there % 2, "seq", 1, F32)
    item = halve(item, 1, here % 2, "dp", 1, F32)
    item = halve(item, 0, here // 2, "dp", 2, F32)
    item = halve(item, 1, (there // 2) % 2, "seq", 2, F32)
    return halve(item, 0, there // 4, "seq", 4, F32)


def body(
    target,
    source,
    target_len,
    source_len,
    self_query,
    self_key,
    self_value,
    self_output,
    cross_query,
    cross_key,
    cross_value,
    cross_output,
    feed_in,
    feed_out,
    adapter_down,
    adapter_up,
    self_gain,
    self_shift,
    cross_gain,
    cross_shift,
    final_gain,
    final_shift,
    cotangent,
):
    block, seqs, width = target.shape
    dp, seq = lax.axis_size("dp"), lax.axis_size("seq")
    group = seq // seqs
    rows = seqs * block
    there = lax.axis_index("seq")
    inner, which = there % group, there // group
    apart = [[start + group * step for step in range(seqs)] for start in range(group)]

    def to_sequence(item):
        return lax.all_to_all(
            item.swapaxes(0, 1), "seq", 0, 0, axis_index_groups=apart, tiled=True
        ).reshape(rows, width)

    def from_sequence(item):
        return lax.all_to_all(
            item.reshape(seqs, block, width), "seq", 0, 0, axis_index_groups=apart, tiled=True
        ).swapaxes(0, 1)

    def near(shift):
        return [
            (k * group + c, k * group + (c + shift) % group)
            for k in range(seqs)
            for c in range(group)
        ]

    def spread(item):
        return [item] + [lax.ppermute(item, "seq", near(-s)) for s in range(1, group)]

    def collect(own, others):
        for shift, other in enumerate(others, 1):
            own = own + lax.ppermute(other, "seq", near(shift)).astype(F32)
        return own.astype(BF16)

    inputs = to_sequence(target)
    memory = to_sequence(source)
    grad_out = to_sequence(cotangent).astype(F32)

    place = jnp.stack([lax.axis_index("dp"), there % 2]).astype(jnp.int32)
    if dp == 4 and seq == 8:
        core = there % 2
        parts = gather_group([self_query, self_key, self_value], core)
        w_kv = placed(place, parts, 1, 2)
        w_q = placed(place, parts, 0, 1)
        parts = gather_group(
            [self_output, cross_query, cross_key, cross_value, cross_output], core
        )
        w_o = placed(place, parts, 0, 1)
        w_cq = placed(place, parts, 1, 1)
        w_ckv = placed(place, parts, 2, 2)
        w_co = placed(place, parts, 4, 1)
    else:
        w_q = gather_dp(self_query)
        w_kv = gather_dp(jnp.concatenate([self_key, self_value], axis=1))
        w_o = gather_dp(self_output)
        w_cq = gather_dp(cross_query)
        w_ckv = gather_dp(jnp.concatenate([cross_key, cross_value], axis=1))
        w_co = gather_dp(cross_output)
    w_in = gather_all(feed_in)
    w_out = gather_all(feed_out)
    w_down = gather_all(adapter_down)
    w_up = gather_all(adapter_up)
    norms = jnp.stack([self_gain, self_shift, cross_gain, cross_shift, final_gain, final_shift])
    norms = lax.all_gather(norms, "dp", axis=1, tiled=True).astype(F32)
    gain_one, shift_one, gain_two, shift_two, gain_three, shift_three = [
        norms[index] for index in range(6)
    ]

    local = jnp.arange(rows, dtype=jnp.int32)

    def positions(place_in_group):
        return (local // block * group + place_in_group) * block + local % block

    target_limit = take(target_len, which, 0)
    source_limit = take(source_len, which, 0)
    key_pos = jnp.stack([positions((inner + shift) % group) for shift in range(group)])
    self_keys = jnp.where(key_pos < target_limit, key_pos, NEVER)[..., None]
    cross_keys = jnp.where(key_pos < source_limit, key_pos, NEVER)[..., None]
    self_rows = positions(inner)[None]
    cross_rows = jnp.full((1, rows), ALWAYS, jnp.int32)

    kv_own = dot(inputs, w_kv).astype(BF16)
    kv_all = spread(kv_own)
    queries = dot(inputs, w_q).astype(BF16)
    mixed, totals = attend_forward(queries, kv_all, self_keys, self_rows, block, True)
    resid_one = inputs.astype(F32) + dot(mixed, w_o)
    first, centre_one, rstd_one = norm_forward(resid_one, gain_one, shift_one)
    first_low = first.astype(BF16)
    ckv_own = dot(memory, w_ckv).astype(BF16)
    ckv_all = spread(ckv_own)
    cross_q = dot(first_low, w_cq).astype(BF16)
    cross_mixed, cross_totals = attend_forward(
        cross_q, ckv_all, cross_keys, cross_rows, block, False
    )
    resid_two = first + dot(cross_mixed, w_co)
    second, centre_two, rstd_two = norm_forward(resid_two, gain_two, shift_two)
    second_low = second.astype(BF16)
    pre_ffn = dot(second_low, w_in)
    pre_adapter = dot(second_low, w_down)
    hidden_ffn, gelu_back_ffn = jax.vjp(gelu_exact, pre_ffn)
    hidden_adapter, gelu_back_adapter = jax.vjp(gelu_exact, pre_adapter)
    hidden_adapter = hidden_adapter.astype(BF16)
    resid_three = (
        second + dot(hidden_ffn.astype(BF16), w_out) + 4.0 * dot(hidden_adapter, w_up)
    )
    final, centre_three, rstd_three = norm_forward(resid_three, gain_three, shift_three)
    output = from_sequence(final.astype(BF16))

    d_three, d_gain_three, d_shift_three = norm_backward(
        resid_three, centre_three, rstd_three, gain_three, grad_out
    )
    d_branch = d_three.astype(BF16)
    d_adapter = gelu_back_adapter(4.0 * dot_nt(d_branch, w_up))[0].astype(BF16)
    d_ffn = gelu_back_ffn(dot_nt(d_branch, w_out))[0].astype(BF16)
    d_second = d_three + dot_nt(d_ffn, w_in) + dot_nt(d_adapter, w_down)
    d_two, d_gain_two, d_shift_two = norm_backward(
        resid_two, centre_two, rstd_two, gain_two, d_second
    )
    d_two_low = d_two.astype(BF16)
    grad_down = dot_tn(second_low, d_adapter).astype(BF16)
    grad_up = (4.0 * dot_tn(hidden_adapter, d_branch)).astype(BF16)
    grad_co = dot_tn(cross_mixed, d_two_low).astype(BF16)
    d_cross = dot_nt(d_two_low, w_co).astype(BF16)
    d_cq, *d_ckv = attend_backward(
        cross_q, ckv_all, cross_mixed, d_cross, cross_totals, cross_keys, cross_rows, block, False
    )
    d_ckv = collect(d_ckv[0], d_ckv[1:])
    d_first = d_two + dot_nt(d_cq, w_cq)
    d_one, d_gain_one, d_shift_one = norm_backward(
        resid_one, centre_one, rstd_one, gain_one, d_first
    )
    d_one_low = d_one.astype(BF16)
    d_mixed = dot_nt(d_one_low, w_o).astype(BF16)
    grad_source = from_sequence(
        (dot_nt(d_ckv[0], w_ckv[:, :width]) + dot_nt(d_ckv[1], w_ckv[:, width:])).astype(BF16)
    )
    grad_o = dot_tn(mixed, d_one_low).astype(BF16)
    grad_cq = dot_tn(first_low, d_cq).astype(BF16)
    grad_ck = dot_tn(memory, d_ckv[0]).astype(BF16)
    grad_cv = dot_tn(memory, d_ckv[1]).astype(BF16)
    norm_sums = scatter_norms(
        [d_gain_one, d_shift_one, d_gain_two, d_shift_two, d_gain_three, d_shift_three]
    )
    d_q, *d_kv = attend_backward(
        queries, kv_all, mixed, d_mixed, totals, self_keys, self_rows, block, True
    )
    d_kv = collect(d_kv[0], d_kv[1:])
    grad_target = from_sequence(
        (
            d_one
            + dot_nt(d_q, w_q)
            + dot_nt(d_kv[0], w_kv[:, :width])
            + dot_nt(d_kv[1], w_kv[:, width:])
        ).astype(BF16)
    )
    grad_q = dot_tn(inputs, d_q).astype(BF16)
    grad_k = dot_tn(inputs, d_kv[0]).astype(BF16)
    grad_v = dot_tn(inputs, d_kv[1]).astype(BF16)

    sum_up = scatter_sum(grad_up)
    early = scatter_sum(jnp.concatenate([grad_down, grad_co], axis=1))
    adapter_width = grad_down.shape[1]
    middle = scatter_sum(jnp.concatenate([grad_o, grad_cq, grad_ck, grad_cv], axis=1))
    late = scatter_sum(jnp.concatenate([grad_q, grad_k, grad_v], axis=1))
    return (
        output,
        grad_target,
        grad_source,
        late[:, :width],
        late[:, width : 2 * width],
        late[:, 2 * width :],
        middle[:, :width],
        middle[:, width : 2 * width],
        middle[:, 2 * width : 3 * width],
        middle[:, 3 * width :],
        early[:, adapter_width:],
        early[:, :adapter_width],
        sum_up,
        norm_sums[0],
        norm_sums[1],
        norm_sums[2],
        norm_sums[3],
        norm_sums[4],
        norm_sums[5],
    )


def solution(mesh):
    tokens = P("seq", "dp", None)
    rows = P("dp", None)
    vector = P("dp")
    both = P(("dp", "seq"), None)
    return jax.shard_map(
        body,
        mesh=mesh,
        in_specs=(tokens, tokens, vector, vector) + (rows,) * 12 + (vector,) * 6 + (tokens,),
        out_specs=(tokens,) * 3 + (both,) * 10 + (P(("dp", "seq")),) * 6,
        check_vma=False,
    )
```

time: 2420 us -> 746 us (0.31)
  waiting for transfers between devices: 1180 us -> 222 us
  matrix products: 616 us -> 145 us
  blocking collectives: 200 us -> 8.32 us
  local copies, waits for them, and re-layouts: 254 us -> 97.2 us
  Pallas kernels: 0 us -> 117 us
  other arithmetic: 107 us -> 64.2 us
  starting transfers between devices: 30.9 us -> 68.6 us
    all_gather x54 -> x4, waiting for transfers between devices: 809 us -> 25.9 us  [gather_all(): return lax.all_gather(mine, ('dp', 'seq'), axis=0, tiled=True)]
    dot_general x158 -> x31, matrix products: 616 us -> 145 us  [the longest x10 71.1 us: dot(): return jnp.dot(left, right, preferred_element_type=F32)]
    reduce_scatter x10 -> x0, waiting for transfers between devices: 288 us -> none  [the longest x1 30 us: body(): lax.psum_scatter(product_tn(inputs_ex, dq_all).astype(jnp.bfloat16), 'seq...]
    ppermute x0 -> x51, waiting for transfers between devices: none -> 184 us  [the longest x33 128 us: halve(): lax.ppermute(take(item, 1 - bit, axis), name, swap_pairs(size, mask))]
    all_gather x14 -> x1, blocking collectives: 158 us -> 8.32 us  [body(): norms = lax.all_gather(norms, 'dp', axis=1, tiled=True).astype(F32)]
    all_gather x32 -> x0, local copies, waits for them, and re-layouts: 136 us -> none  [the longest x4 25 us: body(): lax.all_gather(keys_now, 'seq', axis=0, tiled=True)]
    pallas_call x0 -> x10, Pallas kernels: none -> 117 us  [the longest x2 49.2 us: attend_backward(): pl.pallas_call(functools.partial(backward_kernel, pieces, block, causal),...]
    all_to_all x7 -> x6, waiting for transfers between devices: 72.8 us -> 11.6 us  [the longest x3 11.6 us: to_sequence(): lax.all_to_all(item.swapaxes(0, 1), 'seq', 0, 0, axis_index_groups=apart,...]
  transfers between devices with their start and end apart: 71 -> 61, of which waited for: 45 -> 19; matrix products, arithmetic and copies ran while one was open for 39% -> 33% of each run, Pallas kernels for 0% -> 12%
where the time goes in v1:
time: 746 us; the launch traced here: 738 us
  waiting for transfers between devices  222 us (30%)
  matrix products  145 us (19%)
  Pallas kernels  117 us (16%)
  local copies, waits for them, and re-layouts  97.2 us (13%)
  starting transfers between devices  68.6 us (9%)
  other arithmetic  64.2 us (9%)
  between operations  15.9 us (2%)
  blocking collectives  8.32 us (1%)
    ppermute x33, waiting for transfers between devices, halve(): lax.ppermute(take(item, 1 - bit, axis), name, swap_pairs(size, mask))  128 us
    dot_general x10, matrix products, dot(): return jnp.dot(left, right, preferred_element_type=F32)  71.1 us
    pallas_call x2, Pallas kernels, attend_backward(): pl.pallas_call(functools.partial(backward_kernel, pieces, block, causal),...  49.2 us
    dot_general x11, matrix products, dot_nt(): lax.dot_general(left, right, (((1,), (1,)), ((), ())), preferred_element_...  45.1 us
    ppermute x2, waiting for transfers between devices, gather_group(): from_y = lax.ppermute(mine, 'dp', along_y)  43.7 us
    pallas_call x2, Pallas kernels, attend_forward(): pl.pallas_call(functools.partial(forward_kernel, pieces, block, causal),...  42.6 us
    unnamed x174, local copies, waits for them, and re-layouts  32.5 us
    dot_general x10, matrix products, dot_tn(): lax.dot_general(left, right, (((0,), (0,)), ((), ())), preferred_element_...  29.2 us
  transfers between devices with their start and end apart: 61, of which 19 were waited for; matrix products, arithmetic and copies ran while one was open for 33% of the time, Pallas kernels for 12%

profile of v1, /device:TPU:0, one launch (start us, length us, event | category | flops | bytes accessed | tf_op | source)
XLA Modules:
  0.0 738.0 jit_solution(9422408281289886420)
XLA Ops:
  12.7 6.4 all-to-all-start
  31.0 43.7 %collective-permute-done.1.refs_2_ = bf16[256,1536]{1,0:T(8,128)(2,1)S(1)} collective-permute-done((bf16[256,1536]{1,0:T(8,128)(2,1)S(1)}, bf16[256,1536]{1,0:T(8,128)(2,1)S(1)}, u32[]{:S(2)}, u32[]{:S(2)}) %collective-permute-start.1) | collective-permute-done | bytes 786464 | tf_op jit(solution)/shard_map/ppermute | solution.py:293
  124.8 6.3 fusion.12.refs_3_.refs_5_.refs_6_.refs_8_
  134.3 8.3 %all_gather.15 = bf16[6,1024]{1,0:T(8,128)(2,1)S(1)} all-gather(bf16[6,256]{1,0:T(8,128)(2,1)S(1)} %stack.72), channel_id=1, replica_groups=mesh['dp'=4,'seq'=8] {'dp'}, dimensions={1}, use_global_device_ids=true | all-gather | bytes 15360 | tf_op jit(solution)/shard_map/all_gather | solution.py:454
  156.9 11.6 %all-to-all-done.1 = bf16[4,128,1024]{2,1,0:T(8,128)(2,1)} async-done(((bf16[4,128,1024]{2,1,0:T(8,128)(2,1)}), bf16[4,128,1024]{2,1,0:T(8,128)(2,1)}, u32[]{:S(2)}, u32[]{:S(2)}) %all-to-all-start.1) | async-done | bytes 1048608 | tf_op jit(solution)/shard_map/all_to_all | solution.py:401
  188.0 18.9 %shard_map.368 = (bf16[512,1024]{1,0:T(8,128)(2,1)}, f32[8,2,512]{2,1,0:T(2,128)}) custom-call(bf16[512,1024]{1,0:T(8,128)(2,1)} %fusion.38.refs_0_, s32[2,512,1]{2,1,0:T(8,128)} %get-tuple-element.144.refs_1_.refs_4_, s32[1,512]{1,0:T(1,128)} %multiply_add_fusion.3.refs_2_.refs_5_, bf16[512,2048]{1,0:T(8,128)(2,1)} %fusion.12.refs_3_.refs_5_.refs_6_.refs_8_, ...), custom_call_target="tpu_custom_call" | custom-call | flops 4294967296 | bytes 6291456 | tf_op jit(solution)/shard_map/pallas_call | solution.py:129
  215.0 23.7 %shard_map.372 = (bf16[512,1024]{1,0:T(8,128)(2,1)}, f32[8,2,512]{2,1,0:T(2,128)}) custom-call(bf16[512,1024]{1,0:T(8,128)(2,1)} %convolution_convert_fusion.8.refs_0_, s32[2,512,1]{2,1,0:T(8,128)} %get-tuple-element.143.refs_1_.refs_4_, s32[1,512]{1,0:T(1,128)} %broadcast_in_dim.8.refs_2_.refs_5_, bf16[512,2048]{1,0:T(8,128)(2,1)} %copy-done.64, ...), custom_call_target="tpu_custom_call" | custom-call | flops 4294967296 | bytes 6291456 | tf_op jit(solution)/shard_map/pallas_call | solution.py:129
  248.8 25.3 %fusion = (f32[512,4096]{1,0:T(8,128)}, f32[512,4096]{1,0:T(8,128)}) fusion(bf16[512,1024]{1,0:T(8,128)(2,1)} %fusion.33, bf16[1024,4096]{1,0:T(8,128)(2,1)} %all-gather.5.cloned.1.call-done), kind=kOutput, calls=%fused_computation.1 | convolution fusion | flops 4424990720 | bytes 26214400 | tf_op jit(solution)/shard_map/dot_general | solution.py:22
  274.2 14.0 %fusion.8 = f32[512,1024]{1,0:T(8,128)} fusion(bf16[4096,1024]{1,0:T(8,128)(2,1)} %all-gather.7.cloned.1.call-done, f32[512,4096]{1,0:T(8,128)} %get-tuple-element.188, f32[512,4096]{1,0:T(8,128)} %get-tuple-element.189), kind=kOutput, calls=%fused_computation.23 | convolution fusion | flops 4301258752 | bytes 27262976 | tf_op jit(solution)/shard_map/dot_general | solution.py:22
  288.2 25.9 %all-gather.11.cloned.1.call-done = bf16[512,1024]{1,0:T(8,128)(2,1)} async-done(((bf16[16,1024]{1,0:T(8,128)(2,1)}), bf16[512,1024]{1,0:T(8,128)(2,1)}) %all-gather.11.cloned.1.call-update) | async-done | bytes 1048592 | tf_op jit(solution)/shard_map/all_gather | solution.py:315
  324.5 18.7 %fusion.10 = f32[512,1024]{1,0:T(8,128)} fusion(bf16[1024,4096]{1,0:T(8,128)(2,1)} %all-gather.5.cloned.1.call-done, f32[512,4096]{1,0:T(8,128)} %get-tuple-element.188, f32[512,4096]{1,0:T(8,128)} %get-tuple-element.189, bf16[4096,1024]{1,0:T(8,128)(2,1)} %all-gather.7.cloned.1.call-done, f32[512,1024]{1,0:T(8,128)} %copy-done.5), kind=kOutput, calls=%fused_computation.28 | convolution fusion | flops 8619819008 | bytes 37748736 | tf_op jit(solution)/shard_map/dot_general | solution.py:30
  357.1 27.1 %shard_map.374 = (bf16[512,1024]{1,0:T(8,128)(2,1)}, f32[2,512,1024]{2,1,0:T(8,128)}, bf16[2,512,1024]{2,1,0:T(8,128)(2,1)}) custom-call(bf16[512,1024]{1,0:T(8,128)(2,1)} %convolution_convert_fusion.8.refs_0_, bf16[512,1024]{1,0:T(8,128)(2,1)} %get-tuple-element.30.refs_1_, bf16[512,1024]{1,0:T(8,128)(2,1)} %convolution_convert_fusion.7.refs_2_, ...), custom_call_target="tpu_custom_call" | custom-call | flops 10737418240 | bytes 14680064 | tf_op jit(solution)/shard_map/pallas_call | solution.py:216
  412.3 22.0 %shard_map.375 = (bf16[512,1024]{1,0:T(8,128)(2,1)}, f32[2,512,1024]{2,1,0:T(8,128)}, bf16[2,512,1024]{2,1,0:T(8,128)(2,1)}) custom-call(bf16[512,1024]{1,0:T(8,128)(2,1)} %fusion.38.refs_0_, bf16[512,1024]{1,0:T(8,128)(2,1)} %get-tuple-element.29.refs_1_, bf16[512,1024]{1,0:T(8,128)(2,1)} %convolution_convert_fusion.6.refs_2_, ...), custom_call_target="tpu_custom_call" | custom-call | flops 10737418240 | bytes 14680064 | tf_op jit(solution)/shard_map/pallas_call | solution.py:216
  449.7 21.5 %collective-permute-done.50 = f32[6,32]{1,0:T(8,128)S(1)} collective-permute-done((f32[6,32]{1,0:T(8,128)S(1)}, f32[6,32]{1,0:T(8,128)S(1)}, u32[]{:S(2)}, u32[]{:S(2)}) %collective-permute-start.50) | collective-permute-done | bytes 800 | tf_op jit(solution)/shard_map/ppermute | solution.py:324
  529.8 11.8 %copy.209 = bf16[1024,4096]{1,0:T(8,128)(2,1)} copy(bf16[1024,4096]{0,1:T(8,128)(2,1)} %pad_maximum_fusion) | data formatting | bytes 16777216 | tf_op jit(solution)/shard_map/concatenate | solution.py:553
  546.6 13.6 %pad_maximum_fusion.1 = bf16[1024,3072]{0,1:T(8,128)(2,1)} fusion(bf16[1024,1024]{0,1:T(8,128)(2,1)S(1)} %copy-done.41, bf16[1024,1024]{0,1:T(8,128)(2,1)S(1)} %copy-done.42, bf16[1024,1024]{0,1:T(8,128)(2,1)S(1)} %copy-done.35), kind=kLoop, calls=%fused_computation.20 | loop fusion | flops 18874368 | bytes 12582912 | tf_op jit(solution)/shard_map/concatenate | solution.py:554
  560.1 8.6 %copy.207 = bf16[1024,3072]{1,0:T(8,128)(2,1)} copy(bf16[1024,3072]{0,1:T(8,128)(2,1)} %pad_maximum_fusion.1) | data formatting | bytes 12582912 | tf_op jit(solution)/shard_map/concatenate | solution.py:554
  593.5 10.2 %collective-permute-done.37 = bf16[2,32,1536]{2,1,0:T(8,128)(2,1)S(1)} collective-permute-done((bf16[2,32,1536]{2,1,0:T(8,128)(2,1)S(1)}, bf16[2,32,1536]{2,1,0:T(8,128)(2,1)S(1)}, u32[]{:S(2)}, u32[]{:S(2)}) %collective-permute-start.37) | collective-permute-done | bytes 196640 | tf_op jit(solution)/shard_map/ppermute | solution.py:324
  608.6 6.1 all-to-all-start.4
  624.6 20.2 %collective-permute-done.38 = bf16[32,1536]{1,0:T(8,128)(2,1)S(1)} collective-permute-done((bf16[32,1536]{1,0:T(8,128)(2,1)S(1)}, bf16[32,1536]{1,0:T(8,128)(2,1)S(1)}, u32[]{:S(2)}, u32[]{:S(2)}) %collective-permute-start.38) | collective-permute-done | bytes 98336 | tf_op jit(solution)/shard_map/ppermute | solution.py:324
  667.7 20.7 %collective-permute-done.26 = bf16[2,4,32,2048]{3,2,1,0:T(8,128)(2,1)S(1)} collective-permute-done((bf16[2,4,32,2048]{3,2,1,0:T(8,128)(2,1)S(1)}, bf16[2,4,32,2048]{3,2,1,0:T(8,128)(2,1)S(1)}, u32[]{:S(2)}, u32[]{:S(2)}) %collective-permute-start.26) | collective-permute-done | bytes 1048608 | tf_op jit(solution)/shard_map/ppermute | solution.py:324
  690.8 10.5 %collective-permute-done.27 = bf16[4,32,2048]{2,1,0:T(8,128)(2,1)S(1)} collective-permute-done((bf16[4,32,2048]{2,1,0:T(8,128)(2,1)S(1)}, bf16[4,32,2048]{2,1,0:T(8,128)(2,1)S(1)}, u32[]{:S(2)}, u32[]{:S(2)}) %collective-permute-start.27) | collective-permute-done | bytes 524320 | tf_op jit(solution)/shard_map/ppermute | solution.py:324
  702.7 15.1 %collective-permute-done.30 = bf16[2,32,4096]{2,1,0:T(8,128)(2,1)S(1)} collective-permute-done((bf16[2,32,4096]{2,1,0:T(8,128)(2,1)S(1)}, bf16[2,32,4096]{2,1,0:T(8,128)(2,1)S(1)}, u32[]{:S(2)}, u32[]{:S(2)}) %collective-permute-start.30) | collective-permute-done | bytes 524320 | tf_op jit(solution)/shard_map/ppermute | solution.py:324
  718.8 11.3 %collective-permute-done.31 = bf16[32,4096]{1,0:T(8,128)(2,1)S(1)} collective-permute-done((bf16[32,4096]{1,0:T(8,128)(2,1)S(1)}, bf16[32,4096]{1,0:T(8,128)(2,1)S(1)}, u32[]{:S(2)}, u32[]{:S(2)}) %collective-permute-start.31) | collective-permute-done | bytes 262176 | tf_op jit(solution)/shard_map/ppermute | solution.py:324
  (468 shorter events, 320.4 us)
Async XLA Ops:
  7.2 236.0 %all-gather.9.cloned.1.call-start = ((), (), s32[]{:S(2)}) async-start(), calls=%async_computation.8 | async-start | bytes 1081344 | tf_op jit(solution)/shard_map/all_gather | solution.py:315
  8.8 240.0 %all-gather.5.cloned.1.call-start = ((), (), s32[]{:S(2)}) async-start(), calls=%async_computation.6 | async-start | bytes 8650752 | tf_op jit(solution)/shard_map/all_gather | solution.py:315
  9.6 264.6 %all-gather.7.cloned.1.call-start = ((), (), s32[]{:S(2)}) async-start(), calls=%async_computation.7 | async-start | bytes 8650752 | tf_op jit(solution)/shard_map/all_gather | solution.py:315
  12.7 66.4 %all-to-all-start = ((bf16[4,128,1024]{2,1,0:T(8,128)(2,1)}), bf16[4,128,1024]{2,1,0:T(8,128)(2,1)}, u32[]{:S(2)}, u32[]{:S(2)}) async-start(bf16[4,128,1024]{2,1,0:T(8,128)(2,1)} %bitcast.327), calls=%async_computation | async-start | bytes 2097152 | tf_op jit(solution)/shard_map/all_to_all | solution.py:401
  25.2 62.2 %collective-permute-start.9 = (bf16[256,2560]{1,0:T(8,128)(2,1)}, bf16[256,2560]{1,0:T(8,128)(2,1)S(1)}, u32[]{:S(2)}, u32[]{:S(2)}) collective-permute-start(bf16[256,2560]{1,0:T(8,128)(2,1)} %get-tuple-element.152.refs_0_), channel_id=1, source_target_pairs={{0,16},{8,24},{16,0},{24,8},{1,17},{9,25},{17,1},{25,9},{2,18},{10... | collective-permute-start | bytes 3932168 | tf_op jit(solution)/shard_map/ppermute | solution.py:293
  28.4 46.3 %collective-permute-start.1 = (bf16[256,1536]{1,0:T(8,128)(2,1)S(1)}, bf16[256,1536]{1,0:T(8,128)(2,1)S(1)}, u32[]{:S(2)}, u32[]{:S(2)}) collective-permute-start(bf16[256,1536]{1,0:T(8,128)(2,1)S(1)} %pad_maximum_fusion.4.refs_0_), channel_id=1, source_target_pairs={{0,16},{8,24},{16,0},{24,8},{1,17},{9,25},{17,1},{25,9},{2,18},{10... | collective-permute-start | bytes 2359304 | tf_op jit(solution)/shard_map/ppermute | solution.py:293
  28.9 64.9 %collective-permute-start.8 = (bf16[256,2560]{1,0:T(8,128)(2,1)}, bf16[256,2560]{1,0:T(8,128)(2,1)S(1)}, u32[]{:S(2)}, u32[]{:S(2)}) collective-permute-start(bf16[256,2560]{1,0:T(8,128)(2,1)} %get-tuple-element.152.refs_0_), channel_id=1, source_target_pairs={{0,8},{8,0},{16,24},{24,16},{1,9},{9,1},{17,25},{25,17},{2,10},{10... | collective-permute-start | bytes 3932168 | tf_op jit(solution)/shard_map/ppermute | solution.py:292
  30.4 53.5 %collective-permute-start = (bf16[256,1536]{1,0:T(8,128)(2,1)S(1)}, bf16[256,1536]{1,0:T(8,128)(2,1)}, u32[]{:S(2)}, u32[]{:S(2)}) collective-permute-start(bf16[256,1536]{1,0:T(8,128)(2,1)S(1)} %pad_maximum_fusion.4.refs_0_), channel_id=1, source_target_pairs={{0,8},{8,0},{16,24},{24,16},{1,9},{9,1},{17,25},{25,17},{2,10},{10... | collective-permute-start | bytes 2359304 | tf_op jit(solution)/shard_map/ppermute | solution.py:292
  79.1 40.6 %all-to-all-start.3 = ((bf16[4,128,1024]{2,1,0:T(8,128)(2,1)}), bf16[4,128,1024]{2,1,0:T(8,128)(2,1)}, u32[]{:S(2)}, u32[]{:S(2)}) async-start(bf16[4,128,1024]{2,1,0:T(8,128)(2,1)} %bitcast.350), calls=%async_computation.3 | async-start | bytes 2097152 | tf_op jit(solution)/shard_map/all_to_all | solution.py:401
  104.8 46.5 %collective-permute-start.12 = (bf16[256,2560]{1,0:T(8,128)(2,1)S(1)}, bf16[256,2560]{1,0:T(8,128)(2,1)}, u32[]{:S(2)}, u32[]{:S(2)}) collective-permute-start(bf16[256,2560]{1,0:T(8,128)(2,1)S(1)} %collective-permute-done.8.refs_1_), channel_id=1, source_target_pairs={{0,1},{1,0},{2,3},{3,2},{4,5},{5,4},{6,7},{7,6},{8,9},{9,8},{10,11... | collective-permute-start | bytes 3932168 | tf_op jit(solution)/shard_map/ppermute | solution.py:303
  110.9 40.4 %collective-permute-start.13 = (bf16[256,2560]{1,0:T(8,128)(2,1)S(1)}, bf16[256,2560]{1,0:T(8,128)(2,1)}, u32[]{:S(2)}, u32[]{:S(2)}) collective-permute-start(bf16[256,2560]{1,0:T(8,128)(2,1)S(1)} %collective-permute-done.9.refs_2_), channel_id=1, source_target_pairs={{0,1},{1,0},{2,3},{3,2},{4,5},{5,4},{6,7},{7,6},{8,9},{9,8},{10,11... | collective-permute-start | bytes 3932168 | tf_op jit(solution)/shard_map/ppermute | solution.py:303
  111.8 39.6 %collective-permute-start.14 = (bf16[256,2560]{1,0:T(8,128)(2,1)}, bf16[256,2560]{1,0:T(8,128)(2,1)}, u32[]{:S(2)}, u32[]{:S(2)}) collective-permute-start(bf16[256,2560]{1,0:T(8,128)(2,1)} %constant_dynamic-update-slice_fusion.2.refs_3_), channel_id=1, source_target_pairs={{0,1},{1,0},{2,3},{3,2},{4,5},{5,4},{6,7},{7,6},{8,9},{9,8},{10,11... | collective-permute-start | bytes 3932168 | tf_op jit(solution)/shard_map/ppermute | solution.py:303
  119.7 48.8 %all-to-all-start.1 = ((bf16[4,128,1024]{2,1,0:T(8,128)(2,1)}), bf16[4,128,1024]{2,1,0:T(8,128)(2,1)}, u32[]{:S(2)}, u32[]{:S(2)}) async-start(bf16[4,128,1024]{2,1,0:T(8,128)(2,1)} %bitcast.349), calls=%async_computation.1 | async-start | bytes 2097152 | tf_op jit(solution)/shard_map/all_to_all | solution.py:401
  124.7 189.4 %all-gather.11.cloned.1.call-start = ((), (), s32[]{:S(2)}) async-start(), calls=%async_computation.9 | async-start | bytes 1081344 | tf_op jit(solution)/shard_map/all_gather | solution.py:315
  131.0 56.9 %collective-permute-start.7 = (bf16[512,2048]{1,0:T(8,128)(2,1)}, bf16[512,2048]{1,0:T(8,128)(2,1)}, u32[]{:S(2)}, u32[]{:S(2)}) collective-permute-start(bf16[512,2048]{1,0:T(8,128)(2,1)} %fusion.12.refs_3_.refs_5_.refs_6_.refs_8_), channel_id=1, source_target_pairs={{0,1},{1,0},{2,3},{3,2},{4,5},{5,4},{6,7},{7,6},{8,9},{9,8},{10,11... | collective-permute-start | bytes 6291464 | tf_op jit(solution)/shard_map/ppermute | solution.py:418
  173.5 40.9 %collective-permute-start.15 = (bf16[512,2048]{1,0:T(8,128)(2,1)S(1)}, bf16[512,2048]{1,0:T(8,128)(2,1)}, u32[]{:S(2)}, u32[]{:S(2)}) collective-permute-start(bf16[512,2048]{1,0:T(8,128)(2,1)S(1)} %fusion.13.refs_3_.refs_5_.refs_6_.refs_8_), channel_id=1, source_target_pairs={{0,1},{1,0},{2,3},{3,2},{4,5},{5,4},{6,7},{7,6},{8,9},{9,8},{10,11... | collective-permute-start | bytes 6291464 | tf_op jit(solution)/shard_map/ppermute | solution.py:418
  398.0 49.6 %collective-permute-start.39 = (bf16[2,2,4,16,1024]{4,3,2,1,0:T(8,128)(2,1)}, bf16[2,2,4,16,1024]{4,3,2,1,0:T(8,128)(2,1)}, u32[]{:S(2)}, u32[]{:S(2)}) collective-permute-start(bf16[2,2,4,16,1024]{4,3,2,1,0:T(8,128)(2,1)} %dynamic-slice_bitcast_fusion.7), channel_id=1, source_target_pairs={{0,1},{1,0},{2,3},{3,2},{4,5},{5,4},{6,7},{7,6},{8,9},{9,8},{10,11... | collective-permute-start | bytes 1572872 | tf_op jit(solution)/shard_map/ppermute | solution.py:324
  410.8 74.9 %collective-permute-start.32 = (bf16[2,2,4,32,1536]{4,3,2,1,0:T(8,128)(2,1)}, bf16[2,2,4,32,1536]{4,3,2,1,0:T(8,128)(2,1)}, u32[]{:S(2)}, u32[]{:S(2)}) collective-permute-start(bf16[2,2,4,32,1536]{4,3,2,1,0:T(8,128)(2,1)} %dynamic-slice_bitcast_fusion.2), channel_id=1, source_target_pairs={{0,1},{1,0},{2,3},{3,2},{4,5},{5,4},{6,7},{7,6},{8,9},{9,8},{10,11... | collective-permute-start | bytes 4718600 | tf_op jit(solution)/shard_map/ppermute | solution.py:324
  410.8 92.8 %collective-permute-start.17 = (bf16[2,512,1024]{2,1,0:T(8,128)(2,1)}, bf16[2,512,1024]{2,1,0:T(8,128)(2,1)}, u32[]{:S(2)}, u32[]{:S(2)}) collective-permute-start(bf16[2,512,1024]{2,1,0:T(8,128)(2,1)} %get-tuple-element.38), channel_id=1, source_target_pairs={{0,1},{1,0},{2,3},{3,2},{4,5},{5,4},{6,7},{7,6},{8,9},{9,8},{10,11... | collective-permute-start | bytes 6291464 | tf_op jit(solution)/shard_map/ppermute | solution.py:422
  434.4 77.6 %collective-permute-start.16 = (bf16[2,512,1024]{2,1,0:T(8,128)(2,1)}, bf16[2,512,1024]{2,1,0:T(8,128)(2,1)}, u32[]{:S(2)}, u32[]{:S(2)}) collective-permute-start(bf16[2,512,1024]{2,1,0:T(8,128)(2,1)} %get-tuple-element.36), channel_id=1, source_target_pairs={{0,1},{1,0},{2,3},{3,2},{4,5},{5,4},{6,7},{7,6},{8,9},{9,8},{10,11... | collective-permute-start | bytes 6291464 | tf_op jit(solution)/shard_map/ppermute | solution.py:422
  440.2 54.5 %all-to-all-start.2 = ((bf16[4,128,1024]{2,1,0:T(8,128)(2,1)}), bf16[4,128,1024]{2,1,0:T(8,128)(2,1)}, u32[]{:S(2)}, u32[]{:S(2)}) async-start(bf16[4,128,1024]{2,1,0:T(8,128)(2,1)} %bitcast.354), calls=%async_computation.2 | async-start | bytes 2097152 | tf_op jit(solution)/shard_map/all_to_all | solution.py:406
  499.7 87.2 %collective-permute-start.34 = (bf16[4,32,768]{2,1,0:T(8,128)(2,1)}, bf16[4,32,768]{2,1,0:T(8,128)(2,1)}, u32[]{:S(2)}, u32[]{:S(2)}) collective-permute-start(bf16[4,32,768]{2,1,0:T(8,128)(2,1)} %dynamic-slice_bitcast_fusion.19), channel_id=1, source_target_pairs={{0,16},{8,24},{16,0},{24,8},{1,17},{9,25},{17,1},{25,9},{2,18},{10... | collective-permute-start | bytes 589832 | tf_op jit(solution)/shard_map/ppermute | solution.py:324
  502.1 85.9 %collective-permute-start.36 = (bf16[4,32,768]{2,1,0:T(8,128)(2,1)}, bf16[4,32,768]{2,1,0:T(8,128)(2,1)}, u32[]{:S(2)}, u32[]{:S(2)}) collective-permute-start(bf16[4,32,768]{2,1,0:T(8,128)(2,1)} %dynamic-slice_bitcast_fusion.18), channel_id=1, source_target_pairs={{0,8},{8,0},{16,24},{24,16},{1,9},{9,1},{17,25},{25,17},{2,10},{10... | collective-permute-start | bytes 589832 | tf_op jit(solution)/shard_map/ppermute | solution.py:324
  546.5 109.5 %collective-permute-start.25 = (bf16[2,2,4,32,4096]{4,3,2,1,0:T(8,128)(2,1)}, bf16[2,2,4,32,4096]{4,3,2,1,0:T(8,128)(2,1)}, u32[]{:S(2)}, u32[]{:S(2)}) collective-permute-start(bf16[2,2,4,32,4096]{4,3,2,1,0:T(8,128)(2,1)} %dynamic-slice_bitcast_fusion), channel_id=1, source_target_pairs={{0,1},{1,0},{2,3},{3,2},{4,5},{5,4},{6,7},{7,6},{8,9},{9,8},{10,11... | collective-permute-start | bytes 12582920 | tf_op jit(solution)/shard_map/ppermute | solution.py:324
  (115 other events, 1332.1 us)
Sparse Core Ops, SparseCore 0:
  11.6 66.7 all-gather.8
  81.4 99.0 all-gather.4
  183.5 74.6 all-gather.6
  261.7 52.3 all-gather.10

commit v2 on v1

v2 whole, which is shorter than its diff:
```python
import functools

import jax
import jax.numpy as jnp
from jax import lax
from jax.experimental import pallas as pl
from jax.experimental.pallas import tpu as pltpu
from jax.sharding import PartitionSpec as P

HEAD = 64
PAIR = 2 * HEAD
SCALE = HEAD ** (-0.5)
MASKED_SCORE = -1e30
NEVER = 2**30
ALWAYS = 2**29
F32 = jnp.float32
BF16 = jnp.bfloat16
STRIP = 128
ROOT_HALF = 0.7071067811865476
PDF_SCALE = 0.3989422804014327


def dot(left, right):
    return jnp.dot(left, right, preferred_element_type=F32)


def dot_tn(left, right):
    return lax.dot_general(left, right, (((0,), (0,)), ((), ())), preferred_element_type=F32)


def dot_nt(left, right):
    return lax.dot_general(left, right, (((1,), (1,)), ((), ())), preferred_element_type=F32)


def gelu_pair(inputs):
    below_it = 0.5 * (1.0 + lax.erf(inputs * ROOT_HALF))
    density = PDF_SCALE * jnp.exp(-0.5 * inputs * inputs)
    return inputs * below_it, below_it + inputs * density


def norm_parts(inputs):
    centre = jnp.mean(inputs, axis=-1, keepdims=True)
    centred = inputs - centre
    spread = jnp.mean(centred * centred, axis=-1, keepdims=True)
    rstd = lax.rsqrt(spread + 1e-05)
    return centred * rstd, rstd


def norm_backward(normed, rstd, gain, grad):
    inner = grad * gain
    mean_one = jnp.mean(inner, axis=-1, keepdims=True)
    mean_two = jnp.mean(inner * normed, axis=-1, keepdims=True)
    return rstd * (inner - mean_one - normed * mean_two)


def strips(rows):
    return [slice(start, start + STRIP) for start in range(0, rows, STRIP)]


MIB = 1024 * 1024


def bytes_of(shape, kind):
    size = jnp.dtype(kind).itemsize
    for extent in shape:
        size *= extent
    return size


def params(blocks, scratch=0, spare=10):
    limit = 2 * sum(bytes_of(shape, kind) for shape, kind in blocks) + scratch + spare * MIB
    return pltpu.CompilerParams(vmem_limit_bytes=min(limit, 60 * MIB))


def cost(micros):
    return pl.CostEstimate(
        flops=int(micros * 1.15e9), bytes_accessed=int(micros * 3.6e6), transcendentals=0
    )


def tile_of(rows):
    return 128 if rows % 128 == 0 else rows


def key_rows(tile_end, rows, block, causal):
    if not causal:
        return rows
    return min(rows, ((tile_end - 1) // block + 1) * block)


def beside(top):
    row = lax.broadcasted_iota(jnp.int32, top.shape, 0)
    zero = jnp.zeros_like(top)
    return jnp.concatenate(
        [jnp.where(row < HEAD, top, zero), jnp.where(row < HEAD, zero, top)], axis=1
    )


def below(side):
    lane = lax.broadcasted_iota(jnp.int32, side.shape, 1)
    zero = jnp.zeros_like(side)
    return jnp.concatenate(
        [jnp.where(lane < HEAD, side, zero), jnp.where(lane < HEAD, zero, side)], axis=0
    )


def heads_back(wide, tile):
    return jnp.concatenate([wide[:HEAD, :tile], wide[HEAD:, tile:]], axis=0).T


def forward_kernel(pieces, block, causal, *refs):
    query_ref, key_pos_ref, query_pos_ref = refs[:3]
    key_refs = refs[3 : 3 + pieces]
    value_refs = refs[3 + pieces : 3 + 2 * pieces]
    out_ref, total_ref = refs[3 + 2 * pieces :]
    rows = query_ref.shape[0]
    tile = tile_of(rows)
    scaled = query_ref[...].astype(F32) * SCALE
    query_up = scaled.T.astype(BF16)
    values_up = [ref[...].astype(F32).T.astype(BF16) for ref in value_refs]
    for start in range(0, rows, tile):
        keys = key_rows(start + tile, rows, block, causal)
        wide = beside(query_up[:, start : start + tile])
        query_pos = query_pos_ref[:, start : start + tile]
        limit = jnp.concatenate([query_pos, query_pos], axis=1)
        scores = []
        for piece in range(pieces):
            score = dot(key_refs[piece][:keys, :], wide)
            allowed = key_pos_ref[piece, :keys, :] <= limit
            scores.append(jnp.where(allowed, score, MASKED_SCORE))
        highest = functools.reduce(
            jnp.maximum, [jnp.max(score, axis=0, keepdims=True) for score in scores]
        )
        summed = jnp.zeros_like(highest)
        mixed = jnp.zeros((PAIR, 2 * tile), F32)
        for piece in range(pieces):
            raised = jnp.exp(scores[piece] - highest)
            summed = summed + jnp.sum(raised, axis=0, keepdims=True)
            mixed = mixed + dot(values_up[piece][:, :keys], raised.astype(BF16))
        mixed = mixed / summed
        out_ref[start : start + tile, :] = heads_back(mixed, tile).astype(BF16)
        total = highest + jnp.log(summed)
        total_ref[0, 0:1, start : start + tile] = total[:, :tile]
        total_ref[0, 1:2, start : start + tile] = total[:, tile:]


def attend_forward(queries, keys_values, key_pos, query_pos, block, causal):
    rows, width = queries.shape
    pieces = len(keys_values)
    pairs = width // PAIR
    column = pl.BlockSpec((rows, PAIR), lambda p: (0, p))
    second = pl.BlockSpec((rows, PAIR), lambda p: (0, p + pairs))
    whole_pos = pl.BlockSpec((pieces, rows, 1), lambda p: (0, 0, 0))
    row_pos = pl.BlockSpec((1, rows), lambda p: (0, 0))
    return pl.pallas_call(
        functools.partial(forward_kernel, pieces, block, causal),
        grid=(pairs,),
        in_specs=[column, whole_pos, row_pos] + [column] * pieces + [second] * pieces,
        out_specs=[column, pl.BlockSpec((1, 2, rows), lambda p: (p, 0, 0))],
        out_shape=[
            jax.ShapeDtypeStruct((rows, width), BF16),
            jax.ShapeDtypeStruct((pairs, 2, rows), F32),
        ],
        compiler_params=params(
            [((rows, PAIR), BF16)] * (2 + 2 * pieces) + [((pieces, rows, 128), F32)],
            spare=10 + 4 * (pieces > 2),
        ),
        cost_estimate=cost(18 if causal else 22),
        name="attend_forward",
    )(queries, key_pos, query_pos, *keys_values, *keys_values)


def backward_kernel(pieces, block, causal, *refs):
    query_ref, out_ref, grad_ref, total_ref, key_pos_ref, query_pos_ref = refs[:6]
    key_refs = refs[6 : 6 + pieces]
    value_refs = refs[6 + pieces : 6 + 2 * pieces]
    dquery_ref, down_ref = refs[6 + 2 * pieces : 8 + 2 * pieces]
    dother_refs = refs[8 + 2 * pieces : 7 + 3 * pieces]
    dkey_ref, dvalue_ref = refs[7 + 3 * pieces :]
    rows = query_ref.shape[0]
    tile = tile_of(rows)
    scaled = query_ref[...].astype(F32) * SCALE
    query_up = scaled.T
    scaled = scaled.astype(BF16)
    grad_up = grad_ref[...].astype(F32).T
    out_up = out_ref[...].astype(F32).T
    keys_up = [ref[...].astype(F32).T.astype(BF16) for ref in key_refs]
    product_up = grad_up * out_up
    query_up = query_up.astype(BF16)
    grad_up = grad_up.astype(BF16)
    dkey_ref[...] = jnp.zeros_like(dkey_ref)
    dvalue_ref[...] = jnp.zeros_like(dvalue_ref)
    for start in range(0, rows, tile):
        stop = start + tile
        keys = key_rows(stop, rows, block, causal)
        query_wide = beside(query_up[:, start:stop])
        grad_wide = beside(grad_up[:, start:stop])
        query_tall = below(scaled[start:stop, :])
        grad_tall = below(grad_ref[start:stop, :])
        product = product_up[:, start:stop]
        centre = jnp.concatenate(
            [
                jnp.sum(product[:HEAD], axis=0, keepdims=True),
                jnp.sum(product[HEAD:], axis=0, keepdims=True),
            ],
            axis=1,
        )
        total = jnp.concatenate(
            [total_ref[0, 0:1, start:stop], total_ref[0, 1:2, start:stop]], axis=1
        )
        query_pos = query_pos_ref[:, start:stop]
        limit = jnp.concatenate([query_pos, query_pos], axis=1)
        dquery = jnp.zeros((PAIR, 2 * tile), F32)
        for piece in range(pieces):
            score = dot(key_refs[piece][:keys, :], query_wide)
            allowed = key_pos_ref[piece, :keys, :] <= limit
            probs = jnp.exp(jnp.where(allowed, score, MASKED_SCORE) - total)
            dprob = dot(value_refs[piece][:keys, :], grad_wide)
            dscore = (probs * (dprob - centre)).astype(BF16)
            dvalue_ref[piece, :keys, :] += dot(probs.astype(BF16), grad_tall)
            dkey_ref[piece, :keys, :] += dot(dscore, query_tall)
            dquery = dquery + dot(keys_up[piece][:, :keys], dscore)
        dquery_ref[start:stop, :] = (heads_back(dquery, tile) * SCALE).astype(BF16)
    down_ref[0] = dkey_ref[0]
    down_ref[1] = dvalue_ref[0]
    for piece in range(1, pieces):
        dother_refs[piece - 1][0] = dkey_ref[piece].astype(BF16)
        dother_refs[piece - 1][1] = dvalue_ref[piece].astype(BF16)


def attend_backward(
    queries, keys_values, outputs, grads, totals, key_pos, query_pos, block, causal, first, pairs
):
    rows, width = queries.shape
    pieces = len(keys_values)
    shift = width // PAIR
    column = pl.BlockSpec((rows, PAIR), lambda p: (0, p + first))
    second = pl.BlockSpec((rows, PAIR), lambda p: (0, p + first + shift))
    whole_pos = pl.BlockSpec((pieces, rows, 1), lambda p: (0, 0, 0))
    row_pos = pl.BlockSpec((1, rows), lambda p: (0, 0))
    both = pl.BlockSpec((2, rows, PAIR), lambda p: (0, 0, p))
    size = pairs * PAIR
    return pl.pallas_call(
        functools.partial(backward_kernel, pieces, block, causal),
        grid=(pairs,),
        in_specs=[
            column,
            column,
            column,
            pl.BlockSpec((1, 2, rows), lambda p: (p + first, 0, 0)),
            whole_pos,
            row_pos,
        ]
        + [column] * pieces
        + [second] * pieces,
        out_specs=[pl.BlockSpec((rows, PAIR), lambda p: (0, p)), both] + [both] * (pieces - 1),
        out_shape=[
            jax.ShapeDtypeStruct((rows, size), BF16),
            jax.ShapeDtypeStruct((2, rows, size), F32),
        ]
        + [jax.ShapeDtypeStruct((2, rows, size), BF16)] * (pieces - 1),
        scratch_shapes=[pltpu.VMEM((pieces, rows, PAIR), F32)] * 2,
        compiler_params=params(
            [((rows, PAIR), BF16)] * (6 + 4 * pieces) + [((pieces, rows, 128), F32)] * 2,
            spare=10 + 4 * (pieces > 2),
        ),
        cost_estimate=cost((24 if causal else 28) * size / width),
        name="attend_backward",
    )(queries, outputs, grads, totals, key_pos, query_pos, *keys_values, *keys_values)


def offset(slot, size):
    return pl.multiple_of(slot * size, size)


def row_parts(place, refs):
    if len(refs) == 1:
        return [(0, refs[0][...])]
    own, one, two, near, far = [ref[...] for ref in refs]
    near_first = jnp.concatenate([near, far], axis=0)
    far_first = jnp.concatenate([far, near], axis=0)
    diagonal = jnp.where(place[4] == 0, near_first, far_first)
    return [(place[0], own), (place[1], one), (place[2], two), (place[3], diagonal)]


def times(left_ref, place, refs):
    total = None
    for slot, part in row_parts(place, refs):
        rows = part.shape[0]
        term = dot(left_ref[:, pl.ds(offset(slot, rows), rows)], part)
        total = term if total is None else total + term
    return total


def times_up(left, place, refs, store):
    for slot, part in row_parts(place, refs):
        rows = part.shape[0]
        store(pl.ds(offset(slot, rows), rows), dot_nt(left, part))


def part_specs(arrays, columns, index):
    return [pl.BlockSpec((item.shape[0], columns), lambda *at: (0, index(*at))) for item in arrays]


def fixed(shape):
    zeros = (0,) * len(shape)
    return pl.BlockSpec(shape, lambda *at: zeros)


def view(item, columns, index):
    if item.ndim == 2:
        return (item, pl.BlockSpec((item.shape[0], columns), lambda *at: (0, index)))
    return (item, pl.BlockSpec((1, item.shape[1], columns), lambda *at: (index, 0, 0)))


def run(kernel, name, place, grid, ins, outs, micros, scratch=(), spare=10):
    kept = [bool(out[3:]) for out in outs]
    outs = [out[:3] for out in outs]
    blocks = [(spec.block_shape, item.dtype) for item, spec in ins]
    blocks += [(spec.block_shape, kind) for _, kind, spec in outs]
    held = sum(bytes_of(item.shape, item.dtype) for item in scratch)
    return pl.pallas_call(
        kernel,
        grid_spec=pltpu.PrefetchScalarGridSpec(
            num_scalar_prefetch=1,
            grid=grid,
            in_specs=[spec for _, spec in ins],
            out_specs=[spec for _, _, spec in outs],
            scratch_shapes=list(scratch),
        ),
        out_shape=[
            pltpu.HBM(shape, kind) if keep else jax.ShapeDtypeStruct(shape, kind)
            for keep, (shape, kind, _) in zip(kept, outs)
        ],
        compiler_params=params(blocks, held, spare),
        cost_estimate=cost(micros),
        name=name,
    )(place, *[item for item, _ in ins])


def project_kernel(place, left_ref, *refs):
    refs[-1][...] = times(left_ref, place, refs[:-1]).astype(BF16)


def project(place, left, weight, first, count, name):
    rows, depth = left[1].block_shape
    chunk = 512
    steps = count * 1024 // chunk
    base = first * 1024 // chunk
    return run(
        project_kernel,
        name,
        place,
        (steps,),
        [left]
        + list(zip(weight, part_specs(weight, chunk, lambda j, s: base + j))),
        [((rows, count * 1024), BF16, pl.BlockSpec((rows, chunk), lambda j, s: (0, j)))],
        2.5 * count,
    )[0]


def mix_kernel(parts, both, place, mixed_ref, resid_ref, norm_ref, *refs):
    out_parts = refs[:parts]
    query_parts = refs[parts : 2 * parts] if both else ()
    outs = refs[2 * parts :] if both else refs[parts:]
    summed_ref, normed_ref, low_ref = outs[:3]
    step = pl.program_id(0)
    rows, width = summed_ref.shape
    half = width // 2

    @pl.when(step < 2)
    def _():
        columns = pl.ds(offset(step, half), half)
        summed_ref[:, columns] = resid_ref[:, columns].astype(F32) + times(
            mixed_ref, place, out_parts
        )

    @pl.when(step == 1)
    def _():
        for strip in strips(rows):
            normed, _ = norm_parts(summed_ref[strip, :])
            value = normed * norm_ref[0:1, :] + norm_ref[1:2, :]
            normed_ref[strip, :] = value
            low_ref[strip, :] = value.astype(BF16)

    if both:

        @pl.when(step >= 2)
        def _():
            outs[3][...] = times(low_ref, place, query_parts).astype(BF16)


def mix(place, mixed, resid, norm, w_out, at_out, w_query, at_query, name):
    rows, width = mixed.shape
    half = width // 2
    both = w_query is not None
    ins = [(mixed, fixed(mixed.shape)), resid, (norm, fixed(norm.shape))]
    ins += zip(
        w_out, part_specs(w_out, half, lambda j, s: at_out * 2 + jnp.minimum(j, 1))
    )
    outs = [
        ((rows, width), F32, fixed((rows, width)), True),
        ((rows, width), F32, fixed((rows, width)), True),
        ((rows, width), BF16, fixed((rows, width)), True),
    ]
    if both:
        ins += zip(
            w_query,
            part_specs(w_query, half, lambda j, s: at_query * 2 + jnp.maximum(j - 2, 0)),
        )
        outs += [
            (
                (rows, width),
                BF16,
                pl.BlockSpec((rows, half), lambda j, s: (0, jnp.maximum(j - 2, 0))),
            )
        ]
    return run(
        functools.partial(mix_kernel, len(w_out), both),
        name,
        place,
        (4 if both else 2,),
        ins,
        outs,
        6.3 if both else 4,
    )


def up_parts(place, refs, packed):
    if not packed:
        return [(0, refs[0][...])]
    unpacked = []
    for slot, part in row_parts(place, refs):
        rows = part.shape[0] // 2
        unpacked.append((slot, jnp.concatenate([part[:rows], part[rows:]], axis=1)))
    return unpacked


def chunk_of(refs, step, counts, use):
    low = 0
    for ref, count in zip(refs, counts):

        @pl.when((step >= low) & (step < low + count))
        def _(ref=ref):
            use(ref)

        low += count


def feed_specs(w_in, w_out, counts, first, chunk, width):
    in_specs = part_specs(w_in, chunk, lambda j, s: s[8 + first + j])
    shift = first if len(w_in) == 1 else 0
    out_specs, start = [], 0
    for count in counts:
        out_specs.append(
            pl.BlockSpec(
                (chunk, width),
                lambda j, s, start=start, count=count: (
                    shift + jnp.clip(j - start, 0, count - 1),
                    0,
                ),
            )
        )
        start += count
    return in_specs, out_specs


def feed_first_kernel(
    sizes, counts, packed, place, low_ref, second_ref, *refs
):
    n_in, n_out, n_down, n_up = sizes
    in_refs, refs = refs[:n_in], refs[n_in:]
    out_refs, refs = refs[:n_out], refs[n_out:]
    down_refs, refs = refs[:n_down], refs[n_down:]
    up_refs, refs = refs[:n_up], refs[n_up:]
    total_ref, slope_ref, hidden_ref, aslope_ref = refs
    step = pl.program_id(0)

    @pl.when(step == 0)
    def _():
        hidden, slope = gelu_pair(times(low_ref, place, down_refs))
        hidden_ref[...] = hidden.astype(BF16)
        aslope_ref[...] = slope.astype(BF16)
        total = None
        for slot, part in up_parts(place, up_refs, packed):
            count = part.shape[0]
            term = dot(hidden_ref[:, pl.ds(offset(slot, count), count)], part)
            total = term if total is None else total + term
        total_ref[...] = second_ref[...] + 4.0 * total

    feed_chunk(place, low_ref, in_refs, out_refs, counts, total_ref, slope_ref)


def feed_chunk(place, low_ref, in_refs, out_refs, counts, total_ref, slope_ref):
    hidden, slope = gelu_pair(times(low_ref, place, in_refs))
    slope_ref[...] = slope.astype(BF16)
    hidden = hidden.astype(BF16)

    def use(ref):
        total_ref[...] += dot(hidden, ref[...])

    chunk_of(out_refs, pl.program_id(0), counts, use)


def feed_second_kernel(
    sizes, counts, steps, place, low_ref, first_ref, grad_ref, norm_ref, *refs
):
    n_in, n_out = sizes
    in_refs, refs = refs[:n_in], refs[n_in:]
    out_refs, refs = refs[:n_out], refs[n_out:]
    final_ref, d_ref, dlow_ref, dnorm_ref, slope_ref, total_ref = refs
    step = pl.program_id(0)
    rows, width = total_ref.shape

    @pl.when(step == 0)
    def _():
        total_ref[...] = first_ref[...]

    feed_chunk(place, low_ref, in_refs, out_refs, counts, total_ref, slope_ref)

    @pl.when(step == steps - 1)
    def _():
        gain, shift = norm_ref[0:1, :], norm_ref[1:2, :]
        dgain = jnp.zeros((1, width), F32)
        dshift = jnp.zeros((1, width), F32)
        for strip in strips(rows):
            normed, rstd = norm_parts(total_ref[strip, :])
            final_ref[strip, :] = (normed * gain + shift).astype(BF16)
            grad = grad_ref[strip, :].astype(F32)
            dgain += jnp.sum(grad * normed, axis=0, keepdims=True)
            dshift += jnp.sum(grad, axis=0, keepdims=True)
            back = norm_backward(normed, rstd, gain, grad)
            d_ref[strip, :] = back
            dlow_ref[strip, :] = back.astype(BF16)
        dnorm_ref[0:1, :] = dgain
        dnorm_ref[1:2, :] = dshift


CHUNK = 512


def feed_first(place, low, second, w_in, w_out, counts, w_down, at_down, w_up, at_up):
    rows, width = low.shape
    adapter = 512
    packed = len(w_up) > 1
    steps = sum(counts)
    in_specs, out_specs = feed_specs(w_in, w_out, counts, 0, CHUNK, width)
    up_columns = 512 if packed else width
    full = fixed((rows, width))
    ins = [(low, full), (second, full)]
    ins += zip(w_in, in_specs)
    ins += zip(w_out, out_specs)
    ins += zip(w_down, part_specs(w_down, adapter, lambda j, s: at_down))
    ins += zip(w_up, part_specs(w_up, up_columns, lambda j, s: at_up))
    return run(
        functools.partial(
            feed_first_kernel, (len(w_in), len(w_out), len(w_down), len(w_up)), counts, packed
        ),
        "feed_first",
        place,
        (steps,),
        ins,
        [
            ((rows, width), F32, full),
            ((rows, steps * CHUNK), BF16, pl.BlockSpec((rows, CHUNK), lambda j, s: (0, j)), True),
            ((rows, adapter), BF16, fixed((rows, adapter)), True),
            ((rows, adapter), BF16, fixed((rows, adapter)), True),
        ],
        13,
    )


def feed_second(place, low, first, grad, norm, w_in, w_out, counts, start):
    rows, width = low.shape
    steps = sum(counts)
    in_specs, out_specs = feed_specs(w_in, w_out, counts, start, CHUNK, width)
    full = fixed((rows, width))
    ins = [(low, full), (first, full), (grad, full), (norm, fixed(norm.shape))]
    ins += zip(w_in, in_specs)
    ins += zip(w_out, out_specs)
    return run(
        functools.partial(feed_second_kernel, (len(w_in), len(w_out)), counts, steps),
        "feed_second",
        place,
        (steps,),
        ins,
        [
            ((rows, width), BF16, full, True),
            ((rows, width), F32, full),
            ((rows, width), BF16, full),
            ((2, width), F32, fixed((2, width)), True),
            ((rows, steps * CHUNK), BF16, pl.BlockSpec((rows, CHUNK), lambda j, s: (0, j)), True),
        ],
        13.5,
        scratch=[pltpu.VMEM((rows, width), F32)],
    )


def feed_backward_kernel(
    sizes,
    counts,
    packed,
    steps,
    place,
    dlow_ref,
    d_ref,
    resid_ref,
    norm_ref,
    slope_ref,
    later_ref,
    aslope_ref,
    *refs,
):
    n_in, n_out, n_down, n_up, n_mix = sizes
    in_refs, refs = refs[:n_in], refs[n_in:]
    out_refs, refs = refs[:n_out], refs[n_out:]
    down_refs, refs = refs[:n_down], refs[n_down:]
    up_refs, refs = refs[:n_up], refs[n_up:]
    mix_refs, refs = refs[:n_mix], refs[n_mix:]
    dtwo_ref, dtwo_low_ref, dnorm_ref, dadapter_ref, dmixed_ref, total_ref, dhidden_ref = refs
    step = pl.program_id(0)
    rows, width = total_ref.shape

    def add(columns, value):
        total_ref[:, columns] += value

    @pl.when(step == 0)
    def _():
        total_ref[...] = d_ref[...]
        for slot, part in up_parts(place, up_refs, packed):
            count = part.shape[0]
            columns = pl.ds(offset(slot, count), count)
            back = 4.0 * dot_nt(dlow_ref[...], part)
            dadapter_ref[:, columns] = (aslope_ref[:, columns].astype(F32) * back).astype(BF16)
        times_up(dadapter_ref[...], place, down_refs, add)

    def use(ref):
        back = dot_nt(dlow_ref[...], ref[...])
        chosen = jnp.where(step < steps // 2, slope_ref[...], later_ref[...])
        dhidden_ref[...] = (chosen.astype(F32) * back).astype(BF16)

    chunk_of(out_refs, step, counts, use)
    times_up(dhidden_ref[...], place, in_refs, add)

    @pl.when(step == steps - 1)
    def _():
        finish_norm(total_ref, resid_ref, norm_ref, dtwo_ref, dtwo_low_ref, dnorm_ref)

        def keep(columns, value):
            dmixed_ref[:, columns] = value.astype(BF16)

        times_up(dtwo_low_ref[...], place, mix_refs, keep)


def finish_norm(grad_ref, resid_ref, norm_ref, d_ref, dlow_ref, dnorm_ref):
    rows, width = grad_ref.shape
    gain = norm_ref[0:1, :]
    dgain = jnp.zeros((1, width), F32)
    dshift = jnp.zeros((1, width), F32)
    for strip in strips(rows):
        grad = grad_ref[strip, :]
        normed, rstd = norm_parts(resid_ref[strip, :])
        dgain += jnp.sum(grad * normed, axis=0, keepdims=True)
        dshift += jnp.sum(grad, axis=0, keepdims=True)
        back = norm_backward(normed, rstd, gain, grad)
        d_ref[strip, :] = back
        dlow_ref[strip, :] = back.astype(BF16)
    dnorm_ref[0:1, :] = dgain
    dnorm_ref[1:2, :] = dshift


def feed_backward(
    place,
    dlow,
    d_three,
    resid,
    norm,
    slope,
    later,
    aslope,
    w_in,
    w_out,
    counts,
    w_down,
    at_down,
    w_up,
    at_up,
    w_mix,
    at_mix,
):
    rows, width = dlow.shape
    hidden = w_in[0].shape[1]
    adapter = 512
    packed = len(w_up) > 1
    chunk = CHUNK
    steps = hidden // chunk
    in_specs, out_specs = feed_specs(w_in, w_out, counts, 0, chunk, width)
    middle = steps // 2
    up_columns = 512 if packed else width
    full = fixed((rows, width))
    ins = [
        (dlow, full),
        (d_three, full),
        (resid, full),
        (norm, fixed(norm.shape)),
        (slope, pl.BlockSpec((rows, chunk), lambda j, s: (0, jnp.minimum(j, middle - 1)))),
        (later, pl.BlockSpec((rows, chunk), lambda j, s: (0, jnp.maximum(j - middle, 0)))),
        (aslope, fixed((rows, adapter))),
    ]
    ins += zip(w_in, in_specs)
    ins += zip(w_out, out_specs)
    ins += zip(w_down, part_specs(w_down, adapter, lambda j, s: at_down))
    ins += zip(w_up, part_specs(w_up, up_columns, lambda j, s: at_up))
    ins += zip(w_mix, part_specs(w_mix, width, lambda j, s: at_mix))
    return run(
        functools.partial(
            feed_backward_kernel,
            (len(w_in), len(w_out), len(w_down), len(w_up), len(w_mix)),
            counts,
            packed,
            steps,
        ),
        "feed_backward",
        place,
        (steps,),
        ins,
        [
            ((rows, width), F32, full, True),
            ((rows, width), BF16, full),
            ((2, width), F32, fixed((2, width)), True),
            ((rows, adapter), BF16, fixed((rows, adapter))),
            ((rows, width), BF16, full),
        ],
        29,
        scratch=[pltpu.VMEM((rows, width), F32), pltpu.VMEM((rows, chunk), BF16)],
    )


def norm_step_kernel(parts, place, dquery_ref, d_ref, resid_ref, norm_ref, *refs):
    query_refs, refs = refs[:parts], refs[parts:]
    out_refs, refs = refs[:parts], refs[parts:]
    done_ref, done_low_ref, dnorm_ref, dmixed_ref, total_ref = refs
    step = pl.program_id(0)

    @pl.when(step == 0)
    def _():
        def add(columns, value):
            total_ref[:, columns] = d_ref[:, columns] + value

        times_up(dquery_ref[...], place, query_refs, add)
        finish_norm(total_ref, resid_ref, norm_ref, done_ref, done_low_ref, dnorm_ref)

    @pl.when(step == 1)
    def _():
        def keep(columns, value):
            dmixed_ref[:, columns] = value.astype(BF16)

        times_up(done_low_ref[...], place, out_refs, keep)


def norm_step(place, dquery, d_two, resid, norm, w_query, at_query, w_out, at_out):
    rows, width = dquery.shape
    full = fixed((rows, width))
    ins = [(dquery, full), (d_two, full), (resid, full), (norm, fixed(norm.shape))]
    ins += zip(w_query, part_specs(w_query, width, lambda j, s: at_query))
    ins += zip(w_out, part_specs(w_out, width, lambda j, s: at_out))
    return run(
        functools.partial(norm_step_kernel, len(w_query)),
        "norm_step",
        place,
        (2,),
        ins,
        [
            ((rows, width), F32, full, True),
            ((rows, width), BF16, full),
            ((2, width), F32, fixed((2, width)), True),
            ((rows, width), BF16, full),
        ],
        6.6,
        scratch=[pltpu.VMEM((rows, width), F32)],
    )


def inputs_back_kernel(lefts, parts, extra, place, *refs):
    left_refs, refs = refs[:lefts], refs[lefts:]
    part_refs, refs = refs[:parts], refs[parts:]
    if extra:
        extra_ref, refs = refs[0], refs[1:]
    out_ref, total_ref = refs
    step = pl.program_id(0)
    width = total_ref.shape[1]

    @pl.when(step == 0)
    def _():
        if extra == "base":
            total_ref[...] = extra_ref[...]
        else:
            total_ref[...] = jnp.zeros_like(total_ref)
        if extra == "beside":
            out_ref[:, :width] = extra_ref[...]

    def add(columns, value):
        total_ref[:, columns] += value

    for which in range(lefts):

        @pl.when(step == which)
        def _(which=which):
            left = left_refs[which][...]
            times_up(left.reshape(left.shape[-2:]), place, part_refs, add)

    @pl.when(step == lefts - 1)
    def _():
        out_ref[:, out_ref.shape[1] - width :] = total_ref[...].astype(BF16)


def inputs_back(place, lefts, weight, blocks, extra, item, name):
    depth = lefts[0][1].block_shape[-1]
    rows = lefts[0][1].block_shape[-2]
    width = 1024
    first = blocks[0]
    strides = {blocks[k + 1] - blocks[k] for k in range(len(blocks) - 1)}

    def at(j, s):
        index = first
        for k in range(1, len(blocks)):
            index = jnp.where(j == k, blocks[k], index)
        return first + j if strides == {1} else index

    ins = list(lefts)
    ins += zip(weight, part_specs(weight, depth, at))
    if extra:
        ins += [(item, fixed((rows, width)))]
    size = 2 * width if extra == "beside" else width
    return run(
        functools.partial(inputs_back_kernel, len(lefts), len(weight), extra),
        name,
        place,
        (len(lefts),),
        ins,
        [((rows, size), BF16, fixed((rows, size)))],
        3 * len(lefts) * depth / width,
        scratch=[pltpu.VMEM((rows, width), F32)],
    )[0]


def laid_out_kernel(slots, item_ref, *refs):
    out_ref = refs[-1]
    out_ref[slots[0]] = item_ref[0]
    for index, ref in enumerate(refs[:-1], 1):
        out_ref[slots[index]] = ref[...]


def laid_out(slots, item, parts):
    part = parts[0].shape
    return run(
        laid_out_kernel,
        "laid_out",
        slots,
        (1,),
        [(item, pl.BlockSpec((1,) + part, lambda j, s: (s[0], 0, 0)))]
        + [(piece, fixed(part)) for piece in parts],
        [(item.shape, item.dtype, fixed(item.shape))],
        1.5,
    )[0]


def swap_pairs(size, bit):
    return [(index, index ^ bit) for index in range(size)]


def by_core(even, odd):
    return [
        (d * 8 + s, (d ^ (odd if s % 2 else even)) * 8 + s) for d in range(4) for s in range(8)
    ]


def after(item, *others):
    return lax.optimization_barrier((item,) + others)[0]


def gather_first(own):
    one = lax.ppermute(own, ("dp", "seq"), by_core(1, 2))
    return (own, one, lax.ppermute(one, "seq", swap_pairs(8, 1)))


def gather_rest(parts, core, *others):
    one = parts[1]
    half = one.shape[0] // 2
    half_one = lax.dynamic_slice_in_dim(after(one, *others), core * half, half, 0)
    near = lax.ppermute(half_one, ("dp", "seq"), by_core(2, 1))
    return parts + (near, lax.ppermute(near, "seq", swap_pairs(8, 1)))


def gather_dp(item):
    return (lax.all_gather(item, "dp", axis=0, tiled=True),)


def row_blocks(value, size):
    return [value[start : start + size] for start in range(0, value.shape[0], size)]


def wgrad_kernel(fresh, split, scales, extra, place, *refs):
    count = len(fresh)
    left_refs, right_refs = refs[:count], refs[count : 2 * count]
    outs, up_ref = refs[2 * count + extra : -1], refs[-1]
    step = pl.program_id(0)
    wide = outs[0].shape[1]
    if extra:

        @pl.when(step == count)
        def _():
            rows = jnp.concatenate([ref[...] for ref in refs[2 * count : 2 * count + extra]])
            filler = jnp.zeros((128 - rows.shape[0], rows.shape[1]), F32)
            columns = jnp.concatenate([rows, filler], axis=0).T.astype(BF16)
            for index, item in enumerate(row_blocks(columns, 32)):
                at = (index % 8 * 4 + index // 8) * 32
                outs[0][at : at + 32, :128] = item

    for which in range(count):

        @pl.when(step == which)
        def _(which=which):
            right = right_refs[which][...]
            right = right.reshape(right.shape[-2:])
            tall = left_refs[which].shape[-1]
            if fresh[which]:
                left = left_refs[which][...]
                up_ref[:tall, :] = left.reshape(left.shape[-2:]).T
            value = dot(up_ref[:tall, :], right)
            value = (value * scales[which] if scales[which] != 1.0 else value).astype(BF16)
            own = tall // 32
            blocks = row_blocks(value, own)
            if split:
                even = jnp.concatenate(blocks[0::2], axis=0)
                odd = jnp.concatenate(blocks[1::2], axis=0)
                outs[0][...] = jnp.where(place[4] == 0, odd, even)
                outs[1][...] = jnp.where(place[4] == 0, even, odd)
                return
            folds = right.shape[1] // wide
            for index, item in enumerate(blocks):
                at = (index % 8 * 4 + index // 8) * own * folds
                for fold in range(folds):
                    low = at + fold * own
                    outs[0][low : low + own, :] = item[:, fold * wide : (fold + 1) * wide]


def wgrad(place, lefts, rights, wide, split, scales, name, extra=()):
    fresh = []
    for index, (item, spec) in enumerate(lefts):
        before = lefts[index - 1] if index else (None, None)
        fresh.append(item is not before[0] or spec is not before[1])
    rows, tall = lefts[0][1].block_shape[-2:]
    high = tall // 2 if split else tall
    spec = pl.BlockSpec((high, wide), lambda j, s: (0, j))
    more = 1 if extra else 0
    return run(
        functools.partial(wgrad_kernel, tuple(fresh), split, scales, len(extra)),
        name,
        place,
        (len(lefts) + more,),
        list(lefts) + list(rights) + [(item, fixed(item.shape)) for item in extra],
        [((high, wide * len(lefts) + 128 * more), BF16, spec, True)] * (2 if split else 1),
        1.6 * len(lefts) * wide / 1024,
        scratch=[pltpu.VMEM((tall, rows), BF16)],
    )


def take(item, index, axis):
    return lax.dynamic_index_in_dim(item, index, axis, keepdims=False)


def add(kept, received, kind=BF16):
    return (kept.astype(F32) + received.astype(F32)).astype(kind)


def sum_over(partial, name):
    return lax.psum_scatter(partial, name, scatter_dimension=0, tiled=True)


class Scatter:
    def __init__(self, send, keep):
        here, there = lax.axis_index("dp"), lax.axis_index("seq")
        self.x, self.y = here % 2, here // 2
        self.low, self.high = (there // 2) % 2, there // 4
        self.send, self.keep = send, keep
        self.width = keep.shape[1]

    def core(self):
        received = lax.ppermute(self.send, "seq", swap_pairs(8, 1))
        item = add(self.keep, received).reshape(2, 2, 128, self.width)
        self.one, self.two = item[..., : self.width // 2], item[..., self.width // 2 :]
        return self.one

    def plane_one(self):
        x, y = self.x, self.y
        from_x = lax.ppermute(take(self.one, 1 - x, 1), "dp", swap_pairs(4, 1))
        from_y = lax.ppermute(take(self.two, 1 - y, 0), "dp", swap_pairs(4, 2))
        self.one = add(take(self.one, x, 1), from_x)
        self.two = add(take(self.two, y, 0), from_y)
        return self.one

    def plane_two(self):
        x, y = self.x, self.y
        from_y = lax.ppermute(take(self.one, 1 - y, 0), "dp", swap_pairs(4, 2))
        from_x = lax.ppermute(take(self.two, 1 - x, 0), "dp", swap_pairs(4, 1))
        one = add(take(self.one, y, 0), from_y)
        two = add(take(self.two, x, 0), from_x)
        self.item = jnp.concatenate([one, two], axis=1).reshape(2, 2, 32, self.width)
        return self.item

    def z_one(self):
        received = lax.ppermute(take(self.item, 1 - self.low, 1), "seq", swap_pairs(8, 2))
        self.item = add(take(self.item, self.low, 1), received)
        return self.item

    def z_two(self):
        received = lax.ppermute(take(self.item, 1 - self.high, 0), "seq", swap_pairs(8, 4))
        self.item = add(take(self.item, self.high, 0), received, F32)
        return self.item


def sum_all(partial):
    return lax.psum_scatter(
        partial.astype(BF16), ("dp", "seq"), scatter_dimension=0, tiled=True
    ).astype(F32)


def body(
    target,
    source,
    target_len,
    source_len,
    self_query,
    self_key,
    self_value,
    self_output,
    cross_query,
    cross_key,
    cross_value,
    cross_output,
    feed_in,
    feed_out,
    adapter_down,
    adapter_up,
    self_gain,
    self_shift,
    cross_gain,
    cross_shift,
    final_gain,
    final_shift,
    cotangent,
):
    block, seqs, width = target.shape
    dp, seq = lax.axis_size("dp"), lax.axis_size("seq")
    group = seq // seqs
    rows = seqs * block
    here, there = lax.axis_index("dp"), lax.axis_index("seq")
    inner, which = there % group, there // group
    core = there % 2
    halving = dp == 4 and seq == 8
    apart = [[start + group * step for step in range(seqs)] for start in range(group)]

    def to_sequence(item):
        return lax.all_to_all(
            item.swapaxes(0, 1), "seq", 0, 0, axis_index_groups=apart, tiled=True
        ).reshape(rows, item.shape[-1])

    slots = jnp.stack([which ^ bit for bit in range(seqs)]).astype(jnp.int32)

    def send_back(item):
        item = item.reshape(seqs, block, item.shape[-1])
        parts = [item]
        for bit in range(1, seqs):
            pairs = [(index, (index // group ^ bit) * group + index % group) for index in range(seq)]
            parts.append(lax.ppermute(take(item, which ^ bit, 0), "seq", pairs))
        return parts

    def set_down(parts, *others):
        item, *parts = lax.optimization_barrier((*parts, *others))[: len(parts)]
        return laid_out(slots, item, parts).swapaxes(0, 1)

    def near(shift):
        return [
            (k * group + c, k * group + (c + shift) % group)
            for k in range(seqs)
            for c in range(group)
        ]

    def spread(item):
        return [item] + [lax.ppermute(item, "seq", near(-s)) for s in range(1, group)]

    def collect(own, others):
        for shift, other in enumerate(others, 1):
            own = own + lax.ppermute(other, "seq", near(shift)).astype(F32)
        return own.astype(BF16)

    own_inputs, own_memory = to_sequence(target), to_sequence(source)
    inputs, memory = view(own_inputs, width, 0), view(own_memory, width, 0)
    grad_out = to_sequence(cotangent)
    vectors = jnp.stack([self_gain, self_shift, cross_gain, cross_shift, final_gain, final_shift])
    if halving:
        one = jnp.where(core == 0, here ^ 1, here ^ 2)
        two = jnp.where(core == 0, here ^ 2, here ^ 1)
        diagonal = here ^ 3
        chunks = [item * 2 + part for item in (here, one, two) for part in (0, 1)]
        chunks += [diagonal * 2 + core, diagonal * 2 + 1 - core]
        place = jnp.stack([here, one, two, diagonal, core, core, core, core] + chunks)
        first_group = jnp.concatenate(
            [self_query, self_key, self_value, cross_key, cross_value], axis=1
        )
        half = width // 2
        up_packed = jnp.concatenate([adapter_up[:, :half], adapter_up[:, half:]], axis=0)
        second_group = jnp.concatenate(
            [self_output, cross_query, cross_output, adapter_down, up_packed], axis=1
        )
        vector_parts = [vectors] + [
            lax.ppermute(vectors, "dp", swap_pairs(4, bit)) for bit in (1, 2, 3)
        ]
        w_self = gather_rest(gather_first(first_group), core, own_inputs, *vector_parts)
        w_mid = gather_first(after(second_group, w_self[3]))
        at_q, at_kv, at_ckv = (w_self, 0), (w_self, 1), (w_self, 3)
        parts = jnp.stack(vector_parts)
        vectors = jnp.concatenate([take(parts, here ^ slot, 0) for slot in range(4)], axis=1)
        counts_first, counts_second = (2, 2), (2, 1, 1)
    else:
        steps = feed_in.shape[1] // CHUNK
        place = jnp.stack([jnp.int32(0)] * 8 + [jnp.int32(j) for j in range(steps)])
        at_q = (gather_dp(self_query), 0)
        at_kv = (gather_dp(jnp.concatenate([self_key, self_value], axis=1)), 0)
        at_o, at_cq = (gather_dp(self_output), 0), (gather_dp(cross_query), 0)
        at_ckv = (gather_dp(jnp.concatenate([cross_key, cross_value], axis=1)), 0)
        at_co = (gather_dp(cross_output), 0)
        w_in, w_out = gather_dp(feed_in), gather_dp(feed_out)
        at_down, at_up = (gather_dp(adapter_down), 0), (gather_dp(adapter_up), 0)
        vectors = lax.all_gather(vectors, "dp", axis=1, tiled=True)
        out_first = out_second = w_out
        counts_first, counts_second = (steps // 2,), (steps - steps // 2,)
    place = place.astype(jnp.int32)
    vectors = vectors.astype(F32)
    norm_one, norm_two, norm_three = vectors[0:2], vectors[2:4], vectors[4:6]

    local = jnp.arange(rows, dtype=jnp.int32)

    def positions(place_in_group):
        return (local // block * group + place_in_group) * block + local % block

    target_limit = take(target_len, which, 0)
    source_limit = take(source_len, which, 0)
    key_pos = jnp.stack([positions((inner + shift) % group) for shift in range(group)])
    self_keys = jnp.where(key_pos < target_limit, key_pos, NEVER)[..., None]
    cross_keys = jnp.where(key_pos < source_limit, key_pos, NEVER)[..., None]
    self_rows = positions(inner)[None]
    cross_rows = jnp.full((1, rows), ALWAYS, jnp.int32)

    kv_own = project(place, inputs, *at_kv, 2, "self_kv")
    kv_all = spread(kv_own)
    queries = project(place, inputs, *at_q, 1, "self_q")
    if halving:
        w_mid = gather_rest(w_mid, core, queries)
        w_in = gather_first(after(feed_in, w_mid[1], queries))
    mixed, totals = attend_forward(queries, kv_all, self_keys, self_rows, block, True)
    ckv_own = project(
        place, (after(own_memory, mixed), memory[1]), *at_ckv, 2, "cross_kv"
    )
    ckv_all = spread(ckv_own)
    mixed = after(mixed, ckv_own)
    if halving:
        w_out = gather_first(after(feed_out, w_mid[1], mixed))
        at_o, at_cq, at_co = (w_mid, 0), (w_mid, 1), (w_mid, 2)
        at_down, at_up = (w_mid, 6), (w_mid, 7)
    resid_one, first, first_low, cross_q = mix(
        place, mixed, inputs, norm_one, *at_o, *at_cq, "mix_self"
    )
    if halving:
        w_in = gather_rest(w_in, core, cross_q)
    cross_mixed, cross_totals = attend_forward(
        cross_q, ckv_all, cross_keys, cross_rows, block, False
    )
    if halving:
        w_out = gather_rest(w_out, core, cross_mixed)
        out_first, out_second = w_out[:2], w_out[2:]
    resid_two, second, second_low = mix(
        place, cross_mixed, view(first, width, 0), norm_two, *at_co, None, None, "mix_cross"
    )
    partial, slope, hidden, adapter_slope = feed_first(
        place, second_low, second, w_in, out_first, counts_first, *at_down, *at_up
    )
    final, d_three, d_branch, d_norm_three, later = feed_second(
        place,
        second_low,
        partial,
        grad_out,
        norm_three,
        w_in,
        out_second,
        counts_second,
        sum(counts_first),
    )
    output = send_back(final)

    d_two, d_two_low, d_norm_two, d_adapter, d_cross = feed_backward(
        place,
        d_branch,
        d_three,
        resid_two,
        norm_two,
        slope,
        later,
        adapter_slope,
        w_in,
        w_out,
        counts_first + counts_second if halving else (steps,),
        *at_down,
        *at_up,
        *at_co,
    )

    d_two_low = after(d_two_low, output[1], output[2])

    def whole(item, layer=0):
        return view(item, item.shape[-1], layer)

    pairs = width // PAIR
    if halving:
        half = width // 2
        left = whole(cross_mixed)
        early = wgrad(
            place,
            [left, left, whole(second_low), whole(hidden)],
            [view(d_two_low, half, 0), view(d_two_low, half, 1), whole(d_adapter), whole(d_branch)],
            half,
            False,
            (1.0, 1.0, 1.0, 4.0),
            "wgrad_early",
        )[0]
        d_cross = after(d_cross, early)
        early = sum_over(early, "seq")
    d_cq, *d_ckv = attend_backward(
        cross_q,
        ckv_all,
        cross_mixed,
        d_cross,
        cross_totals,
        cross_keys,
        cross_rows,
        block,
        False,
        0,
        pairs,
    )
    d_cq = after(d_cq, output[3])
    output = set_down(output, d_cq)
    d_one, d_one_low, d_norm_one, d_mixed = norm_step(
        place, d_cq, d_two, resid_one, norm_one, *at_cq, *at_o
    )
    d_ckv = collect(after(d_ckv[0], d_one_low), d_ckv[1:])
    if halving:
        middle = wgrad(
            place,
            [memory, memory],
            [whole(d_ckv, 0), whole(d_ckv, 1)],
            width,
            False,
            (1.0,) * 2,
            "wgrad_memory",
            [d_norm_one, d_norm_two, d_norm_three],
        )[0]
        d_one_low = after(d_one_low, middle)
        middle = sum_over(after(middle, early), "seq")
        d_one_low = after(d_one_low, early)
        inner_sums = Scatter(
            *wgrad(
                place,
                [whole(mixed), whole(first_low)],
                [whole(d_one_low), whole(d_cq)],
                width,
                True,
                (1.0,) * 2,
                "wgrad_inner",
            )
        )
        d_ckv = after(d_ckv, inner_sums.send)
    grad_source = inputs_back(
        place,
        [whole(d_ckv, 0), whole(d_ckv, 1)],
        at_ckv[0],
        [at_ckv[1], at_ckv[1] + 1],
        None,
        None,
        "source_back",
    )
    d_mixed = after(d_mixed, grad_source)
    if halving:
        d_mixed = after(d_mixed, inner_sums.core())
    grad_source = send_back(grad_source)

    def self_backward(grads, first_pair):
        return attend_backward(
            queries,
            kv_all,
            mixed,
            grads,
            totals,
            self_keys,
            self_rows,
            block,
            True,
            first_pair,
            pairs // 2,
        )

    def self_sums(d_q, d_kv):
        return Scatter(
            *wgrad(
                place,
                [inputs] * 3,
                [whole(d_q), whole(d_kv, 0), whole(d_kv, 1)],
                width // 2,
                True,
                (1.0,) * 3,
                "wgrad_self",
            )
        )

    d_q_one, *d_kv_one = self_backward(d_mixed, 0)
    d_mixed = after(d_mixed, d_q_one, grad_source[1])
    if halving:
        d_mixed = after(d_mixed, inner_sums.plane_one())
    d_q_two, *d_kv_two = self_backward(d_mixed, pairs // 2)
    d_kv_one = collect(after(d_kv_one[0], d_q_two), d_kv_one[1:])
    if halving:
        d_q_one = after(d_q_one, d_q_two, grad_source[2], inner_sums.plane_two())
        late_one = self_sums(d_q_one, d_kv_one)
        d_kv_two[0] = after(d_kv_two[0], late_one.send)
    d_kv_two = collect(d_kv_two[0], d_kv_two[1:])
    if halving:
        d_q_two = after(d_q_two, late_one.core(), inner_sums.z_one(), middle)
        late_two = self_sums(d_q_two, d_kv_two)
        grad_source = set_down(grad_source, late_two.send)
        d_q_one = after(d_q_one, late_two.send, grad_source)
    at_self = at_q if halving else ((jnp.concatenate([at_q[0][0], at_kv[0][0]], axis=1),), 0)
    grad_target = inputs_back(
        place,
        [
            whole(d_q_one),
            whole(d_q_two),
            whole(d_kv_one, 0),
            whole(d_kv_two, 0),
            whole(d_kv_one, 1),
            whole(d_kv_two, 1),
        ],
        at_self[0],
        [2 * at_self[1] + index for index in range(6)],
        "base",
        d_one,
        "target_back",
    )
    grad_target = send_back(grad_target)
    if not halving:
        grad_source = set_down(grad_source)
        grad_target = set_down(grad_target)
    if halving:
        both = sum_over(jnp.concatenate([early, middle], axis=1), "dp").astype(F32)
        early, middle = both[:, : early.shape[1]], both[:, early.shape[1] :]
        grad_co, grad_down = early[:, :width], early[:, width : width + half]
        lifted = early[:, width + half :]
        folded = lifted.shape[0] // 2
        grad_up = jnp.concatenate([lifted[:folded], lifted[folded:]], axis=1)
        grad_ck, grad_cv = middle[:, :width], middle[:, width : 2 * width]
        norm_sums = middle[:, 2 * width : 2 * width + 6].T
        late_one.plane_one()
        late_two.core()
        late_one.plane_two()
        late_two.plane_one()
        inner_sums.z_two()
        late_two.plane_two()
        grad_target = set_down(grad_target, late_two.item, both)
        for late in (late_one, late_two):
            late.z_one()
            late.z_two()
        grad_o, grad_cq = inner_sums.item[:, :width], inner_sums.item[:, width:]
        grad_q, grad_k, grad_v = [
            jnp.concatenate(
                [late.item[:, index * half : (index + 1) * half] for late in (late_one, late_two)],
                axis=1,
            )
            for index in range(3)
        ]
    else:
        norm_sums = jnp.concatenate([d_norm_one, d_norm_two, d_norm_three], axis=0)
        norm_sums = lax.psum_scatter(norm_sums, ("dp", "seq"), scatter_dimension=1, tiled=True)
        grad_down = sum_all(dot_tn(second_low, d_adapter))
        grad_up = sum_all(4.0 * dot_tn(hidden, d_branch))
        grad_co = sum_all(dot_tn(cross_mixed, d_two_low))
        grad_o = sum_all(dot_tn(mixed, d_one_low))
        grad_cq = sum_all(dot_tn(first_low, d_cq))
        grad_ck = sum_all(dot_tn(own_memory, d_ckv[0]))
        grad_cv = sum_all(dot_tn(own_memory, d_ckv[1]))
        d_q = jnp.concatenate([d_q_one, d_q_two], axis=1)
        d_kv = jnp.concatenate([d_kv_one, d_kv_two], axis=2)
        grad_q = sum_all(dot_tn(own_inputs, d_q))
        grad_k = sum_all(dot_tn(own_inputs, d_kv[0]))
        grad_v = sum_all(dot_tn(own_inputs, d_kv[1]))
    return (
        output,
        grad_target,
        grad_source,
        grad_q,
        grad_k,
        grad_v,
        grad_o,
        grad_cq,
        grad_ck,
        grad_cv,
        grad_co,
        grad_down,
        grad_up,
        *[norm_sums[index] for index in range(6)],
    )


def solution(mesh):
    tokens = P("seq", "dp", None)
    rows = P("dp", None)
    vector = P("dp")
    both = P(("dp", "seq"), None)
    return jax.shard_map(
        body,
        mesh=mesh,
        in_specs=(tokens, tokens, vector, vector) + (rows,) * 12 + (vector,) * 6 + (tokens,),
        out_specs=(tokens,) * 3 + (both,) * 10 + (P(("dp", "seq")),) * 6,
        check_vma=False,
    )
```

time: 746 us -> 548 us (0.73)
  matrix products: 145 us -> 0 us
  Pallas kernels: 117 us -> 233 us
  waiting for transfers between devices: 222 us -> 110 us
  other arithmetic: 64.2 us -> 23.3 us
  local copies, waits for them, and re-layouts: 97.2 us -> 81.8 us
  blocking collectives: 8.32 us -> 0 us
    dot_general x31 -> x0, matrix products: 145 us -> none  [the longest x10 71.1 us: dot(): return jnp.dot(left, right, preferred_element_type=F32)]
    pallas_call x6 -> x19, Pallas kernels: 24.7 us -> 141 us  [run(): pl.pallas_call(kernel, grid_spec=pltpu.PrefetchScalarGridSpec(num_scalar_...]
    ppermute x47 -> x49, waiting for transfers between devices: 184 us -> 109 us  [the longest x9 23.8 us: send_back(): parts.append(lax.ppermute(take(item, which ^ bit, 0), 'seq', pairs))]
    unnamed x174 -> x228, local copies, waits for them, and re-layouts: 32.5 us -> 62.6 us
    concatenate x6 -> x1, local copies, waits for them, and re-layouts: 27.8 us -> 0.86 us  [body(): jnp.concatenate([self_query, self_key, self_value, cross_key, cross_value...]
    all_gather x4 -> x0, waiting for transfers between devices: 25.9 us -> none  [gather_all(): return lax.all_gather(mine, ('dp', 'seq'), axis=0, tiled=True)]
    ppermute x47 -> x49, starting transfers between devices: 36.9 us -> 58.3 us  [the longest x9 17.8 us: send_back(): parts.append(lax.ppermute(take(item, which ^ bit, 0), 'seq', pairs))]
    concatenate x9, other arithmetic: 22.6 us -> 5.5 us  [the longest x3 1.99 us: body(): jnp.concatenate([late.item[:, index * half:(index + 1) * half] for late i...]
  transfers between devices with their start and end apart: 61 -> 60, of which waited for: 19 -> 19; matrix products, arithmetic and copies ran while one was open for 33% -> 9% of each run, Pallas kernels for 12% -> 39%
where the time goes in v2:
time: 548 us; the launch traced here: 537 us
  Pallas kernels  233 us (43%)
  waiting for transfers between devices  110 us (20%)
  local copies, waits for them, and re-layouts  81.8 us (15%)
  starting transfers between devices  73.5 us (13%)
  other arithmetic  23.3 us (4%)
  between operations  15.5 us (3%)
    pallas_call x19, Pallas kernels, run(): pl.pallas_call(kernel, grid_spec=pltpu.PrefetchScalarGridSpec(num_scalar_...  141 us
    unnamed x228, local copies, waits for them, and re-layouts  62.6 us
    pallas_call x3, Pallas kernels, attend_backward(): pl.pallas_call(functools.partial(backward_kernel, pieces, block, causal),...  51.6 us
    pallas_call x2, Pallas kernels, attend_forward(): pl.pallas_call(functools.partial(forward_kernel, pieces, block, causal),...  40.6 us
    ppermute x9, waiting for transfers between devices, send_back(): parts.append(lax.ppermute(take(item, which ^ bit, 0), 'seq', pairs))  23.8 us
    ppermute x3, waiting for transfers between devices, body(): lax.ppermute(vectors, 'dp', swap_pairs(4, bit))  21.5 us
    ppermute x9, starting transfers between devices, send_back(): parts.append(lax.ppermute(take(item, which ^ bit, 0), 'seq', pairs))  17.8 us
    ppermute x4, waiting for transfers between devices, gather_rest(): near = lax.ppermute(half_one, ('dp', 'seq'), by_core(2, 1))  15.8 us
  transfers between devices with their start and end apart: 60, of which 19 were waited for; matrix products, arithmetic and copies ran while one was open for 9% of the time, Pallas kernels for 39%

profile of v2, /device:TPU:0, one launch (start us, length us, event | category | flops | bytes accessed | tf_op | source)
XLA Modules:
  0.0 537.3 jit_solution(6669725576192206516)
XLA Ops:
  26.9 20.0 %collective-permute-done.2 = bf16[6,256]{1,0:T(8,128)(2,1)S(1)} collective-permute-done((bf16[6,256]{1,0:T(8,128)(2,1)S(1)}, bf16[6,256]{1,0:T(8,128)(2,1)S(1)}, u32[]{:S(2)}, u32[]{:S(2)}) %collective-permute-start.2) | collective-permute-done | bytes 3104 | tf_op jit(solution)/shard_map/ppermute | solution.py:1118
  53.0 13.7 %collective-permute-done.5.refs_3_.refs_5_.refs_9_ = bf16[128,5120]{1,0:T(8,128)(2,1)} collective-permute-done((bf16[128,5120]{1,0:T(8,128)(2,1)S(1)}, bf16[128,5120]{1,0:T(8,128)(2,1)}, u32[]{:S(2)}, u32[]{:S(2)}) %collective-permute-start.5) | collective-permute-done | bytes 1310752 | tf_op jit(solution)/shard_map/ppermute | solution.py:891
  70.1 6.5 %self_kv.1.refs_3_.refs_5_.refs_6_.refs_8_ = bf16[512,2048]{1,0:T(8,128)(2,1)} custom-call(s32[16]{0:T(128)S(1)} %stack.123.place, bf16[512,1024]{1,0:T(8,128)(2,1)} %bitcast.18.left_ref.resid_ref.refs_0_.refs_1_.refs_2_, bf16[256,5120]{1,0:T(8,128)(2,1)} %constant_dynamic-update-slice_fusion.refs_0_.refs_2_.refs_6_, ...), custom_call_target="tpu_custom_call" | custom-call | flops 5750000128 | bytes 18000000 | tf_op jit(solution)/shard_map/self_kv/pallas_call | solution.py:322
  80.3 13.5 %collective-permute-done.8.refs_1_.refs_6_.refs_8_.refs_13_.refs_11_.refs_16_.refs_21_ = bf16[256,4096]{1,0:T(8,128)(2,1)} collective-permute-done((bf16[256,4096]{1,0:T(8,128)(2,1)}, bf16[256,4096]{1,0:T(8,128)(2,1)}, u32[]{:S(2)}, u32[]{:S(2)}) %collective-permute-start.8) | collective-permute-done | bytes 2097184 | tf_op jit(solution)/shard_map/ppermute | solution.py:883
  112.7 17.9 %attend_forward.2 = (bf16[512,1024]{1,0:T(8,128)(2,1)S(1)}, f32[8,2,512]{2,1,0:T(2,128)S(1)}) custom-call(bf16[512,1024]{1,0:T(8,128)(2,1)S(1)} %copy-done.5, s32[2,512,1]{2,1,0:T(8,128)S(1)} %get-tuple-element.281.refs_1_.refs_4_, s32[1,512]{1,0:T(1,128)S(1)} %multiply_add_fusion.refs_2_.refs_5_, bf16[512,2048]{1,0:T(8,128)(2,1)} %self_kv.1.refs_3_.refs_5_.refs_6_.refs_8_, ...), custom_call_target="tpu_custom_call" | custom-call | flops 20700000256 | bytes 64800000 | tf_op jit(solution)/shard_map/attend_forward/pallas_call | solution.py:155
  132.4 6.5 %cross_kv.1.refs_3_.refs_5_.refs_6_.refs_8_ = bf16[512,2048]{1,0:T(8,128)(2,1)} custom-call(s32[16]{0:T(128)S(1)} %stack.123.place, bf16[512,1024]{1,0:T(8,128)(2,1)} %bitcast.23.left_ref.refs_0_.refs_1_, bf16[256,5120]{1,0:T(8,128)(2,1)} %constant_dynamic-update-slice_fusion.refs_0_.refs_2_.refs_6_, ...), custom_call_target="tpu_custom_call" | custom-call | flops 5750000128 | bytes 18000000 | tf_op jit(solution)/shard_map/cross_kv/pallas_call | solution.py:322
  143.2 9.2 %mix_self.1 = (f32[512,1024]{1,0:T(8,128)}, f32[512,1024]{1,0:T(8,128)}, bf16[512,1024]{1,0:T(8,128)(2,1)}, bf16[512,1024]{1,0:T(8,128)(2,1)S(1)}) custom-call(s32[16]{0:T(128)S(1)} %stack.123.place, bf16[512,1024]{1,0:T(8,128)(2,1)S(1)} %copy-done.63, bf16[512,1024]{1,0:T(8,128)(2,1)} %bitcast.18.left_ref.resid_ref.refs_0_.refs_1_.refs_2_, ...), custom_call_target="tpu_custom_call" | custom-call | flops 7245000192 | bytes 22680000 | tf_op jit(solution)/shard_map/mix_self/pallas_call | solution.py:322
  154.7 22.7 %attend_forward.3 = (bf16[512,1024]{1,0:T(8,128)(2,1)S(1)}, f32[8,2,512]{2,1,0:T(2,128)S(1)}) custom-call(bf16[512,1024]{1,0:T(8,128)(2,1)S(1)} %get-tuple-element.107.refs_0_, s32[2,512,1]{2,1,0:T(8,128)S(1)} %get-tuple-element.280.refs_1_.refs_4_, s32[1,512]{1,0:T(1,128)S(1)} %broadcast_in_dim.12.refs_2_.refs_5_, ...), custom_call_target="tpu_custom_call" | custom-call | flops 25300000768 | bytes 79200000 | tf_op jit(solution)/shard_map/attend_forward/pallas_call | solution.py:155
  190.9 6.5 %mix_cross.1 = (f32[512,1024]{1,0:T(8,128)}, f32[512,1024]{1,0:T(8,128)}, bf16[512,1024]{1,0:T(8,128)(2,1)}) custom-call(s32[16]{0:T(128)S(1)} %stack.123.place, bf16[512,1024]{1,0:T(8,128)(2,1)S(1)} %copy-done.35, f32[512,1024]{1,0:T(8,128)S(1)} %copy-done.46, f32[2,1024]{1,0:T(2,128)S(1)} %get-tuple-element.298.norm_ref, ...), custom_call_target="tpu_custom_call" | custom-call | flops 4600000000 | bytes 14400000 | tf_op jit(solution)/shard_map/mix_cross/pallas_call | solution.py:322
  200.3 13.6 %feed_first.1 = (f32[512,1024]{1,0:T(8,128)S(1)}, bf16[512,2048]{1,0:T(8,128)(2,1)}, bf16[512,512]{1,0:T(8,128)(2,1)}, bf16[512,512]{1,0:T(8,128)(2,1)}) custom-call(s32[16]{0:T(128)S(1)} %stack.123.place, bf16[512,1024]{1,0:T(8,128)(2,1)S(1)} %copy-done.38, f32[512,1024]{1,0:T(8,128)S(1)} %copy-done.47, bf16[256,4096]{1,0:T(8,128)(2,1)S(1)} %copy-done.23, ...), custom_call_target="tpu_custom_call" | custom-call | flops 14949999616 | bytes 46800000 | tf_op jit(solution)/shard_map/feed_first/pallas_call | solution.py:322
  219.7 13.5 %feed_second.1 = (bf16[512,1024]{1,0:T(8,128)(2,1)}, f32[512,1024]{1,0:T(8,128)S(1)}, bf16[512,1024]{1,0:T(8,128)(2,1)S(1)}, f32[2,1024]{1,0:T(2,128)}, bf16[512,2048]{1,0:T(8,128)(2,1)}) custom-call(s32[16]{0:T(128)S(1)} %stack.123.place, bf16[512,1024]{1,0:T(8,128)(2,1)S(1)} %copy-done.39, f32[512,1024]{1,0:T(8,128)S(1)} %copy-done.70, ...), custom_call_target="tpu_custom_call" | custom-call | flops 15525000192 | bytes 48600000 | tf_op jit(solution)/shard_map/feed_second/pallas_call | solution.py:322
  241.2 30.1 %feed_backward.1 = (f32[512,1024]{1,0:T(8,128)}, bf16[512,1024]{1,0:T(8,128)(2,1)}, f32[2,1024]{1,0:T(2,128)}, bf16[512,512]{1,0:T(8,128)(2,1)}, bf16[512,1024]{1,0:T(8,128)(2,1)}) custom-call(s32[16]{0:T(128)} %copy-done.19, bf16[512,1024]{1,0:T(8,128)(2,1)} %copy-done.41, f32[512,1024]{1,0:T(8,128)} %copy-done.71, ...), custom_call_target="tpu_custom_call" | custom-call | flops 33350000640 | bytes 104400000 | tf_op jit(solution)/shard_map/feed_backward/pallas_call | solution.py:322
  283.2 28.0 %attend_backward.3 = (bf16[512,1024]{1,0:T(8,128)(2,1)S(1)}, f32[2,512,1024]{2,1,0:T(8,128)S(1)}, bf16[2,512,1024]{2,1,0:T(8,128)(2,1)S(1)}) custom-call(bf16[512,1024]{1,0:T(8,128)(2,1)S(1)} %copy-done.68, bf16[512,1024]{1,0:T(8,128)(2,1)S(1)} %copy-done.37, bf16[512,1024]{1,0:T(8,128)(2,1)S(1)} %copy-done.75, f32[8,2,512]{2,1,0:T(2,128)S(1)} %get-tuple-element.130.refs_3_, ...), custom_call_target="tpu_custom_call" | custom-call | flops 32199999488 | bytes 100800000 | tf_op jit(solution)/shard_map/attend_backward/pallas_call | solution.py:243
  311.3 16.5 %collective-permute-done.23.refs_2_ = bf16[128,1024]{1,0:T(8,128)(2,1)S(1)} collective-permute-done((bf16[128,1024]{1,0:T(8,128)(2,1)S(1)}, bf16[128,1024]{1,0:T(8,128)(2,1)S(1)}, u32[]{:S(2)}, u32[]{:S(2)}) %collective-permute-start.23) | collective-permute-done | bytes 262176 | tf_op jit(solution)/shard_map/ppermute | solution.py:1076
  329.5 8.1 %norm_step.1 = (f32[512,1024]{1,0:T(8,128)}, bf16[512,1024]{1,0:T(8,128)(2,1)S(1)}, f32[2,1024]{1,0:T(2,128)}, bf16[512,1024]{1,0:T(8,128)(2,1)S(1)}) custom-call(s32[16]{0:T(128)S(1)} %copy-done.20, bf16[512,1024]{1,0:T(8,128)(2,1)S(1)} %get-tuple-element.132.dquery_ref.refs_3_, f32[512,1024]{1,0:T(8,128)S(1)} %copy-done.50, f32[512,1024]{1,0:T(8,128)S(1)} %copy-done.49, ...), custom_call_target="tpu_custom_call" | custom-call | flops 7590000128 | bytes 23760000 | tf_op jit(solution)/shard_map/norm_step/pallas_call | solution.py:322
  340.9 6.2 %wgrad_memory.1 = bf16[1024,2176]{1,0:T(8,128)(2,1)} custom-call(s32[16]{0:T(128)S(1)} %copy-done.20, bf16[512,1024]{1,0:T(8,128)(2,1)} %bitcast.23.left_ref.refs_0_.refs_1_, bf16[512,1024]{1,0:T(8,128)(2,1)} %bitcast.23.left_ref.refs_0_.refs_1_, bf16[2,512,1024]{2,1,0:T(8,128)(2,1)S(1)} %add_convert_fusion.1.refs_2_.refs_3_.refs_0_.refs_1_, ...), custom_call_target="tpu_custom_call" | custom-call | flops 3680000000 | bytes 11520000 | tf_op jit(solution)/shard_map/wgrad_memory/pallas_call | solution.py:322
  366.5 6.9 %collective-permute-start.26 = (bf16[128,1024]{1,0:T(8,128)(2,1)S(1)}, bf16[128,1024]{1,0:T(8,128)(2,1)S(1)}, u32[]{:S(2)}, u32[]{:S(2)}) collective-permute-start(bf16[128,1024]{1,0:T(8,128)(2,1)S(1)} %get-tuple-element.276), channel_id=1, source_target_pairs={{0,2},{1,3},{2,0},{3,1},{4,6},{5,7},{6,4},{7,5},{8,10},{9,11},{10,... | collective-permute-start | bytes 786440 | tf_op jit(solution)/shard_map/ppermute | solution.py:1076
  378.7 11.8 %attend_backward.4 = (bf16[512,512]{1,0:T(8,128)(2,1)S(1)}, f32[2,512,512]{2,1,0:T(8,128)S(1)}, bf16[2,512,512]{2,1,0:T(8,128)(2,1)S(1)}) custom-call(bf16[512,1024]{1,0:T(8,128)(2,1)S(1)} %copy-done.6, bf16[512,1024]{1,0:T(8,128)(2,1)S(1)} %copy-done.65, bf16[512,1024]{1,0:T(8,128)(2,1)S(1)} %copy-done.52, f32[8,2,512]{2,1,0:T(2,128)S(1)} %get-tuple-element.155.refs_3_, ...), custom_call_target="tpu_custom_call" | custom-call | flops 13799999488 | bytes 43200000 | tf_op jit(solution)/shard_map/attend_backward/pallas_call | solution.py:243
  397.1 11.8 %attend_backward.5 = (bf16[512,512]{1,0:T(8,128)(2,1)S(1)}, f32[2,512,512]{2,1,0:T(8,128)S(1)}, bf16[2,512,512]{2,1,0:T(8,128)(2,1)S(1)}) custom-call(bf16[512,1024]{1,0:T(8,128)(2,1)S(1)} %copy-done.6, bf16[512,1024]{1,0:T(8,128)(2,1)S(1)} %copy-done.65, bf16[512,1024]{1,0:T(8,128)(2,1)S(1)} %copy-done.52, f32[8,2,512]{2,1,0:T(2,128)S(1)} %get-tuple-element.155.refs_3_, ...), custom_call_target="tpu_custom_call" | custom-call | flops 13799999488 | bytes 43200000 | tf_op jit(solution)/shard_map/attend_backward/pallas_call | solution.py:243
  412.6 6.6 %wgrad_self.2 = (bf16[512,1536]{1,0:T(8,128)(2,1)}, bf16[512,1536]{1,0:T(8,128)(2,1)}) custom-call(s32[16]{0:T(128)S(1)} %copy-done.20, bf16[512,1024]{1,0:T(8,128)(2,1)} %bitcast.18.left_ref.resid_ref.refs_0_.refs_1_.refs_2_, bf16[512,1024]{1,0:T(8,128)(2,1)} %bitcast.18.left_ref.resid_ref.refs_0_.refs_1_.refs_2_, ...), custom_call_target="tpu_custom_call" | custom-call | flops 2760000000 | bytes 8640000 | tf_op jit(solution)/shard_map/wgrad_self/pallas_call | solution.py:322
  436.4 10.0 %collective-permute-done.53 = bf16[32,2048]{1,0:T(8,128)(2,1)S(1)} collective-permute-done((bf16[32,2048]{1,0:T(8,128)(2,1)S(1)}, bf16[32,2048]{1,0:T(8,128)(2,1)S(1)}, u32[]{:S(2)}, u32[]{:S(2)}) %collective-permute-start.53) | collective-permute-done | bytes 131104 | tf_op jit(solution)/shard_map/ppermute | solution.py:1018
  462.6 6.2 %wgrad_self.3 = (bf16[512,1536]{1,0:T(8,128)(2,1)}, bf16[512,1536]{1,0:T(8,128)(2,1)}) custom-call(s32[16]{0:T(128)S(1)} %copy-done.20, bf16[512,1024]{1,0:T(8,128)(2,1)} %bitcast.18.left_ref.resid_ref.refs_0_.refs_1_.refs_2_, bf16[512,1024]{1,0:T(8,128)(2,1)} %bitcast.18.left_ref.resid_ref.refs_0_.refs_1_.refs_2_, ...), custom_call_target="tpu_custom_call" | custom-call | flops 2760000000 | bytes 8640000 | tf_op jit(solution)/shard_map/wgrad_self/pallas_call | solution.py:322
  478.8 7.9 %target_back.1 = bf16[512,1024]{1,0:T(8,128)(2,1)S(1)} custom-call(s32[16]{0:T(128)S(1)} %copy-done.20, bf16[512,512]{1,0:T(8,128)(2,1)S(1)} %copy-done.58, bf16[512,512]{1,0:T(8,128)(2,1)S(1)} %copy-done.61, bf16[2,512,512]{2,1,0:T(8,128)(2,1)S(1)} %copy-done.8, bf16[2,512,512]{2,1,0:T(8,128)(2,1)S(1)} %copy-done.10, bf16[2,512,512]{2,1,0:T(8,128)(2,1)S(1)} %copy-done.8, ...), custom_call_target="tpu_custom_call" | custom-call | flops 10350000128 | bytes 32400000 | tf_op jit(solution)/shard_map/target_back/pallas_call | solution.py:322
  519.3 5.6 %collective-permute-start.52 = (bf16[32,1536]{1,0:T(8,128)(2,1)S(1)}, bf16[32,1536]{1,0:T(8,128)(2,1)S(1)}, u32[]{:S(2)}, u32[]{:S(2)}) collective-permute-start(bf16[32,1536]{1,0:T(8,128)(2,1)S(1)} %dynamic-slice_bitcast_fusion.25), channel_id=1, source_target_pairs={{0,4},{1,5},{2,6},{3,7},{4,0},{5,1},{6,2},{7,3},{8,12},{9,13},{10,... | collective-permute-start | bytes 294920 | tf_op jit(solution)/shard_map/ppermute | solution.py:1018
  (443 shorter events, 222.3 us)
Async XLA Ops:
  13.9 34.9 %collective-permute-start = (bf16[256,5120]{1,0:T(8,128)(2,1)}, bf16[256,5120]{1,0:T(8,128)(2,1)S(1)}, u32[]{:S(2)}, u32[]{:S(2)}) collective-permute-start(bf16[256,5120]{1,0:T(8,128)(2,1)} %constant_dynamic-update-slice_fusion.refs_0_.refs_2_.refs_6_), channel_id=1, source_target_pairs={{0,8},{1,17},{2,10},{3,19},{4,12},{5,21},{6,14},{7,23},{8,0},{9,25... | collective-permute-start | bytes 7864328 | tf_op jit(solution)/shard_map/ppermute | solution.py:883
  18.2 30.6 %all-to-all-start = ((bf16[4,128,1024]{2,1,0:T(8,128)(2,1)}), bf16[4,128,1024]{2,1,0:T(8,128)(2,1)}, u32[]{:S(2)}, u32[]{:S(2)}) async-start(bf16[4,128,1024]{2,1,0:T(8,128)(2,1)} %bitcast.184), calls=%async_computation | async-start | bytes 2097152 | tf_op jit(solution)/shard_map/all_to_all | solution.py:1065
  23.3 23.5 %collective-permute-start.2 = (bf16[6,256]{1,0:T(8,128)(2,1)S(1)}, bf16[6,256]{1,0:T(8,128)(2,1)S(1)}, u32[]{:S(2)}, u32[]{:S(2)}) collective-permute-start(bf16[6,256]{1,0:T(8,128)(2,1)S(1)} %stack.130), channel_id=1, source_target_pairs={{0,8},{8,0},{16,24},{24,16},{1,9},{9,1},{17,25},{25,17},{2,10},{10... | collective-permute-start | bytes 9224 | tf_op jit(solution)/shard_map/ppermute | solution.py:1118
  67.4 26.4 %collective-permute-start.8 = (bf16[256,4096]{1,0:T(8,128)(2,1)}, bf16[256,4096]{1,0:T(8,128)(2,1)}, u32[]{:S(2)}, u32[]{:S(2)}) collective-permute-start(bf16[256,4096]{1,0:T(8,128)(2,1)} %maximum_dynamic-update-slice_fusion.refs_0_.refs_5_.refs_7_.refs_12_.refs_10_.refs_15_.refs_20_), channel_id=1, source_target_pairs={{0,8},{1,17},{2,10},{3,19},{4,12},{5,21},{6,14},{7,23},{8,0},{9,25... | collective-permute-start | bytes 6291464 | tf_op jit(solution)/shard_map/ppermute | solution.py:883
  76.5 34.9 %collective-permute-start.7 = (bf16[512,2048]{1,0:T(8,128)(2,1)}, bf16[512,2048]{1,0:T(8,128)(2,1)}, u32[]{:S(2)}, u32[]{:S(2)}) collective-permute-start(bf16[512,2048]{1,0:T(8,128)(2,1)} %self_kv.1.refs_3_.refs_5_.refs_6_.refs_8_), channel_id=1, source_target_pairs={{0,1},{1,0},{2,3},{3,2},{4,5},{5,4},{6,7},{7,6},{8,9},{9,8},{10,11... | collective-permute-start | bytes 6291464 | tf_op jit(solution)/shard_map/ppermute | solution.py:1091
  97.9 34.5 %all-to-all-start.1 = ((bf16[4,128,1024]{2,1,0:T(8,128)(2,1)}), bf16[4,128,1024]{2,1,0:T(8,128)(2,1)}, u32[]{:S(2)}, u32[]{:S(2)}) async-start(bf16[4,128,1024]{2,1,0:T(8,128)(2,1)} %bitcast.183), calls=%async_computation.1 | async-start | bytes 2097152 | tf_op jit(solution)/shard_map/all_to_all | solution.py:1065
  107.8 44.6 %collective-permute-start.13 = (bf16[256,4096]{1,0:T(8,128)(2,1)}, bf16[256,4096]{1,0:T(8,128)(2,1)}, u32[]{:S(2)}, u32[]{:S(2)}) collective-permute-start(bf16[256,4096]{1,0:T(8,128)(2,1)} %refs_0_.2), channel_id=1, source_target_pairs={{0,8},{1,17},{2,10},{3,19},{4,12},{5,21},{6,14},{7,23},{8,0},{9,25... | collective-permute-start | bytes 6291464 | tf_op jit(solution)/shard_map/ppermute | solution.py:883
  109.4 32.6 %collective-permute-start.9 = (bf16[256,4096]{1,0:T(8,128)(2,1)}, bf16[256,4096]{1,0:T(8,128)(2,1)}, u32[]{:S(2)}, u32[]{:S(2)}) collective-permute-start(bf16[256,4096]{1,0:T(8,128)(2,1)} %collective-permute-done.8.refs_1_.refs_6_.refs_8_.refs_13_.refs_11_.refs_16_.refs_21_), channel_id=1, source_target_pairs={{0,1},{1,0},{2,3},{3,2},{4,5},{5,4},{6,7},{7,6},{8,9},{9,8},{10,11... | collective-permute-start | bytes 6291464 | tf_op jit(solution)/shard_map/ppermute | solution.py:884
  111.5 30.5 %collective-permute-start.11 = (bf16[128,4096]{1,0:T(8,128)(2,1)}, bf16[128,4096]{1,0:T(8,128)(2,1)}, u32[]{:S(2)}, u32[]{:S(2)}) collective-permute-start(bf16[128,4096]{1,0:T(8,128)(2,1)} %collective-permute-done.10.refs_3_.refs_8_.refs_10_.refs_15_.refs_13_.refs_18_.refs_23_), channel_id=1, source_target_pairs={{0,1},{1,0},{2,3},{3,2},{4,5},{5,4},{6,7},{7,6},{8,9},{9,8},{10,11... | collective-permute-start | bytes 3145736 | tf_op jit(solution)/shard_map/ppermute | solution.py:892
  139.5 38.0 %collective-permute-start.17 = (bf16[1024,1024]{1,0:T(8,128)(2,1)}, bf16[1024,1024]{1,0:T(8,128)(2,1)}, u32[]{:S(2)}, u32[]{:S(2)}) collective-permute-start(bf16[1024,1024]{1,0:T(8,128)(2,1)} %refs_5_.1), channel_id=1, source_target_pairs={{0,8},{1,17},{2,10},{3,19},{4,12},{5,21},{6,14},{7,23},{8,0},{9,25... | collective-permute-start | bytes 6291464 | tf_op jit(solution)/shard_map/ppermute | solution.py:883
  154.1 27.5 %collective-permute-start.15 = (bf16[128,4096]{1,0:T(8,128)(2,1)S(1)}, bf16[128,4096]{1,0:T(8,128)(2,1)}, u32[]{:S(2)}, u32[]{:S(2)}) collective-permute-start(bf16[128,4096]{1,0:T(8,128)(2,1)S(1)} %constant_dynamic-slice_fusion.1), channel_id=1, source_target_pairs={{0,16},{1,9},{2,18},{3,11},{4,20},{5,13},{6,22},{7,15},{8,24},{9,1... | collective-permute-start | bytes 3145736 | tf_op jit(solution)/shard_map/ppermute | solution.py:891
  154.7 42.8 %collective-permute-start.14 = (bf16[256,4096]{1,0:T(8,128)(2,1)}, bf16[256,4096]{1,0:T(8,128)(2,1)}, u32[]{:S(2)}, u32[]{:S(2)}) collective-permute-start(bf16[256,4096]{1,0:T(8,128)(2,1)} %collective-permute-done.13.refs_1_), channel_id=1, source_target_pairs={{0,1},{1,0},{2,3},{3,2},{4,5},{5,4},{6,7},{7,6},{8,9},{9,8},{10,11... | collective-permute-start | bytes 6291464 | tf_op jit(solution)/shard_map/ppermute | solution.py:884
  181.7 33.7 %collective-permute-start.18 = (bf16[1024,1024]{1,0:T(8,128)(2,1)}, bf16[1024,1024]{1,0:T(8,128)(2,1)}, u32[]{:S(2)}, u32[]{:S(2)}) collective-permute-start(bf16[1024,1024]{1,0:T(8,128)(2,1)} %collective-permute-done.17.refs_6_), channel_id=1, source_target_pairs={{0,1},{1,0},{2,3},{3,2},{4,5},{5,4},{6,7},{7,6},{8,9},{9,8},{10,11... | collective-permute-start | bytes 6291464 | tf_op jit(solution)/shard_map/ppermute | solution.py:884
  183.5 31.8 %all-to-all-start.2 = ((bf16[4,128,1024]{2,1,0:T(8,128)(2,1)}), bf16[4,128,1024]{2,1,0:T(8,128)(2,1)}, u32[]{:S(2)}, u32[]{:S(2)}) async-start(bf16[4,128,1024]{2,1,0:T(8,128)(2,1)} %bitcast.185), calls=%async_computation.2 | async-start | bytes 2097152 | tf_op jit(solution)/shard_map/all_to_all | solution.py:1065
  187.8 160.6 %reduce-scatter.4.cloned.1.call-start = ((), (), s32[]{:S(2)}) async-start(), calls=%async_computation.6 | async-start | bytes 4718592 | tf_op jit(solution)/shard_map/reduce_scatter | solution.py:978
  236.8 34.5 %collective-permute-start.21 = (bf16[128,1024]{1,0:T(8,128)(2,1)S(1)}, bf16[128,1024]{1,0:T(8,128)(2,1)S(1)}, u32[]{:S(2)}, u32[]{:S(2)}) collective-permute-start(bf16[128,1024]{1,0:T(8,128)(2,1)S(1)} %get-tuple-element.279), channel_id=1, source_target_pairs={{0,2},{1,3},{2,0},{3,1},{4,6},{5,7},{6,4},{7,5},{8,10},{9,11},{10,... | collective-permute-start | bytes 786440 | tf_op jit(solution)/shard_map/ppermute | solution.py:1076
  238.8 32.5 %collective-permute-start.22 = (bf16[128,1024]{1,0:T(8,128)(2,1)S(1)}, bf16[128,1024]{1,0:T(8,128)(2,1)S(1)}, u32[]{:S(2)}, u32[]{:S(2)}) collective-permute-start(bf16[128,1024]{1,0:T(8,128)(2,1)S(1)} %get-tuple-element.278), channel_id=1, source_target_pairs={{0,4},{1,5},{2,6},{3,7},{4,0},{5,1},{6,2},{7,3},{8,12},{9,13},{10,... | collective-permute-start | bytes 786440 | tf_op jit(solution)/shard_map/ppermute | solution.py:1076
  279.3 181.0 %reduce-scatter.6.cloned.1.call-start = ((), (), s32[]{:S(2)}) async-start(), calls=%async_computation.7 | async-start | bytes 5013504 | tf_op jit(solution)/shard_map/reduce_scatter | solution.py:978
  311.2 26.5 %collective-permute-start.24 = (bf16[2,512,1024]{2,1,0:T(8,128)(2,1)S(1)}, bf16[2,512,1024]{2,1,0:T(8,128)(2,1)}, u32[]{:S(2)}, u32[]{:S(2)}) collective-permute-start(bf16[2,512,1024]{2,1,0:T(8,128)(2,1)S(1)} %get-tuple-element.143), channel_id=1, source_target_pairs={{0,1},{1,0},{2,3},{3,2},{4,5},{5,4},{6,7},{7,6},{8,9},{9,8},{10,11... | collective-permute-start | bytes 6291464 | tf_op jit(solution)/shard_map/ppermute | solution.py:1095
  357.9 151.2 %reduce-scatter.8.cloned.1.call-start = ((), (), s32[]{:S(2)}) async-start(), calls=%async_computation.8 | async-start | bytes 1351680 | tf_op jit(solution)/shard_map/reduce_scatter | solution.py:978
  366.5 27.7 %collective-permute-start.26 = (bf16[128,1024]{1,0:T(8,128)(2,1)S(1)}, bf16[128,1024]{1,0:T(8,128)(2,1)S(1)}, u32[]{:S(2)}, u32[]{:S(2)}) collective-permute-start(bf16[128,1024]{1,0:T(8,128)(2,1)S(1)} %get-tuple-element.276), channel_id=1, source_target_pairs={{0,2},{1,3},{2,0},{3,1},{4,6},{5,7},{6,4},{7,5},{8,10},{9,11},{10,... | collective-permute-start | bytes 786440 | tf_op jit(solution)/shard_map/ppermute | solution.py:1076
  373.5 38.0 %collective-permute-start.28 = (bf16[128,1024]{1,0:T(8,128)(2,1)S(1)}, bf16[128,1024]{1,0:T(8,128)(2,1)S(1)}, u32[]{:S(2)}, u32[]{:S(2)}) collective-permute-start(bf16[128,1024]{1,0:T(8,128)(2,1)S(1)} %get-tuple-element.275), channel_id=1, source_target_pairs={{0,4},{1,5},{2,6},{3,7},{4,0},{5,1},{6,2},{7,3},{8,12},{9,13},{10,... | collective-permute-start | bytes 786440 | tf_op jit(solution)/shard_map/ppermute | solution.py:1076
  425.1 47.1 %collective-permute-start.36 = (bf16[128,1024]{1,0:T(8,128)(2,1)}, bf16[128,1024]{1,0:T(8,128)(2,1)S(1)}, u32[]{:S(2)}, u32[]{:S(2)}) collective-permute-start(bf16[128,1024]{1,0:T(8,128)(2,1)} %get-tuple-element.274), channel_id=1, source_target_pairs={{0,6},{1,7},{2,4},{3,5},{4,2},{5,3},{6,0},{7,1},{8,14},{9,15},{10,... | collective-permute-start | bytes 786440 | tf_op jit(solution)/shard_map/ppermute | solution.py:1076
  427.1 26.3 %collective-permute-start.35 = (bf16[2,512,512]{2,1,0:T(8,128)(2,1)S(1)}, bf16[2,512,512]{2,1,0:T(8,128)(2,1)S(1)}, u32[]{:S(2)}, u32[]{:S(2)}) collective-permute-start(bf16[2,512,512]{2,1,0:T(8,128)(2,1)S(1)} %copy-done.27), channel_id=1, source_target_pairs={{0,1},{1,0},{2,3},{3,2},{4,5},{5,4},{6,7},{7,6},{8,9},{9,8},{10,11... | collective-permute-start | bytes 3145736 | tf_op jit(solution)/shard_map/ppermute | solution.py:1095
  (143 other events, 1460.7 us)
Sparse Core Ops, SparseCore 0:
  279.5 52.7 reduce-scatter.3
  358.0 67.3 reduce-scatter.5
  472.3 34.2 reduce-scatter.7

commit v3 on v2

--- a/solution.py
+++ b/solution.py
@@ -65,6 +65,12 @@
     for extent in shape:
         size *= extent
     return size
+
+
+def in_hbm(item):
+    if item.size * item.dtype.itemsize < 256 * 1024:
+        return item
+    return pltpu.with_memory_space_constraint(item, pltpu.HBM)
 
 
 def params(blocks, scratch=0, spare=10):
@@ -170,7 +176,8 @@
     )(queries, key_pos, query_pos, *keys_values, *keys_values)
 
 
-def backward_kernel(pieces, block, causal, *refs):
+def backward_kernel(pieces, block, causal, begun, *refs):
+    refs = refs[: 6 + 2 * pieces] + refs[6 + 2 * pieces + begun :]
     query_ref, out_ref, grad_ref, total_ref, key_pos_ref, query_pos_ref = refs[:6]
     key_refs = refs[6 : 6 + pieces]
     value_refs = refs[6 + pieces : 6 + 2 * pieces]
@@ -229,8 +236,9 @@
 
 
 def attend_backward(
-    queries, keys_values, outputs, grads, totals, key_pos, query_pos, block, causal, first, pairs
+    queries, keys_values, outputs, grads, totals, key_pos, query_pos, block, causal, span, begun=()
 ):
+    first, pairs = span
     rows, width = queries.shape
     pieces = len(keys_values)
     shift = width // PAIR
@@ -238,10 +246,10 @@
     second = pl.BlockSpec((rows, PAIR), lambda p: (0, p + first + shift))
     whole_pos = pl.BlockSpec((pieces, rows, 1), lambda p: (0, 0, 0))
     row_pos = pl.BlockSpec((1, rows), lambda p: (0, 0))
-    both = pl.BlockSpec((2, rows, PAIR), lambda p: (0, 0, p))
-    size = pairs * PAIR
+    both = pl.BlockSpec((2, rows, PAIR), lambda p: (0, 0, p + first))
+    held = 6 + 2 * pieces
     return pl.pallas_call(
-        functools.partial(backward_kernel, pieces, block, causal),
+        functools.partial(backward_kernel, pieces, block, causal, len(begun)),
         grid=(pairs,),
         in_specs=[
             column,
@@ -252,21 +260,23 @@
             row_pos,
         ]
         + [column] * pieces
-        + [second] * pieces,
-        out_specs=[pl.BlockSpec((rows, PAIR), lambda p: (0, p)), both] + [both] * (pieces - 1),
+        + [second] * pieces
+        + [pl.BlockSpec(memory_space=pl.ANY)] * len(begun),
+        out_specs=[column, both] + [both] * (pieces - 1),
         out_shape=[
-            jax.ShapeDtypeStruct((rows, size), BF16),
-            jax.ShapeDtypeStruct((2, rows, size), F32),
+            pltpu.HBM((rows, width), BF16),
+            pltpu.HBM((2, rows, width), F32),
         ]
-        + [jax.ShapeDtypeStruct((2, rows, size), BF16)] * (pieces - 1),
+        + [pltpu.HBM((2, rows, width), BF16)] * (pieces - 1),
+        input_output_aliases={held + index: index for index in range(len(begun))},
         scratch_shapes=[pltpu.VMEM((pieces, rows, PAIR), F32)] * 2,
         compiler_params=params(
             [((rows, PAIR), BF16)] * (6 + 4 * pieces) + [((pieces, rows, 128), F32)] * 2,
             spare=10 + 4 * (pieces > 2),
         ),
-        cost_estimate=cost((24 if causal else 28) * size / width),
+        cost_estimate=cost((24 if causal else 28) * pairs * PAIR / width),
         name="attend_backward",
-    )(queries, outputs, grads, totals, key_pos, query_pos, *keys_values, *keys_values)
+    )(queries, outputs, grads, totals, key_pos, query_pos, *keys_values, *keys_values, *begun)
 
 
 def offset(slot, size):
@@ -335,7 +345,7 @@
         compiler_params=params(blocks, held, spare),
         cost_estimate=cost(micros),
         name=name,
-    )(place, *[item for item, _ in ins])
+    )(place, *[in_hbm(item) for item, _ in ins])
 
 
 def project_kernel(place, left_ref, *refs):
@@ -880,16 +890,22 @@
 
 
 def gather_first(own):
-    one = lax.ppermute(own, ("dp", "seq"), by_core(1, 2))
-    return (own, one, lax.ppermute(one, "seq", swap_pairs(8, 1)))
-
-
-def gather_rest(parts, core, *others):
+    return (own, lax.ppermute(own, ("dp", "seq"), by_core(1, 2)))
+
+
+def gather_swap(parts, *others):
+    return parts + (lax.ppermute(after(parts[1], *others), "seq", swap_pairs(8, 1)),)
+
+
+def gather_near(parts, core, *others):
     one = parts[1]
     half = one.shape[0] // 2
     half_one = lax.dynamic_slice_in_dim(after(one, *others), core * half, half, 0)
-    near = lax.ppermute(half_one, ("dp", "seq"), by_core(2, 1))
-    return parts + (near, lax.ppermute(near, "seq", swap_pairs(8, 1)))
+    return parts + (lax.ppermute(half_one, ("dp", "seq"), by_core(2, 1)),)
+
+
+def gather_far(parts, *others):
+    return parts + (lax.ppermute(after(parts[3], *others), "seq", swap_pairs(8, 1)),)
 
 
 def gather_dp(item):
@@ -1006,10 +1022,11 @@
         from_x = lax.ppermute(take(self.two, 1 - x, 0), "dp", swap_pairs(4, 1))
         one = add(take(self.one, y, 0), from_y)
         two = add(take(self.two, x, 0), from_x)
-        self.item = jnp.concatenate([one, two], axis=1).reshape(2, 2, 32, self.width)
+        self.item = jnp.concatenate([one, two], axis=1)
         return self.item
 
     def z_one(self):
+        self.item = self.item.reshape(2, 2, 32, self.width)
         received = lax.ppermute(take(self.item, 1 - self.low, 1), "seq", swap_pairs(8, 2))
         self.item = add(take(self.item, self.low, 1), received)
         return self.item
@@ -1117,8 +1134,12 @@
         vector_parts = [vectors] + [
             lax.ppermute(vectors, "dp", swap_pairs(4, bit)) for bit in (1, 2, 3)
         ]
-        w_self = gather_rest(gather_first(first_group), core, own_inputs, *vector_parts)
-        w_mid = gather_first(after(second_group, w_self[3]))
+        w_self = gather_swap(gather_first(first_group))
+        w_self = gather_far(
+            gather_near(w_self, core, own_inputs, second_group, *vector_parts)
+        )
+        w_mid = gather_swap(gather_first(after(second_group, w_self[3])))
+        w_in = gather_first(after(feed_in, w_mid[1]))
         at_q, at_kv, at_ckv = (w_self, 0), (w_self, 1), (w_self, 3)
         parts = jnp.stack(vector_parts)
         vectors = jnp.concatenate([take(parts, here ^ slot, 0) for slot in range(4)], axis=1)
@@ -1157,8 +1178,8 @@
     kv_all = spread(kv_own)
     queries = project(place, inputs, *at_q, 1, "self_q")
     if halving:
-        w_mid = gather_rest(w_mid, core, queries)
-        w_in = gather_first(after(feed_in, w_mid[1], queries))
+        w_mid = gather_near(w_mid, core, queries)
+        queries = after(queries, w_mid[1])
     mixed, totals = attend_forward(queries, kv_all, self_keys, self_rows, block, True)
     ckv_own = project(
         place, (after(own_memory, mixed), memory[1]), *at_ckv, 2, "cross_kv"
@@ -1166,19 +1187,22 @@
     ckv_all = spread(ckv_own)
     mixed = after(mixed, ckv_own)
     if halving:
-        w_out = gather_first(after(feed_out, w_mid[1], mixed))
+        w_mid = gather_far(w_mid, mixed)
+        w_out = gather_first(after(feed_out, mixed))
+        mixed = after(mixed, w_in[1])
         at_o, at_cq, at_co = (w_mid, 0), (w_mid, 1), (w_mid, 2)
         at_down, at_up = (w_mid, 6), (w_mid, 7)
     resid_one, first, first_low, cross_q = mix(
         place, mixed, inputs, norm_one, *at_o, *at_cq, "mix_self"
     )
     if halving:
-        w_in = gather_rest(w_in, core, cross_q)
+        w_in = gather_near(gather_swap(w_in, cross_q), core, cross_q)
     cross_mixed, cross_totals = attend_forward(
         cross_q, ckv_all, cross_keys, cross_rows, block, False
     )
     if halving:
-        w_out = gather_rest(w_out, core, cross_mixed)
+        w_in = gather_far(w_in, cross_mixed)
+        w_out = gather_far(gather_near(gather_swap(w_out, cross_mixed), core, cross_mixed))
         out_first, out_second = w_out[:2], w_out[2:]
     resid_two, second, second_low = mix(
         place, cross_mixed, view(first, width, 0), norm_two, *at_co, None, None, "mix_cross"
@@ -1216,7 +1240,7 @@
         *at_co,
     )
 
-    d_two_low = after(d_two_low, output[1], output[2])
+    d_two_low = after(d_two_low, *output[1:])
 
     def whole(item, layer=0):
         return view(item, item.shape[-1], layer)
@@ -1246,15 +1270,24 @@
         cross_rows,
         block,
         False,
-        0,
-        pairs,
-    )
-    d_cq = after(d_cq, output[3])
+        (0, pairs),
+    )
     output = set_down(output, d_cq)
     d_one, d_one_low, d_norm_one, d_mixed = norm_step(
         place, d_cq, d_two, resid_one, norm_one, *at_cq, *at_o
     )
     d_ckv = collect(after(d_ckv[0], d_one_low), d_ckv[1:])
+    grad_source = inputs_back(
+        place,
+        [whole(d_ckv, 0), whole(d_ckv, 1)],
+        at_ckv[0],
+        [at_ckv[1], at_ckv[1] + 1],
+        None,
+        None,
+        "source_back",
+    )
+    d_ckv = after(d_ckv, grad_source)
+    grad_source = send_back(grad_source)
     if halving:
         middle = wgrad(
             place,
@@ -1269,6 +1302,7 @@
         d_one_low = after(d_one_low, middle)
         middle = sum_over(after(middle, early), "seq")
         d_one_low = after(d_one_low, early)
+        early = sum_over(early, "dp")
         inner_sums = Scatter(
             *wgrad(
                 place,
@@ -1280,112 +1314,79 @@
                 "wgrad_inner",
             )
         )
-        d_ckv = after(d_ckv, inner_sums.send)
-    grad_source = inputs_back(
-        place,
-        [whole(d_ckv, 0), whole(d_ckv, 1)],
-        at_ckv[0],
-        [at_ckv[1], at_ckv[1] + 1],
-        None,
-        None,
-        "source_back",
-    )
-    d_mixed = after(d_mixed, grad_source)
     if halving:
         d_mixed = after(d_mixed, inner_sums.core())
-    grad_source = send_back(grad_source)
-
-    def self_backward(grads, first_pair):
-        return attend_backward(
+    else:
+        d_mixed = after(d_mixed, grad_source[0])
+
+    begun = ()
+    split = pairs * 3 // 4
+    for span in ((0, split), (split, pairs - split)):
+        begun = attend_backward(
             queries,
             kv_all,
             mixed,
-            grads,
+            d_mixed,
             totals,
             self_keys,
             self_rows,
             block,
             True,
-            first_pair,
-            pairs // 2,
+            span,
+            begun,
         )
-
-    def self_sums(d_q, d_kv):
-        return Scatter(
+        if halving and span[0] == 0:
+            d_mixed = after(d_mixed, begun[0], inner_sums.plane_one(), *grad_source[1:3])
+    d_q, *d_kv = begun
+    d_kv = collect(d_kv[0], d_kv[1:])
+    if halving:
+        late = Scatter(
             *wgrad(
                 place,
                 [inputs] * 3,
                 [whole(d_q), whole(d_kv, 0), whole(d_kv, 1)],
-                width // 2,
+                width,
                 True,
                 (1.0,) * 3,
                 "wgrad_self",
             )
         )
-
-    d_q_one, *d_kv_one = self_backward(d_mixed, 0)
-    d_mixed = after(d_mixed, d_q_one, grad_source[1])
-    if halving:
-        d_mixed = after(d_mixed, inner_sums.plane_one())
-    d_q_two, *d_kv_two = self_backward(d_mixed, pairs // 2)
-    d_kv_one = collect(after(d_kv_one[0], d_q_two), d_kv_one[1:])
-    if halving:
-        d_q_one = after(d_q_one, d_q_two, grad_source[2], inner_sums.plane_two())
-        late_one = self_sums(d_q_one, d_kv_one)
-        d_kv_two[0] = after(d_kv_two[0], late_one.send)
-    d_kv_two = collect(d_kv_two[0], d_kv_two[1:])
-    if halving:
-        d_q_two = after(d_q_two, late_one.core(), inner_sums.z_one(), middle)
-        late_two = self_sums(d_q_two, d_kv_two)
-        grad_source = set_down(grad_source, late_two.send)
-        d_q_one = after(d_q_one, late_two.send, grad_source)
+        late.keep = after(late.keep, inner_sums.plane_two(), grad_source[3])
+        d_q = after(d_q, late.send, late.core(), middle)
     at_self = at_q if halving else ((jnp.concatenate([at_q[0][0], at_kv[0][0]], axis=1),), 0)
     grad_target = inputs_back(
         place,
-        [
-            whole(d_q_one),
-            whole(d_q_two),
-            whole(d_kv_one, 0),
-            whole(d_kv_two, 0),
-            whole(d_kv_one, 1),
-            whole(d_kv_two, 1),
-        ],
+        [whole(d_q), whole(d_kv, 0), whole(d_kv, 1)],
         at_self[0],
-        [2 * at_self[1] + index for index in range(6)],
+        [at_self[1] + index for index in range(3)],
         "base",
         d_one,
         "target_back",
     )
+    grad_source = set_down(grad_source, grad_target)
     grad_target = send_back(grad_target)
     if not halving:
-        grad_source = set_down(grad_source)
         grad_target = set_down(grad_target)
     if halving:
-        both = sum_over(jnp.concatenate([early, middle], axis=1), "dp").astype(F32)
-        early, middle = both[:, : early.shape[1]], both[:, early.shape[1] :]
+        late.plane_one()
+        late.one, late.two, *_ = lax.optimization_barrier((late.one, late.two, *grad_target))
+        inner_sums.z_one()
+        late.plane_two()
+        inner_sums.z_two()
+        late.z_one()
+        late.z_two()
+        middle = sum_over(middle, "dp").astype(F32)
+        grad_target = set_down(grad_target, late.item)
+        early = early.astype(F32)
         grad_co, grad_down = early[:, :width], early[:, width : width + half]
         lifted = early[:, width + half :]
         folded = lifted.shape[0] // 2
         grad_up = jnp.concatenate([lifted[:folded], lifted[folded:]], axis=1)
         grad_ck, grad_cv = middle[:, :width], middle[:, width : 2 * width]
         norm_sums = middle[:, 2 * width : 2 * width + 6].T
-        late_one.plane_one()
-        late_two.core()
-        late_one.plane_two()
-        late_two.plane_one()
-        inner_sums.z_two()
-        late_two.plane_two()
-        grad_target = set_down(grad_target, late_two.item, both)
-        for late in (late_one, late_two):
-            late.z_one()
-            late.z_two()
         grad_o, grad_cq = inner_sums.item[:, :width], inner_sums.item[:, width:]
         grad_q, grad_k, grad_v = [
-            jnp.concatenate(
-                [late.item[:, index * half : (index + 1) * half] for late in (late_one, late_two)],
-                axis=1,
-            )
-            for index in range(3)
+            late.item[:, index * width : (index + 1) * width] for index in range(3)
         ]
     else:
         norm_sums = jnp.concatenate([d_norm_one, d_norm_two, d_norm_three], axis=0)
@@ -1397,8 +1398,6 @@
         grad_cq = sum_all(dot_tn(first_low, d_cq))
         grad_ck = sum_all(dot_tn(own_memory, d_ckv[0]))
         grad_cv = sum_all(dot_tn(own_memory, d_ckv[1]))
-        d_q = jnp.concatenate([d_q_one, d_q_two], axis=1)
-        d_kv = jnp.concatenate([d_kv_one, d_kv_two], axis=2)
         grad_q = sum_all(dot_tn(own_inputs, d_q))
         grad_k = sum_all(dot_tn(own_inputs, d_kv[0]))
         grad_v = sum_all(dot_tn(own_inputs, d_kv[1]))

time: 548 us -> 527 us (0.962)
  local copies, waits for them, and re-layouts: 81.8 us -> 48 us
  Pallas kernels: 233 us -> 247 us
  waiting for transfers between devices: 110 us -> 121 us
  starting transfers between devices: 73.5 us -> 65.6 us
    unnamed x228 -> x132, local copies, waits for them, and re-layouts: 62.6 us -> 26.6 us
    reduce_scatter x3 -> x4, waiting for transfers between devices: 0.01 us -> 15.3 us  [sum_over(): return lax.psum_scatter(partial, name, scatter_dimension=0, tiled=True)]
    pallas_call x19 -> x18, Pallas kernels: 141 us -> 155 us  [run(): pl.pallas_call(kernel, grid_spec=pltpu.PrefetchScalarGridSpec(num_scalar_...]
    ppermute x3 -> x2, waiting for transfers between devices: 12.9 us -> 0.01 us  [z_two(): lax.ppermute(take(self.item, 1 - self.high, 0), 'seq', swap_pairs(8, 4))]
    ppermute x3 -> x2, waiting for transfers between devices: 2.55 us -> 9.99 us  [plane_one(): from_y = lax.ppermute(take(self.two, 1 - y, 0), 'dp', swap_pairs(4, 2))]
    ppermute x9, waiting for transfers between devices: 23.8 us -> 17.6 us  [send_back(): parts.append(lax.ppermute(take(item, which ^ bit, 0), 'seq', pairs))]
    ppermute x3 -> x2, waiting for transfers between devices: 6.43 us -> 11.4 us  [z_one(): lax.ppermute(take(self.item, 1 - self.low, 1), 'seq', swap_pairs(8, 2))]
  transfers between devices with their start and end apart: 60 -> 53, of which waited for: 19 -> 22; matrix products, arithmetic and copies ran while one was open for 9% -> 9% of each run, Pallas kernels for 39% -> 42%
where the time goes in v3:
time: 527 us; the launch traced here: 518 us
  Pallas kernels  247 us (47%)
  waiting for transfers between devices  121 us (23%)
  starting transfers between devices  65.6 us (12%)
  local copies, waits for them, and re-layouts  48 us (9%)
  other arithmetic  20.2 us (4%)
  between operations  15.4 us (3%)
    pallas_call x18, Pallas kernels, run(): pl.pallas_call(kernel, grid_spec=pltpu.PrefetchScalarGridSpec(num_scalar_...  155 us
    pallas_call x3, Pallas kernels, attend_backward(): pl.pallas_call(functools.partial(backward_kernel, pieces, block, causal,...  51.3 us
    pallas_call x2, Pallas kernels, attend_forward(): pl.pallas_call(functools.partial(forward_kernel, pieces, block, causal),...  41 us
    unnamed x132, local copies, waits for them, and re-layouts  26.6 us
    ppermute x3, waiting for transfers between devices, body(): lax.ppermute(vectors, 'dp', swap_pairs(4, bit))  19.9 us
    ppermute x9, waiting for transfers between devices, send_back(): parts.append(lax.ppermute(take(item, which ^ bit, 0), 'seq', pairs))  17.6 us
    ppermute x9, starting transfers between devices, send_back(): parts.append(lax.ppermute(take(item, which ^ bit, 0), 'seq', pairs))  17.5 us
    ppermute x4, waiting for transfers between devices, gather_near(): return parts + (lax.ppermute(half_one, ('dp', 'seq'), by_core(2, 1)),)  17 us
  transfers between devices with their start and end apart: 53, of which 22 were waited for; matrix products, arithmetic and copies ran while one was open for 9% of the time, Pallas kernels for 42%

profile of v3, /device:TPU:0, one launch (start us, length us, event | category | flops | bytes accessed | tf_op | source)
XLA Modules:
  0.0 517.7 jit_solution(12804621390797105175)
XLA Ops:
  28.5 18.4 %collective-permute-done.2 = bf16[6,256]{1,0:T(8,128)(2,1)S(1)} collective-permute-done((bf16[6,256]{1,0:T(8,128)(2,1)S(1)}, bf16[6,256]{1,0:T(8,128)(2,1)S(1)}, u32[]{:S(2)}, u32[]{:S(2)}) %collective-permute-start.2) | collective-permute-done | bytes 3104 | tf_op jit(solution)/shard_map/ppermute | solution.py:1135
  51.2 16.9 %collective-permute-done.5.refs_3_.refs_5_.refs_6_ = bf16[128,5120]{1,0:T(8,128)(2,1)S(1)} collective-permute-done((bf16[128,5120]{1,0:T(8,128)(2,1)S(1)}, bf16[128,5120]{1,0:T(8,128)(2,1)S(1)}, u32[]{:S(2)}, u32[]{:S(2)}) %collective-permute-start.5) | collective-permute-done | bytes 1310752 | tf_op jit(solution)/shard_map/ppermute | solution.py:904
  99.0 18.4 %attend_forward.2 = (bf16[512,1024]{1,0:T(8,128)(2,1)S(1)}, f32[8,2,512]{2,1,0:T(2,128)S(1)}) custom-call(bf16[512,1024]{1,0:T(8,128)(2,1)S(1)} %self_q.1.refs_0_, s32[2,512,1]{2,1,0:T(8,128)S(1)} %get-tuple-element.275.refs_1_.refs_4_, s32[1,512]{1,0:T(1,128)S(1)} %multiply_add_fusion.refs_2_.refs_5_, ...), custom_call_target="tpu_custom_call" | custom-call | flops 20700000256 | bytes 64800000 | tf_op jit(solution)/shard_map/attend_forward/pallas_call | solution.py:161
  118.3 6.8 %cross_kv.1.refs_3_.refs_5_.refs_6_.refs_8_ = bf16[512,2048]{1,0:T(8,128)(2,1)} custom-call(s32[16]{0:T(128)S(1)} %stack.123.place, bf16[512,1024]{1,0:T(8,128)(2,1)} %bitcast.23.left_ref.refs_0_.refs_1_, bf16[256,5120]{1,0:T(8,128)(2,1)} %constant_dynamic-update-slice_fusion.refs_0_.refs_2_.refs_3_, ...), custom_call_target="tpu_custom_call" | custom-call | flops 5750000128 | bytes 18000000 | tf_op jit(solution)/shard_map/cross_kv/pallas_call | solution.py:332
  126.4 6.8 %collective-permute-done.9.refs_1_ = bf16[256,4096]{1,0:T(8,128)(2,1)} collective-permute-done((bf16[256,4096]{1,0:T(8,128)(2,1)}, bf16[256,4096]{1,0:T(8,128)(2,1)}, u32[]{:S(2)}, u32[]{:S(2)}) %collective-permute-start.9) | collective-permute-done | bytes 2097184 | tf_op jit(solution)/shard_map/ppermute | solution.py:893
  133.2 9.5 %mix_self.1 = (f32[512,1024]{1,0:T(8,128)}, f32[512,1024]{1,0:T(8,128)}, bf16[512,1024]{1,0:T(8,128)(2,1)}, bf16[512,1024]{1,0:T(8,128)(2,1)S(1)}) custom-call(s32[16]{0:T(128)S(1)} %stack.123.place, bf16[512,1024]{1,0:T(8,128)(2,1)} %copy-done.17, bf16[512,1024]{1,0:T(8,128)(2,1)} %bitcast.148, f32[2,1024]{1,0:T(2,128)S(1)} %get-tuple-element.289.norm_ref, ...), custom_call_target="tpu_custom_call" | custom-call | flops 7245000192 | bytes 22680000 | tf_op jit(solution)/shard_map/mix_self/pallas_call | solution.py:332
  145.9 22.7 %attend_forward.3 = (bf16[512,1024]{1,0:T(8,128)(2,1)S(1)}, f32[8,2,512]{2,1,0:T(2,128)S(1)}) custom-call(bf16[512,1024]{1,0:T(8,128)(2,1)S(1)} %get-tuple-element.109.refs_0_, s32[2,512,1]{2,1,0:T(8,128)S(1)} %get-tuple-element.274.refs_1_.refs_4_, s32[1,512]{1,0:T(1,128)S(1)} %broadcast_in_dim.12.refs_2_.refs_5_, ...), custom_call_target="tpu_custom_call" | custom-call | flops 25300000768 | bytes 79200000 | tf_op jit(solution)/shard_map/attend_forward/pallas_call | solution.py:161
  179.5 7.5 %mix_cross.1 = (f32[512,1024]{1,0:T(8,128)}, f32[512,1024]{1,0:T(8,128)}, bf16[512,1024]{1,0:T(8,128)(2,1)}) custom-call(s32[16]{0:T(128)S(1)} %stack.123.place, bf16[512,1024]{1,0:T(8,128)(2,1)} %copy-done.11, f32[512,1024]{1,0:T(8,128)} %get-tuple-element.111.resid_ref, f32[2,1024]{1,0:T(2,128)S(1)} %get-tuple-element.288.norm_ref, ...), custom_call_target="tpu_custom_call" | custom-call | flops 4600000000 | bytes 14400000 | tf_op jit(solution)/shard_map/mix_cross/pallas_call | solution.py:332
  187.1 15.4 %feed_first.1 = (f32[512,1024]{1,0:T(8,128)S(1)}, bf16[512,2048]{1,0:T(8,128)(2,1)}, bf16[512,512]{1,0:T(8,128)(2,1)}, bf16[512,512]{1,0:T(8,128)(2,1)}) custom-call(s32[16]{0:T(128)S(1)} %stack.123.place, bf16[512,1024]{1,0:T(8,128)(2,1)} %get-tuple-element.112.low_ref.refs_2_, f32[512,1024]{1,0:T(8,128)} %get-tuple-element.113.second_ref, ...), custom_call_target="tpu_custom_call" | custom-call | flops 14949999616 | bytes 46800000 | tf_op jit(solution)/shard_map/feed_first/pallas_call | solution.py:332
  205.3 15.0 %feed_second.1 = (bf16[512,1024]{1,0:T(8,128)(2,1)}, f32[512,1024]{1,0:T(8,128)S(1)}, bf16[512,1024]{1,0:T(8,128)(2,1)S(1)}, f32[2,1024]{1,0:T(2,128)}, bf16[512,2048]{1,0:T(8,128)(2,1)}) custom-call(s32[16]{0:T(128)S(1)} %stack.123.place, bf16[512,1024]{1,0:T(8,128)(2,1)} %get-tuple-element.112.low_ref.refs_2_, f32[512,1024]{1,0:T(8,128)} %copy-done.21, ...), custom_call_target="tpu_custom_call" | custom-call | flops 15525000192 | bytes 48600000 | tf_op jit(solution)/shard_map/feed_second/pallas_call | solution.py:332
  227.6 29.5 %feed_backward.1 = (f32[512,1024]{1,0:T(8,128)}, bf16[512,1024]{1,0:T(8,128)(2,1)}, f32[2,1024]{1,0:T(2,128)}, bf16[512,512]{1,0:T(8,128)(2,1)}, bf16[512,1024]{1,0:T(8,128)(2,1)}) custom-call(s32[16]{0:T(128)} %copy-done.7, bf16[512,1024]{1,0:T(8,128)(2,1)} %copy-done.13, f32[512,1024]{1,0:T(8,128)} %copy-done.22, ...), custom_call_target="tpu_custom_call" | custom-call | flops 33350000640 | bytes 104400000 | tf_op jit(solution)/shard_map/feed_backward/pallas_call | solution.py:332
  258.6 7.8 %wgrad_early.1 = bf16[1024,2048]{1,0:T(8,128)(2,1)} custom-call(s32[16]{0:T(128)S(1)} %copy-done.8, bf16[512,1024]{1,0:T(8,128)(2,1)} %copy-done.11, bf16[512,1024]{1,0:T(8,128)(2,1)} %copy-done.11, bf16[512,1024]{1,0:T(8,128)(2,1)} %get-tuple-element.112.low_ref.refs_2_, bf16[512,512]{1,0:T(8,128)(2,1)} %get-tuple-element.127.refs_3_, ...), custom_call_target="tpu_custom_call" | custom-call | flops 3680000000 | bytes 11520000 | tf_op jit(solution)/shard_map/wgrad_early/pallas_call | solution.py:332
  270.1 27.3 %attend_backward.3 = (bf16[512,1024]{1,0:T(8,128)(2,1)}, f32[2,512,1024]{2,1,0:T(8,128)}, bf16[2,512,1024]{2,1,0:T(8,128)(2,1)}) custom-call(bf16[512,1024]{1,0:T(8,128)(2,1)S(1)} %copy-done.20, bf16[512,1024]{1,0:T(8,128)(2,1)S(1)} %copy-done.12, bf16[512,1024]{1,0:T(8,128)(2,1)S(1)} %copy-done.26, f32[8,2,512]{2,1,0:T(2,128)S(1)} %get-tuple-element.132.refs_3_, ...), custom_call_target="tpu_custom_call" | custom-call | flops 32199999488 | bytes 100800000 | tf_op jit(solution)/shard_map/attend_backward/pallas_call | solution.py:251
  297.4 10.0 %norm_step.1 = (f32[512,1024]{1,0:T(8,128)}, bf16[512,1024]{1,0:T(8,128)(2,1)S(1)}, f32[2,1024]{1,0:T(2,128)}, bf16[512,1024]{1,0:T(8,128)(2,1)S(1)}) custom-call(s32[16]{0:T(128)S(1)} %copy-done.8, bf16[512,1024]{1,0:T(8,128)(2,1)} %get-tuple-element.133.dquery_ref.refs_3_, f32[512,1024]{1,0:T(8,128)} %get-tuple-element.138.d_ref, ...), custom_call_target="tpu_custom_call" | custom-call | flops 7590000128 | bytes 23760000 | tf_op jit(solution)/shard_map/norm_step/pallas_call | solution.py:332
  309.6 6.2 %source_back.1 = bf16[512,1024]{1,0:T(8,128)(2,1)S(1)} custom-call(s32[16]{0:T(128)S(1)} %copy-done.8, bf16[2,512,1024]{2,1,0:T(8,128)(2,1)} %add_convert_fusion.3.refs_0_.refs_1_.refs_2_.refs_3_, bf16[2,512,1024]{2,1,0:T(8,128)(2,1)} %add_convert_fusion.3.refs_0_.refs_1_.refs_2_.refs_3_, ...), custom_call_target="tpu_custom_call" | custom-call | flops 6899999744 | bytes 21600000 | tf_op jit(solution)/shard_map/source_back/pallas_call | solution.py:332
  315.8 7.0 %wgrad_memory.1 = bf16[1024,2176]{1,0:T(8,128)(2,1)} custom-call(s32[16]{0:T(128)S(1)} %copy-done.8, bf16[512,1024]{1,0:T(8,128)(2,1)} %bitcast.23.left_ref.refs_0_.refs_1_, bf16[512,1024]{1,0:T(8,128)(2,1)} %bitcast.23.left_ref.refs_0_.refs_1_, bf16[2,512,1024]{2,1,0:T(8,128)(2,1)} %add_convert_fusion.3.refs_0_.refs_1_.refs_2_.refs_3_, ...), custom_call_target="tpu_custom_call" | custom-call | flops 3680000000 | bytes 11520000 | tf_op jit(solution)/shard_map/wgrad_memory/pallas_call | solution.py:332
  322.8 6.9 %wgrad_inner.1 = (bf16[512,2048]{1,0:T(8,128)(2,1)}, bf16[512,2048]{1,0:T(8,128)(2,1)}) custom-call(s32[16]{0:T(128)S(1)} %copy-done.8, bf16[512,1024]{1,0:T(8,128)(2,1)} %copy-done.17, bf16[512,1024]{1,0:T(8,128)(2,1)} %get-tuple-element.141.refs_1_, bf16[512,1024]{1,0:T(8,128)(2,1)} %copy-done.16, bf16[512,1024]{1,0:T(8,128)(2,1)} %get-tuple-element.133.dquery_ref.refs_3_), custom_call_target="tpu_custom_call" | custom-call | flops 3680000000 | bytes 11520000 | tf_op jit(solution)/shard_map/wgrad_inner/pallas_call | solution.py:332
  339.4 17.3 %attend_backward.4 = (bf16[512,1024]{1,0:T(8,128)(2,1)}, f32[2,512,1024]{2,1,0:T(8,128)}, bf16[2,512,1024]{2,1,0:T(8,128)(2,1)}) custom-call(bf16[512,1024]{1,0:T(8,128)(2,1)S(1)} %copy-done.1, bf16[512,1024]{1,0:T(8,128)(2,1)S(1)} %copy-done.18, bf16[512,1024]{1,0:T(8,128)(2,1)S(1)} %copy-done.15, f32[8,2,512]{2,1,0:T(2,128)S(1)} %get-tuple-element.155.refs_3_, ...), custom_call_target="tpu_custom_call" | custom-call | flops 20700000256 | bytes 64800000 | tf_op jit(solution)/shard_map/attend_backward/pallas_call | solution.py:251
  357.7 6.7 %attend_backward.5 = (bf16[512,1024]{1,0:T(8,128)(2,1)}, f32[2,512,1024]{2,1,0:T(8,128)}, bf16[2,512,1024]{2,1,0:T(8,128)(2,1)}) custom-call(bf16[512,1024]{1,0:T(8,128)(2,1)S(1)} %copy-done.1, bf16[512,1024]{1,0:T(8,128)(2,1)S(1)} %copy-done.18, bf16[512,1024]{1,0:T(8,128)(2,1)S(1)} %copy-done.15, ...), custom_call_target="tpu_custom_call", output_to_operand_aliasing={{0}: (10, {}), {1}: (11, {}), {2}: (12, {})} | custom-call | flops 6899999744 | bytes 21600000 | tf_op jit(solution)/shard_map/attend_backward/pallas_call | solution.py:251
  373.3 9.3 %wgrad_self.1 = (bf16[512,3072]{1,0:T(8,128)(2,1)}, bf16[512,3072]{1,0:T(8,128)(2,1)}) custom-call(s32[16]{0:T(128)S(1)} %copy-done.8, bf16[512,1024]{1,0:T(8,128)(2,1)} %bitcast.149, bf16[512,1024]{1,0:T(8,128)(2,1)} %bitcast.150, bf16[512,1024]{1,0:T(8,128)(2,1)} %bitcast.151, bf16[512,1024]{1,0:T(8,128)(2,1)} %get-tuple-element.167.refs_3_.refs_0_, ...), custom_call_target="tpu_custom_call" | custom-call | flops 5520000000 | bytes 17280000 | tf_op jit(solution)/shard_map/wgrad_self/pallas_call | solution.py:332
  411.5 8.1 %collective-permute-done.44 = bf16[2,32,2048]{2,1,0:T(8,128)(2,1)S(1)} collective-permute-done((bf16[2,32,2048]{2,1,0:T(8,128)(2,1)S(1)}, bf16[2,32,2048]{2,1,0:T(8,128)(2,1)S(1)}, u32[]{:S(2)}, u32[]{:S(2)}) %collective-permute-start.44) | collective-permute-done | bytes 262176 | tf_op jit(solution)/shard_map/ppermute | solution.py:1030
  428.9 8.9 %target_back.1 = bf16[512,1024]{1,0:T(8,128)(2,1)S(1)} custom-call(s32[16]{0:T(128)S(1)} %copy-done.8, bf16[512,1024]{1,0:T(8,128)(2,1)} %get-tuple-element.167.refs_3_.refs_0_, bf16[2,512,1024]{2,1,0:T(8,128)(2,1)} %add_convert_fusion.1.refs_4_.refs_5_.refs_1_.refs_2_, bf16[2,512,1024]{2,1,0:T(8,128)(2,1)} %add_convert_fusion.1.refs_4_.refs_5_.refs_1_.refs_2_, ...), custom_call_target="tpu_custom_call" | custom-call | flops 10350000128 | bytes 32400000 | tf_op jit(solution)/shard_map/target_back/pallas_call | solution.py:332
  452.7 12.4 %collective-permute-done.36.refs_1_ = bf16[128,1024]{1,0:T(8,128)(2,1)S(1)} collective-permute-done((bf16[128,1024]{1,0:T(8,128)(2,1)S(1)}, bf16[128,1024]{1,0:T(8,128)(2,1)S(1)}, u32[]{:S(2)}, u32[]{:S(2)}) %collective-permute-start.36) | collective-permute-done | bytes 262176 | tf_op jit(solution)/shard_map/ppermute | solution.py:1093
  488.6 14.4 %reduce-scatter.9.cloned.1.call-done = bf16[32,2176]{1,0:T(8,128)(2,1)} async-done(((bf16[128,2176]{1,0:T(8,128)(2,1)}), bf16[32,2176]{1,0:T(8,128)(2,1)}) %reduce-scatter.9.cloned.1.call-update) | async-done | bytes 139280 | tf_op jit(solution)/shard_map/reduce_scatter | solution.py:994
  (313 shorter events, 193.2 us)
Async XLA Ops:
  13.9 34.8 %collective-permute-start = (bf16[256,5120]{1,0:T(8,128)(2,1)}, bf16[256,5120]{1,0:T(8,128)(2,1)}, u32[]{:S(2)}, u32[]{:S(2)}) collective-permute-start(bf16[256,5120]{1,0:T(8,128)(2,1)} %constant_dynamic-update-slice_fusion.refs_0_.refs_2_.refs_3_), channel_id=1, source_target_pairs={{0,8},{1,17},{2,10},{3,19},{4,12},{5,21},{6,14},{7,23},{8,0},{9,25... | collective-permute-start | bytes 7864328 | tf_op jit(solution)/shard_map/ppermute | solution.py:893
  18.2 30.5 %all-to-all-start = ((bf16[4,128,1024]{2,1,0:T(8,128)(2,1)}), bf16[4,128,1024]{2,1,0:T(8,128)(2,1)S(1)}, u32[]{:S(2)}, u32[]{:S(2)}) async-start(bf16[4,128,1024]{2,1,0:T(8,128)(2,1)} %bitcast.136), calls=%async_computation | async-start | bytes 2097152 | tf_op jit(solution)/shard_map/all_to_all | solution.py:1082
  23.3 23.6 %collective-permute-start.2 = (bf16[6,256]{1,0:T(8,128)(2,1)S(1)}, bf16[6,256]{1,0:T(8,128)(2,1)S(1)}, u32[]{:S(2)}, u32[]{:S(2)}) collective-permute-start(bf16[6,256]{1,0:T(8,128)(2,1)S(1)} %stack.130), channel_id=1, source_target_pairs={{0,8},{8,0},{16,24},{24,16},{1,9},{9,1},{17,25},{25,17},{2,10},{10... | collective-permute-start | bytes 9224 | tf_op jit(solution)/shard_map/ppermute | solution.py:1135
  68.2 26.4 %collective-permute-start.7 = (bf16[256,4096]{1,0:T(8,128)(2,1)}, bf16[256,4096]{1,0:T(8,128)(2,1)}, u32[]{:S(2)}, u32[]{:S(2)}) collective-permute-start(bf16[256,4096]{1,0:T(8,128)(2,1)} %copy-done.44), channel_id=1, source_target_pairs={{0,8},{1,17},{2,10},{3,19},{4,12},{5,21},{6,14},{7,23},{8,0},{9,25... | collective-permute-start | bytes 6291464 | tf_op jit(solution)/shard_map/ppermute | solution.py:893
  78.7 39.6 %all-to-all-start.1 = ((bf16[4,128,1024]{2,1,0:T(8,128)(2,1)}), bf16[4,128,1024]{2,1,0:T(8,128)(2,1)}, u32[]{:S(2)}, u32[]{:S(2)}) async-start(bf16[4,128,1024]{2,1,0:T(8,128)(2,1)} %bitcast.135), calls=%async_computation.1 | async-start | bytes 2097152 | tf_op jit(solution)/shard_map/all_to_all | solution.py:1082
  96.9 28.2 %collective-permute-start.11 = (bf16[128,4096]{1,0:T(8,128)(2,1)}, bf16[128,4096]{1,0:T(8,128)(2,1)}, u32[]{:S(2)}, u32[]{:S(2)}) collective-permute-start(bf16[128,4096]{1,0:T(8,128)(2,1)} %constant_dynamic-slice_fusion.2), channel_id=1, source_target_pairs={{0,16},{1,9},{2,18},{3,11},{4,20},{5,13},{6,22},{7,15},{8,24},{9,1... | collective-permute-start | bytes 3145736 | tf_op jit(solution)/shard_map/ppermute | solution.py:904
  97.4 35.8 %collective-permute-start.9 = (bf16[256,4096]{1,0:T(8,128)(2,1)}, bf16[256,4096]{1,0:T(8,128)(2,1)}, u32[]{:S(2)}, u32[]{:S(2)}) collective-permute-start(bf16[256,4096]{1,0:T(8,128)(2,1)} %refs_0_.2), channel_id=1, source_target_pairs={{0,8},{1,17},{2,10},{3,19},{4,12},{5,21},{6,14},{7,23},{8,0},{9,25... | collective-permute-start | bytes 6291464 | tf_op jit(solution)/shard_map/ppermute | solution.py:893
  98.9 34.3 %collective-permute-start.10 = (bf16[256,4096]{1,0:T(8,128)(2,1)}, bf16[256,4096]{1,0:T(8,128)(2,1)}, u32[]{:S(2)}, u32[]{:S(2)}) collective-permute-start(bf16[256,4096]{1,0:T(8,128)(2,1)} %collective-permute-done.7.refs_1_.refs_6_.refs_8_.refs_13_.refs_11_.refs_16_.refs_21_), channel_id=1, source_target_pairs={{0,1},{1,0},{2,3},{3,2},{4,5},{5,4},{6,7},{7,6},{8,9},{9,8},{10,11... | collective-permute-start | bytes 6291464 | tf_op jit(solution)/shard_map/ppermute | solution.py:897
  125.7 42.9 %collective-permute-start.17 = (bf16[1024,1024]{1,0:T(8,128)(2,1)}, bf16[1024,1024]{1,0:T(8,128)(2,1)}, u32[]{:S(2)}, u32[]{:S(2)}) collective-permute-start(bf16[1024,1024]{1,0:T(8,128)(2,1)} %refs_5_.1), channel_id=1, source_target_pairs={{0,8},{1,17},{2,10},{3,19},{4,12},{5,21},{6,14},{7,23},{8,0},{9,25... | collective-permute-start | bytes 6291464 | tf_op jit(solution)/shard_map/ppermute | solution.py:893
  142.7 44.4 %collective-permute-start.14 = (bf16[256,4096]{1,0:T(8,128)(2,1)}, bf16[256,4096]{1,0:T(8,128)(2,1)}, u32[]{:S(2)}, u32[]{:S(2)}) collective-permute-start(bf16[256,4096]{1,0:T(8,128)(2,1)} %collective-permute-done.9.refs_1_), channel_id=1, source_target_pairs={{0,1},{1,0},{2,3},{3,2},{4,5},{5,4},{6,7},{7,6},{8,9},{9,8},{10,11... | collective-permute-start | bytes 6291464 | tf_op jit(solution)/shard_map/ppermute | solution.py:897
  145.3 27.5 %collective-permute-start.15 = (bf16[128,4096]{1,0:T(8,128)(2,1)S(1)}, bf16[128,4096]{1,0:T(8,128)(2,1)}, u32[]{:S(2)}, u32[]{:S(2)}) collective-permute-start(bf16[128,4096]{1,0:T(8,128)(2,1)S(1)} %constant_dynamic-slice_fusion.1), channel_id=1, source_target_pairs={{0,16},{1,9},{2,18},{3,11},{4,20},{5,13},{6,22},{7,15},{8,24},{9,1... | collective-permute-start | bytes 3145736 | tf_op jit(solution)/shard_map/ppermute | solution.py:904
  172.8 32.5 %collective-permute-start.18 = (bf16[1024,1024]{1,0:T(8,128)(2,1)}, bf16[1024,1024]{1,0:T(8,128)(2,1)}, u32[]{:S(2)}, u32[]{:S(2)}) collective-permute-start(bf16[1024,1024]{1,0:T(8,128)(2,1)} %collective-permute-done.17.refs_6_), channel_id=1, source_target_pairs={{0,1},{1,0},{2,3},{3,2},{4,5},{5,4},{6,7},{7,6},{8,9},{9,8},{10,11... | collective-permute-start | bytes 6291464 | tf_op jit(solution)/shard_map/ppermute | solution.py:897
  174.7 30.6 %all-to-all-start.2 = ((bf16[4,128,1024]{2,1,0:T(8,128)(2,1)}), bf16[4,128,1024]{2,1,0:T(8,128)(2,1)}, u32[]{:S(2)}, u32[]{:S(2)}) async-start(bf16[4,128,1024]{2,1,0:T(8,128)(2,1)} %bitcast.152), calls=%async_computation.2 | async-start | bytes 2097152 | tf_op jit(solution)/shard_map/all_to_all | solution.py:1082
  179.3 143.5 %reduce-scatter.5.cloned.1.call-start = ((), (), s32[]{:S(2)}) async-start(), calls=%async_computation.7 | async-start | bytes 4718592 | tf_op jit(solution)/shard_map/reduce_scatter | solution.py:994
  223.2 34.0 %collective-permute-start.21 = (bf16[128,1024]{1,0:T(8,128)(2,1)S(1)}, bf16[128,1024]{1,0:T(8,128)(2,1)S(1)}, u32[]{:S(2)}, u32[]{:S(2)}) collective-permute-start(bf16[128,1024]{1,0:T(8,128)(2,1)S(1)} %get-tuple-element.273), channel_id=1, source_target_pairs={{0,2},{1,3},{2,0},{3,1},{4,6},{5,7},{6,4},{7,5},{8,10},{9,11},{10,... | collective-permute-start | bytes 786440 | tf_op jit(solution)/shard_map/ppermute | solution.py:1093
  223.8 33.4 %collective-permute-start.22 = (bf16[128,1024]{1,0:T(8,128)(2,1)S(1)}, bf16[128,1024]{1,0:T(8,128)(2,1)S(1)}, u32[]{:S(2)}, u32[]{:S(2)}) collective-permute-start(bf16[128,1024]{1,0:T(8,128)(2,1)S(1)} %get-tuple-element.272), channel_id=1, source_target_pairs={{0,4},{1,5},{2,6},{3,7},{4,0},{5,1},{6,2},{7,3},{8,12},{9,13},{10,... | collective-permute-start | bytes 786440 | tf_op jit(solution)/shard_map/ppermute | solution.py:1093
  226.2 31.1 %collective-permute-start.23 = (bf16[128,1024]{1,0:T(8,128)(2,1)S(1)}, bf16[128,1024]{1,0:T(8,128)(2,1)S(1)}, u32[]{:S(2)}, u32[]{:S(2)}) collective-permute-start(bf16[128,1024]{1,0:T(8,128)(2,1)S(1)} %get-tuple-element.271), channel_id=1, source_target_pairs={{0,6},{1,7},{2,4},{3,5},{4,2},{5,3},{6,0},{7,1},{8,14},{9,15},{10,... | collective-permute-start | bytes 786440 | tf_op jit(solution)/shard_map/ppermute | solution.py:1093
  266.4 123.8 %reduce-scatter.11.cloned.1.call-start = ((), (), s32[]{:S(2)}) async-start(), calls=%async_computation.10 | async-start | bytes 655360 | tf_op jit(solution)/shard_map/reduce_scatter | solution.py:994
  331.0 26.6 %collective-permute-start.27 = (bf16[128,1024]{1,0:T(8,128)(2,1)}, bf16[128,1024]{1,0:T(8,128)(2,1)}, u32[]{:S(2)}, u32[]{:S(2)}) collective-permute-start(bf16[128,1024]{1,0:T(8,128)(2,1)} %get-tuple-element.270), channel_id=1, source_target_pairs={{0,2},{1,3},{2,0},{3,1},{4,6},{5,7},{6,4},{7,5},{8,10},{9,11},{10,... | collective-permute-start | bytes 786440 | tf_op jit(solution)/shard_map/ppermute | solution.py:1093
  331.1 26.6 %collective-permute-start.28 = (bf16[128,1024]{1,0:T(8,128)(2,1)}, bf16[128,1024]{1,0:T(8,128)(2,1)}, u32[]{:S(2)}, u32[]{:S(2)}) collective-permute-start(bf16[128,1024]{1,0:T(8,128)(2,1)} %get-tuple-element.269), channel_id=1, source_target_pairs={{0,4},{1,5},{2,6},{3,7},{4,0},{5,1},{6,2},{7,3},{8,12},{9,13},{10,... | collective-permute-start | bytes 786440 | tf_op jit(solution)/shard_map/ppermute | solution.py:1093
  333.9 95.0 %reduce-scatter.7.cloned.1.call-start = ((), (), s32[]{:S(2)}) async-start(), calls=%async_computation.8 | async-start | bytes 5013504 | tf_op jit(solution)/shard_map/reduce_scatter | solution.py:994
  364.8 138.2 %reduce-scatter.9.cloned.1.call-start = ((), (), s32[]{:S(2)}) async-start(), calls=%async_computation.9 | async-start | bytes 696320 | tf_op jit(solution)/shard_map/reduce_scatter | solution.py:994
  382.5 24.6 %collective-permute-start.34 = (bf16[512,3072]{1,0:T(8,128)(2,1)}, bf16[512,3072]{1,0:T(8,128)(2,1)}, u32[]{:S(2)}, u32[]{:S(2)}) collective-permute-start(bf16[512,3072]{1,0:T(8,128)(2,1)} %get-tuple-element.163), channel_id=1, source_target_pairs={{0,1},{1,0},{2,3},{3,2},{4,5},{5,4},{6,7},{7,6},{8,9},{9,8},{10,11... | collective-permute-start | bytes 9437192 | tf_op jit(solution)/shard_map/ppermute | solution.py:1006
  419.6 46.8 %collective-permute-start.45 = (bf16[32,2048]{1,0:T(8,128)(2,1)S(1)}, bf16[32,2048]{1,0:T(8,128)(2,1)S(1)}, u32[]{:S(2)}, u32[]{:S(2)}) collective-permute-start(bf16[32,2048]{1,0:T(8,128)(2,1)S(1)} %dynamic-slice_bitcast_fusion.20), channel_id=1, source_target_pairs={{0,4},{1,5},{2,6},{3,7},{4,0},{5,1},{6,2},{7,3},{8,12},{9,13},{10,... | collective-permute-start | bytes 393224 | tf_op jit(solution)/shard_map/ppermute | solution.py:1035
  (88 other events, 1056.2 us)
Sparse Core Ops, SparseCore 0:
  266.5 48.1 reduce-scatter.4
  334.0 23.5 reduce-scatter.10
  364.9 63.9 reduce-scatter.6
  479.8 23.1 reduce-scatter.8

commit v4 on v3

--- a/solution.py
+++ b/solution.py
@@ -929,9 +929,13 @@
             rows = jnp.concatenate([ref[...] for ref in refs[2 * count : 2 * count + extra]])
             filler = jnp.zeros((128 - rows.shape[0], rows.shape[1]), F32)
             columns = jnp.concatenate([rows, filler], axis=0).T.astype(BF16)
-            for index, item in enumerate(row_blocks(columns, 32)):
-                at = (index % 8 * 4 + index // 8) * 32
-                outs[0][at : at + 32, :128] = item
+            blocks = row_blocks(columns, 32)
+            even = jnp.concatenate(blocks[0::2], axis=0)
+            odd = jnp.concatenate(blocks[1::2], axis=0)
+            outs[0][:, :128] = jnp.where(place[4] == 0, odd, even)
+            outs[1][:, :128] = jnp.where(place[4] == 0, even, odd)
+            for out in outs:
+                out[:, 128:256] = jnp.zeros(even.shape, BF16)
 
     for which in range(count):
 
@@ -976,7 +980,7 @@
         place,
         (len(lefts) + more,),
         list(lefts) + list(rights) + [(item, fixed(item.shape)) for item in extra],
-        [((high, wide * len(lefts) + 128 * more), BF16, spec, True)] * (2 if split else 1),
+        [((high, wide * len(lefts) + 256 * more), BF16, spec, True)] * (2 if split else 1),
         1.6 * len(lefts) * wide / 1024,
         scratch=[pltpu.VMEM((tall, rows), BF16)],
     )
@@ -1289,29 +1293,18 @@
     d_ckv = after(d_ckv, grad_source)
     grad_source = send_back(grad_source)
     if halving:
-        middle = wgrad(
-            place,
-            [memory, memory],
-            [whole(d_ckv, 0), whole(d_ckv, 1)],
-            width,
-            False,
-            (1.0,) * 2,
-            "wgrad_memory",
-            [d_norm_one, d_norm_two, d_norm_three],
-        )[0]
-        d_one_low = after(d_one_low, middle)
-        middle = sum_over(after(middle, early), "seq")
         d_one_low = after(d_one_low, early)
-        early = sum_over(early, "dp")
+        early = sum_over(early, "dp").astype(F32)
         inner_sums = Scatter(
             *wgrad(
                 place,
-                [whole(mixed), whole(first_low)],
-                [whole(d_one_low), whole(d_cq)],
+                [memory, memory, whole(mixed), whole(first_low)],
+                [whole(d_ckv, 0), whole(d_ckv, 1), whole(d_one_low), whole(d_cq)],
                 width,
                 True,
-                (1.0,) * 2,
+                (1.0,) * 4,
                 "wgrad_inner",
+                [d_norm_one, d_norm_two, d_norm_three],
             )
         )
     if halving:
@@ -1339,7 +1332,23 @@
             d_mixed = after(d_mixed, begun[0], inner_sums.plane_one(), *grad_source[1:3])
     d_q, *d_kv = begun
     d_kv = collect(d_kv[0], d_kv[1:])
+    at_self = at_q if halving else ((jnp.concatenate([at_q[0][0], at_kv[0][0]], axis=1),), 0)
+    grad_target = inputs_back(
+        place,
+        [whole(d_q), whole(d_kv, 0), whole(d_kv, 1)],
+        at_self[0],
+        [at_self[1] + index for index in range(3)],
+        "base",
+        d_one,
+        "target_back",
+    )
+    d_q = after(d_q, grad_target)
+    grad_target = send_back(grad_target)
+    if not halving:
+        grad_source = set_down(grad_source)
+        grad_target = set_down(grad_target)
     if halving:
+        d_q = after(d_q, inner_sums.plane_two())
         late = Scatter(
             *wgrad(
                 place,
@@ -1351,40 +1360,26 @@
                 "wgrad_self",
             )
         )
-        late.keep = after(late.keep, inner_sums.plane_two(), grad_source[3])
-        d_q = after(d_q, late.send, late.core(), middle)
-    at_self = at_q if halving else ((jnp.concatenate([at_q[0][0], at_kv[0][0]], axis=1),), 0)
-    grad_target = inputs_back(
-        place,
-        [whole(d_q), whole(d_kv, 0), whole(d_kv, 1)],
-        at_self[0],
-        [at_self[1] + index for index in range(3)],
-        "base",
-        d_one,
-        "target_back",
-    )
-    grad_source = set_down(grad_source, grad_target)
-    grad_target = send_back(grad_target)
-    if not halving:
-        grad_target = set_down(grad_target)
-    if halving:
+        grad_source = set_down(grad_source, late.send)
+        late.keep = after(late.keep, inner_sums.z_one(), grad_source, grad_target[1])
+        late.core()
         late.plane_one()
-        late.one, late.two, *_ = lax.optimization_barrier((late.one, late.two, *grad_target))
-        inner_sums.z_one()
+        late.one, late.two, *_ = lax.optimization_barrier(
+            (late.one, late.two, inner_sums.z_two(), *grad_target)
+        )
+        grad_target = set_down(grad_target, late.one)
         late.plane_two()
-        inner_sums.z_two()
+        late.item = after(late.item, grad_target)
         late.z_one()
         late.z_two()
-        middle = sum_over(middle, "dp").astype(F32)
-        grad_target = set_down(grad_target, late.item)
-        early = early.astype(F32)
         grad_co, grad_down = early[:, :width], early[:, width : width + half]
         lifted = early[:, width + half :]
         folded = lifted.shape[0] // 2
         grad_up = jnp.concatenate([lifted[:folded], lifted[folded:]], axis=1)
-        grad_ck, grad_cv = middle[:, :width], middle[:, width : 2 * width]
-        norm_sums = middle[:, 2 * width : 2 * width + 6].T
-        grad_o, grad_cq = inner_sums.item[:, :width], inner_sums.item[:, width:]
+        norm_sums = inner_sums.item[:, 4 * width : 4 * width + 6].T
+        grad_ck, grad_cv, grad_o, grad_cq = [
+            inner_sums.item[:, index * width : (index + 1) * width] for index in range(4)
+        ]
         grad_q, grad_k, grad_v = [
             late.item[:, index * width : (index + 1) * width] for index in range(3)
         ]

time: 527 us -> 522 us (level)
  starting transfers between devices: 65.6 us -> 73.1 us
    ppermute x9, waiting for transfers between devices: 17.6 us -> 0.32 us  [send_back(): parts.append(lax.ppermute(take(item, which ^ bit, 0), 'seq', pairs))]
    reduce_scatter x4 -> x2, waiting for transfers between devices: 15.3 us -> 0.02 us  [sum_over(): return lax.psum_scatter(partial, name, scatter_dimension=0, tiled=True)]
    ppermute x2, waiting for transfers between devices: 0.01 us -> 10.1 us  [plane_one(): from_x = lax.ppermute(take(self.one, 1 - x, 1), 'dp', swap_pairs(4, 1))]
    ppermute x2, starting transfers between devices: 4.52 us -> 11.6 us  [z_two(): lax.ppermute(take(self.item, 1 - self.high, 0), 'seq', swap_pairs(8, 4))]
    ppermute x2, waiting for transfers between devices: 6.62 us -> 12.2 us  [plane_two(): from_y = lax.ppermute(take(self.one, 1 - y, 0), 'dp', swap_pairs(4, 2))]
    ppermute x2, waiting for transfers between devices: 0.01 us -> 5.54 us  [z_two(): lax.ppermute(take(self.item, 1 - self.high, 0), 'seq', swap_pairs(8, 4))]
    pallas_call x18 -> x17, Pallas kernels: 155 us -> 152 us  [run(): pl.pallas_call(kernel, grid_spec=pltpu.PrefetchScalarGridSpec(num_scalar_...]
    unnamed x132 -> x136, local copies, waits for them, and re-layouts: 26.6 us -> 25.3 us
  transfers between devices with their start and end apart: 53 -> 51, of which waited for: 22 -> 20; matrix products, arithmetic and copies ran while one was open for 9% -> 8% of each run, Pallas kernels for 42% -> 41%
where the time goes in v4:
time: 522 us; the launch traced here: 512 us
  Pallas kernels  244 us (47%)
  waiting for transfers between devices  118 us (23%)
  starting transfers between devices  73.1 us (14%)
  local copies, waits for them, and re-layouts  44 us (8%)
  other arithmetic  17.3 us (3%)
  between operations  15.7 us (3%)
    pallas_call x17, Pallas kernels, run(): pl.pallas_call(kernel, grid_spec=pltpu.PrefetchScalarGridSpec(num_scalar_...  152 us
    pallas_call x3, Pallas kernels, attend_backward(): pl.pallas_call(functools.partial(backward_kernel, pieces, block, causal,...  51.7 us
    pallas_call x2, Pallas kernels, attend_forward(): pl.pallas_call(functools.partial(forward_kernel, pieces, block, causal),...  41.1 us
    unnamed x136, local copies, waits for them, and re-layouts  25.3 us
    ppermute x3, waiting for transfers between devices, body(): lax.ppermute(vectors, 'dp', swap_pairs(4, bit))  19.9 us
    ppermute x4, waiting for transfers between devices, gather_near(): return parts + (lax.ppermute(half_one, ('dp', 'seq'), by_core(2, 1)),)  17 us
    ppermute x9, starting transfers between devices, send_back(): parts.append(lax.ppermute(take(item, which ^ bit, 0), 'seq', pairs))  15.2 us
    all_to_all x3, starting transfers between devices, to_sequence(): lax.all_to_all(item.swapaxes(0, 1), 'seq', 0, 0, axis_index_groups=apart,...  14.2 us
  transfers between devices with their start and end apart: 51, of which 20 were waited for; matrix products, arithmetic and copies ran while one was open for 8% of the time, Pallas kernels for 41%

profile of v4, /device:TPU:0, one launch (start us, length us, event | category | flops | bytes accessed | tf_op | source)
XLA Modules:
  0.0 512.3 jit_solution(3193089188545906491)
XLA Ops:
  28.4 18.5 %collective-permute-done.2 = bf16[6,256]{1,0:T(8,128)(2,1)S(1)} collective-permute-done((bf16[6,256]{1,0:T(8,128)(2,1)S(1)}, bf16[6,256]{1,0:T(8,128)(2,1)S(1)}, u32[]{:S(2)}, u32[]{:S(2)}) %collective-permute-start.2) | collective-permute-done | bytes 3104 | tf_op jit(solution)/shard_map/ppermute | solution.py:1139
  51.2 16.9 %collective-permute-done.5.refs_3_.refs_5_.refs_6_ = bf16[128,5120]{1,0:T(8,128)(2,1)S(1)} collective-permute-done((bf16[128,5120]{1,0:T(8,128)(2,1)S(1)}, bf16[128,5120]{1,0:T(8,128)(2,1)S(1)}, u32[]{:S(2)}, u32[]{:S(2)}) %collective-permute-start.5) | collective-permute-done | bytes 1310752 | tf_op jit(solution)/shard_map/ppermute | solution.py:904
  99.0 18.4 %attend_forward.2 = (bf16[512,1024]{1,0:T(8,128)(2,1)S(1)}, f32[8,2,512]{2,1,0:T(2,128)S(1)}) custom-call(bf16[512,1024]{1,0:T(8,128)(2,1)S(1)} %self_q.1.refs_0_, s32[2,512,1]{2,1,0:T(8,128)S(1)} %get-tuple-element.279.refs_1_.refs_4_, s32[1,512]{1,0:T(1,128)S(1)} %multiply_add_fusion.refs_2_.refs_5_, ...), custom_call_target="tpu_custom_call" | custom-call | flops 20700000256 | bytes 64800000 | tf_op jit(solution)/shard_map/attend_forward/pallas_call | solution.py:161
  126.4 6.9 %collective-permute-done.9.refs_1_ = bf16[256,4096]{1,0:T(8,128)(2,1)} collective-permute-done((bf16[256,4096]{1,0:T(8,128)(2,1)}, bf16[256,4096]{1,0:T(8,128)(2,1)}, u32[]{:S(2)}, u32[]{:S(2)}) %collective-permute-start.9) | collective-permute-done | bytes 2097184 | tf_op jit(solution)/shard_map/ppermute | solution.py:893
  133.2 9.5 %mix_self.1 = (f32[512,1024]{1,0:T(8,128)}, f32[512,1024]{1,0:T(8,128)}, bf16[512,1024]{1,0:T(8,128)(2,1)}, bf16[512,1024]{1,0:T(8,128)(2,1)S(1)}) custom-call(s32[16]{0:T(128)S(1)} %stack.123.place, bf16[512,1024]{1,0:T(8,128)(2,1)} %copy-done.17, bf16[512,1024]{1,0:T(8,128)(2,1)} %bitcast.150, f32[2,1024]{1,0:T(2,128)S(1)} %get-tuple-element.289.norm_ref, ...), custom_call_target="tpu_custom_call" | custom-call | flops 7245000192 | bytes 22680000 | tf_op jit(solution)/shard_map/mix_self/pallas_call | solution.py:332
  145.9 22.7 %attend_forward.3 = (bf16[512,1024]{1,0:T(8,128)(2,1)S(1)}, f32[8,2,512]{2,1,0:T(2,128)S(1)}) custom-call(bf16[512,1024]{1,0:T(8,128)(2,1)S(1)} %get-tuple-element.109.refs_0_, s32[2,512,1]{2,1,0:T(8,128)S(1)} %get-tuple-element.278.refs_1_.refs_4_, s32[1,512]{1,0:T(1,128)S(1)} %broadcast_in_dim.12.refs_2_.refs_5_, ...), custom_call_target="tpu_custom_call" | custom-call | flops 25300000768 | bytes 79200000 | tf_op jit(solution)/shard_map/attend_forward/pallas_call | solution.py:161
  179.5 7.5 %mix_cross.1 = (f32[512,1024]{1,0:T(8,128)}, f32[512,1024]{1,0:T(8,128)}, bf16[512,1024]{1,0:T(8,128)(2,1)}) custom-call(s32[16]{0:T(128)S(1)} %stack.123.place, bf16[512,1024]{1,0:T(8,128)(2,1)} %copy-done.11, f32[512,1024]{1,0:T(8,128)} %get-tuple-element.111.resid_ref, f32[2,1024]{1,0:T(2,128)S(1)} %get-tuple-element.288.norm_ref, ...), custom_call_target="tpu_custom_call" | custom-call | flops 4600000000 | bytes 14400000 | tf_op jit(solution)/shard_map/mix_cross/pallas_call | solution.py:332
  187.1 15.5 %feed_first.1 = (f32[512,1024]{1,0:T(8,128)S(1)}, bf16[512,2048]{1,0:T(8,128)(2,1)}, bf16[512,512]{1,0:T(8,128)(2,1)}, bf16[512,512]{1,0:T(8,128)(2,1)}) custom-call(s32[16]{0:T(128)S(1)} %stack.123.place, bf16[512,1024]{1,0:T(8,128)(2,1)} %get-tuple-element.112.low_ref.refs_2_, f32[512,1024]{1,0:T(8,128)} %get-tuple-element.113.second_ref, ...), custom_call_target="tpu_custom_call" | custom-call | flops 14949999616 | bytes 46800000 | tf_op jit(solution)/shard_map/feed_first/pallas_call | solution.py:332
  205.3 14.9 %feed_second.1 = (bf16[512,1024]{1,0:T(8,128)(2,1)}, f32[512,1024]{1,0:T(8,128)S(1)}, bf16[512,1024]{1,0:T(8,128)(2,1)S(1)}, f32[2,1024]{1,0:T(2,128)}, bf16[512,2048]{1,0:T(8,128)(2,1)}) custom-call(s32[16]{0:T(128)S(1)} %stack.123.place, bf16[512,1024]{1,0:T(8,128)(2,1)} %get-tuple-element.112.low_ref.refs_2_, f32[512,1024]{1,0:T(8,128)} %copy-done.21, ...), custom_call_target="tpu_custom_call" | custom-call | flops 15525000192 | bytes 48600000 | tf_op jit(solution)/shard_map/feed_second/pallas_call | solution.py:332
  227.6 29.4 %feed_backward.1 = (f32[512,1024]{1,0:T(8,128)}, bf16[512,1024]{1,0:T(8,128)(2,1)}, f32[2,1024]{1,0:T(2,128)}, bf16[512,512]{1,0:T(8,128)(2,1)}, bf16[512,1024]{1,0:T(8,128)(2,1)}) custom-call(s32[16]{0:T(128)} %copy-done.7, bf16[512,1024]{1,0:T(8,128)(2,1)} %copy-done.13, f32[512,1024]{1,0:T(8,128)} %copy-done.22, ...), custom_call_target="tpu_custom_call" | custom-call | flops 33350000640 | bytes 104400000 | tf_op jit(solution)/shard_map/feed_backward/pallas_call | solution.py:332
  258.4 7.7 %wgrad_early.1 = bf16[1024,2048]{1,0:T(8,128)(2,1)} custom-call(s32[16]{0:T(128)S(1)} %copy-done.8, bf16[512,1024]{1,0:T(8,128)(2,1)} %copy-done.11, bf16[512,1024]{1,0:T(8,128)(2,1)} %copy-done.11, bf16[512,1024]{1,0:T(8,128)(2,1)} %get-tuple-element.112.low_ref.refs_2_, bf16[512,512]{1,0:T(8,128)(2,1)} %get-tuple-element.127.refs_3_, ...), custom_call_target="tpu_custom_call" | custom-call | flops 3680000000 | bytes 11520000 | tf_op jit(solution)/shard_map/wgrad_early/pallas_call | solution.py:332
  269.8 27.5 %attend_backward.3 = (bf16[512,1024]{1,0:T(8,128)(2,1)}, f32[2,512,1024]{2,1,0:T(8,128)}, bf16[2,512,1024]{2,1,0:T(8,128)(2,1)}) custom-call(bf16[512,1024]{1,0:T(8,128)(2,1)S(1)} %copy-done.20, bf16[512,1024]{1,0:T(8,128)(2,1)S(1)} %copy-done.12, bf16[512,1024]{1,0:T(8,128)(2,1)S(1)} %copy-done.24, f32[8,2,512]{2,1,0:T(2,128)S(1)} %get-tuple-element.132.refs_3_, ...), custom_call_target="tpu_custom_call" | custom-call | flops 32199999488 | bytes 100800000 | tf_op jit(solution)/shard_map/attend_backward/pallas_call | solution.py:251
  297.4 10.1 %norm_step.1 = (f32[512,1024]{1,0:T(8,128)}, bf16[512,1024]{1,0:T(8,128)(2,1)S(1)}, f32[2,1024]{1,0:T(2,128)}, bf16[512,1024]{1,0:T(8,128)(2,1)S(1)}) custom-call(s32[16]{0:T(128)S(1)} %copy-done.8, bf16[512,1024]{1,0:T(8,128)(2,1)} %get-tuple-element.133.dquery_ref.refs_7_, f32[512,1024]{1,0:T(8,128)} %get-tuple-element.138.d_ref, ...), custom_call_target="tpu_custom_call" | custom-call | flops 7590000128 | bytes 23760000 | tf_op jit(solution)/shard_map/norm_step/pallas_call | solution.py:332
  315.9 11.2 %wgrad_inner.1 = (bf16[512,4352]{1,0:T(8,128)(2,1)}, bf16[512,4352]{1,0:T(8,128)(2,1)}) custom-call(s32[16]{0:T(128)S(1)} %copy-done.8, bf16[512,1024]{1,0:T(8,128)(2,1)} %bitcast.23.left_ref.refs_0_.refs_1_, bf16[512,1024]{1,0:T(8,128)(2,1)} %bitcast.23.left_ref.refs_0_.refs_1_, bf16[512,1024]{1,0:T(8,128)(2,1)} %copy-done.17, ...), custom_call_target="tpu_custom_call" | custom-call | flops 7360000000 | bytes 23040000 | tf_op jit(solution)/shard_map/wgrad_inner/pallas_call | solution.py:332
  342.2 17.3 %attend_backward.4 = (bf16[512,1024]{1,0:T(8,128)(2,1)}, f32[2,512,1024]{2,1,0:T(8,128)}, bf16[2,512,1024]{2,1,0:T(8,128)(2,1)}) custom-call(bf16[512,1024]{1,0:T(8,128)(2,1)S(1)} %copy-done.1, bf16[512,1024]{1,0:T(8,128)(2,1)S(1)} %copy-done.18, bf16[512,1024]{1,0:T(8,128)(2,1)S(1)} %copy-done.15, f32[8,2,512]{2,1,0:T(2,128)S(1)} %get-tuple-element.154.refs_3_, ...), custom_call_target="tpu_custom_call" | custom-call | flops 20700000256 | bytes 64800000 | tf_op jit(solution)/shard_map/attend_backward/pallas_call | solution.py:251
  359.5 9.1 %collective-permute-done.26 = bf16[2,128,2176]{2,1,0:T(8,128)(2,1)S(1)} collective-permute-done((bf16[2,128,2176]{2,1,0:T(8,128)(2,1)S(1)}, bf16[2,128,2176]{2,1,0:T(8,128)(2,1)S(1)}, u32[]{:S(2)}, u32[]{:S(2)}) %collective-permute-start.26) | collective-permute-done | bytes 1114144 | tf_op jit(solution)/shard_map/ppermute | solution.py:1017
  369.8 6.9 %attend_backward.5 = (bf16[512,1024]{1,0:T(8,128)(2,1)}, f32[2,512,1024]{2,1,0:T(8,128)}, bf16[2,512,1024]{2,1,0:T(8,128)(2,1)}) custom-call(bf16[512,1024]{1,0:T(8,128)(2,1)S(1)} %copy-done.1, bf16[512,1024]{1,0:T(8,128)(2,1)S(1)} %copy-done.18, bf16[512,1024]{1,0:T(8,128)(2,1)S(1)} %copy-done.15, ...), custom_call_target="tpu_custom_call", output_to_operand_aliasing={{0}: (10, {}), {1}: (11, {}), {2}: (12, {})} | custom-call | flops 6899999744 | bytes 21600000 | tf_op jit(solution)/shard_map/attend_backward/pallas_call | solution.py:251
  383.3 9.0 %collective-permute-done.35 = bf16[128,2176]{1,0:T(8,128)(2,1)S(1)} collective-permute-done((bf16[128,2176]{1,0:T(8,128)(2,1)S(1)}, bf16[128,2176]{1,0:T(8,128)(2,1)S(1)}, u32[]{:S(2)}, u32[]{:S(2)}) %collective-permute-start.35) | collective-permute-done | bytes 557088 | tf_op jit(solution)/shard_map/ppermute | solution.py:1026
  394.7 8.6 %target_back.1 = bf16[512,1024]{1,0:T(8,128)(2,1)S(1)} custom-call(s32[16]{0:T(128)S(1)} %copy-done.8, bf16[512,1024]{1,0:T(8,128)(2,1)} %get-tuple-element.164.refs_0_.refs_3_, bf16[2,512,1024]{2,1,0:T(8,128)(2,1)} %add_convert_fusion.2.refs_1_.refs_2_.refs_4_.refs_5_, bf16[2,512,1024]{2,1,0:T(8,128)(2,1)} %add_convert_fusion.2.refs_1_.refs_2_.refs_4_.refs_5_, ...), custom_call_target="tpu_custom_call" | custom-call | flops 10350000128 | bytes 32400000 | tf_op jit(solution)/shard_map/target_back/pallas_call | solution.py:332
  403.3 9.3 %wgrad_self.1 = (bf16[512,3072]{1,0:T(8,128)(2,1)}, bf16[512,3072]{1,0:T(8,128)(2,1)}) custom-call(s32[16]{0:T(128)S(1)} %copy-done.8, bf16[512,1024]{1,0:T(8,128)(2,1)} %bitcast.151, bf16[512,1024]{1,0:T(8,128)(2,1)} %bitcast.152, bf16[512,1024]{1,0:T(8,128)(2,1)} %bitcast.153, bf16[512,1024]{1,0:T(8,128)(2,1)} %get-tuple-element.164.refs_0_.refs_3_, ...), custom_call_target="tpu_custom_call" | custom-call | flops 5520000000 | bytes 17280000 | tf_op jit(solution)/shard_map/wgrad_self/pallas_call | solution.py:332
  419.8 8.1 %collective-permute-done.36 = bf16[2,32,4352]{2,1,0:T(8,128)(2,1)} collective-permute-done((bf16[2,32,4352]{2,1,0:T(8,128)(2,1)S(1)}, bf16[2,32,4352]{2,1,0:T(8,128)(2,1)}, u32[]{:S(2)}, u32[]{:S(2)}) %collective-permute-start.36) | collective-permute-done | bytes 557088 | tf_op jit(solution)/shard_map/ppermute | solution.py:1034
  429.9 11.3 %collective-permute-start.41 = (bf16[32,4352]{1,0:T(8,128)(2,1)S(1)}, bf16[32,4352]{1,0:T(8,128)(2,1)S(1)}, u32[]{:S(2)}, u32[]{:S(2)}) collective-permute-start(bf16[32,4352]{1,0:T(8,128)(2,1)S(1)} %dynamic-slice_bitcast_fusion.10), channel_id=1, source_target_pairs={{0,4},{1,5},{2,6},{3,7},{4,0},{5,1},{6,2},{7,3},{8,12},{9,13},{10,... | collective-permute-start | bytes 835592 | tf_op jit(solution)/shard_map/ppermute | solution.py:1039
  454.4 11.4 %collective-permute-done.40 = bf16[2,128,1536]{2,1,0:T(8,128)(2,1)S(1)} collective-permute-done((bf16[2,128,1536]{2,1,0:T(8,128)(2,1)S(1)}, bf16[2,128,1536]{2,1,0:T(8,128)(2,1)S(1)}, u32[]{:S(2)}, u32[]{:S(2)}) %collective-permute-start.40) | collective-permute-done | bytes 786464 | tf_op jit(solution)/shard_map/ppermute | solution.py:1018
  471.5 7.0 %collective-permute-done.42 = bf16[128,1536]{1,0:T(8,128)(2,1)S(1)} collective-permute-done((bf16[128,1536]{1,0:T(8,128)(2,1)S(1)}, bf16[128,1536]{1,0:T(8,128)(2,1)S(1)}, u32[]{:S(2)}, u32[]{:S(2)}) %collective-permute-start.42) | collective-permute-done | bytes 393248 | tf_op jit(solution)/shard_map/ppermute | solution.py:1025
  (308 shorter events, 182.2 us)
Async XLA Ops:
  13.9 34.8 %collective-permute-start = (bf16[256,5120]{1,0:T(8,128)(2,1)}, bf16[256,5120]{1,0:T(8,128)(2,1)}, u32[]{:S(2)}, u32[]{:S(2)}) collective-permute-start(bf16[256,5120]{1,0:T(8,128)(2,1)} %constant_dynamic-update-slice_fusion.refs_0_.refs_2_.refs_3_), channel_id=1, source_target_pairs={{0,8},{1,17},{2,10},{3,19},{4,12},{5,21},{6,14},{7,23},{8,0},{9,25... | collective-permute-start | bytes 7864328 | tf_op jit(solution)/shard_map/ppermute | solution.py:893
  18.2 30.5 %all-to-all-start = ((bf16[4,128,1024]{2,1,0:T(8,128)(2,1)}), bf16[4,128,1024]{2,1,0:T(8,128)(2,1)S(1)}, u32[]{:S(2)}, u32[]{:S(2)}) async-start(bf16[4,128,1024]{2,1,0:T(8,128)(2,1)} %bitcast.136), calls=%async_computation | async-start | bytes 2097152 | tf_op jit(solution)/shard_map/all_to_all | solution.py:1086
  23.3 23.6 %collective-permute-start.2 = (bf16[6,256]{1,0:T(8,128)(2,1)S(1)}, bf16[6,256]{1,0:T(8,128)(2,1)S(1)}, u32[]{:S(2)}, u32[]{:S(2)}) collective-permute-start(bf16[6,256]{1,0:T(8,128)(2,1)S(1)} %stack.130), channel_id=1, source_target_pairs={{0,8},{8,0},{16,24},{24,16},{1,9},{9,1},{17,25},{25,17},{2,10},{10... | collective-permute-start | bytes 9224 | tf_op jit(solution)/shard_map/ppermute | solution.py:1139
  68.2 26.4 %collective-permute-start.7 = (bf16[256,4096]{1,0:T(8,128)(2,1)}, bf16[256,4096]{1,0:T(8,128)(2,1)}, u32[]{:S(2)}, u32[]{:S(2)}) collective-permute-start(bf16[256,4096]{1,0:T(8,128)(2,1)} %copy-done.44), channel_id=1, source_target_pairs={{0,8},{1,17},{2,10},{3,19},{4,12},{5,21},{6,14},{7,23},{8,0},{9,25... | collective-permute-start | bytes 6291464 | tf_op jit(solution)/shard_map/ppermute | solution.py:893
  78.7 39.7 %all-to-all-start.1 = ((bf16[4,128,1024]{2,1,0:T(8,128)(2,1)}), bf16[4,128,1024]{2,1,0:T(8,128)(2,1)}, u32[]{:S(2)}, u32[]{:S(2)}) async-start(bf16[4,128,1024]{2,1,0:T(8,128)(2,1)} %bitcast.135), calls=%async_computation.1 | async-start | bytes 2097152 | tf_op jit(solution)/shard_map/all_to_all | solution.py:1086
  96.9 28.2 %collective-permute-start.11 = (bf16[128,4096]{1,0:T(8,128)(2,1)}, bf16[128,4096]{1,0:T(8,128)(2,1)}, u32[]{:S(2)}, u32[]{:S(2)}) collective-permute-start(bf16[128,4096]{1,0:T(8,128)(2,1)} %constant_dynamic-slice_fusion.2), channel_id=1, source_target_pairs={{0,16},{1,9},{2,18},{3,11},{4,20},{5,13},{6,22},{7,15},{8,24},{9,1... | collective-permute-start | bytes 3145736 | tf_op jit(solution)/shard_map/ppermute | solution.py:904
  97.5 35.8 %collective-permute-start.9 = (bf16[256,4096]{1,0:T(8,128)(2,1)}, bf16[256,4096]{1,0:T(8,128)(2,1)}, u32[]{:S(2)}, u32[]{:S(2)}) collective-permute-start(bf16[256,4096]{1,0:T(8,128)(2,1)} %refs_0_.2), channel_id=1, source_target_pairs={{0,8},{1,17},{2,10},{3,19},{4,12},{5,21},{6,14},{7,23},{8,0},{9,25... | collective-permute-start | bytes 6291464 | tf_op jit(solution)/shard_map/ppermute | solution.py:893
  98.9 34.3 %collective-permute-start.10 = (bf16[256,4096]{1,0:T(8,128)(2,1)}, bf16[256,4096]{1,0:T(8,128)(2,1)}, u32[]{:S(2)}, u32[]{:S(2)}) collective-permute-start(bf16[256,4096]{1,0:T(8,128)(2,1)} %collective-permute-done.7.refs_1_.refs_6_.refs_8_.refs_13_.refs_11_.refs_16_.refs_21_), channel_id=1, source_target_pairs={{0,1},{1,0},{2,3},{3,2},{4,5},{5,4},{6,7},{7,6},{8,9},{9,8},{10,11... | collective-permute-start | bytes 6291464 | tf_op jit(solution)/shard_map/ppermute | solution.py:897
  125.7 42.9 %collective-permute-start.17 = (bf16[1024,1024]{1,0:T(8,128)(2,1)}, bf16[1024,1024]{1,0:T(8,128)(2,1)}, u32[]{:S(2)}, u32[]{:S(2)}) collective-permute-start(bf16[1024,1024]{1,0:T(8,128)(2,1)} %refs_5_.1), channel_id=1, source_target_pairs={{0,8},{1,17},{2,10},{3,19},{4,12},{5,21},{6,14},{7,23},{8,0},{9,25... | collective-permute-start | bytes 6291464 | tf_op jit(solution)/shard_map/ppermute | solution.py:893
  142.7 44.4 %collective-permute-start.14 = (bf16[256,4096]{1,0:T(8,128)(2,1)}, bf16[256,4096]{1,0:T(8,128)(2,1)}, u32[]{:S(2)}, u32[]{:S(2)}) collective-permute-start(bf16[256,4096]{1,0:T(8,128)(2,1)} %collective-permute-done.9.refs_1_), channel_id=1, source_target_pairs={{0,1},{1,0},{2,3},{3,2},{4,5},{5,4},{6,7},{7,6},{8,9},{9,8},{10,11... | collective-permute-start | bytes 6291464 | tf_op jit(solution)/shard_map/ppermute | solution.py:897
  145.4 27.5 %collective-permute-start.15 = (bf16[128,4096]{1,0:T(8,128)(2,1)S(1)}, bf16[128,4096]{1,0:T(8,128)(2,1)}, u32[]{:S(2)}, u32[]{:S(2)}) collective-permute-start(bf16[128,4096]{1,0:T(8,128)(2,1)S(1)} %constant_dynamic-slice_fusion.1), channel_id=1, source_target_pairs={{0,16},{1,9},{2,18},{3,11},{4,20},{5,13},{6,22},{7,15},{8,24},{9,1... | collective-permute-start | bytes 3145736 | tf_op jit(solution)/shard_map/ppermute | solution.py:904
  172.9 32.4 %collective-permute-start.18 = (bf16[1024,1024]{1,0:T(8,128)(2,1)}, bf16[1024,1024]{1,0:T(8,128)(2,1)}, u32[]{:S(2)}, u32[]{:S(2)}) collective-permute-start(bf16[1024,1024]{1,0:T(8,128)(2,1)} %collective-permute-done.17.refs_6_), channel_id=1, source_target_pairs={{0,1},{1,0},{2,3},{3,2},{4,5},{5,4},{6,7},{7,6},{8,9},{9,8},{10,11... | collective-permute-start | bytes 6291464 | tf_op jit(solution)/shard_map/ppermute | solution.py:897
  174.7 30.6 %all-to-all-start.2 = ((bf16[4,128,1024]{2,1,0:T(8,128)(2,1)}), bf16[4,128,1024]{2,1,0:T(8,128)(2,1)}, u32[]{:S(2)}, u32[]{:S(2)}) async-start(bf16[4,128,1024]{2,1,0:T(8,128)(2,1)} %bitcast.154), calls=%async_computation.2 | async-start | bytes 2097152 | tf_op jit(solution)/shard_map/all_to_all | solution.py:1086
  179.3 136.6 %reduce-scatter.3.cloned.1.call-start = ((), (), s32[]{:S(2)}) async-start(), calls=%async_computation.5 | async-start | bytes 4718592 | tf_op jit(solution)/shard_map/reduce_scatter | solution.py:998
  223.1 33.8 %collective-permute-start.21 = (bf16[128,1024]{1,0:T(8,128)(2,1)S(1)}, bf16[128,1024]{1,0:T(8,128)(2,1)S(1)}, u32[]{:S(2)}, u32[]{:S(2)}) collective-permute-start(bf16[128,1024]{1,0:T(8,128)(2,1)S(1)} %get-tuple-element.273), channel_id=1, source_target_pairs={{0,2},{1,3},{2,0},{3,1},{4,6},{5,7},{6,4},{7,5},{8,10},{9,11},{10,... | collective-permute-start | bytes 786440 | tf_op jit(solution)/shard_map/ppermute | solution.py:1097
  223.8 33.2 %collective-permute-start.22 = (bf16[128,1024]{1,0:T(8,128)(2,1)S(1)}, bf16[128,1024]{1,0:T(8,128)(2,1)S(1)}, u32[]{:S(2)}, u32[]{:S(2)}) collective-permute-start(bf16[128,1024]{1,0:T(8,128)(2,1)S(1)} %get-tuple-element.272), channel_id=1, source_target_pairs={{0,4},{1,5},{2,6},{3,7},{4,0},{5,1},{6,2},{7,3},{8,12},{9,13},{10,... | collective-permute-start | bytes 786440 | tf_op jit(solution)/shard_map/ppermute | solution.py:1097
  226.1 30.8 %collective-permute-start.23 = (bf16[128,1024]{1,0:T(8,128)(2,1)S(1)}, bf16[128,1024]{1,0:T(8,128)(2,1)S(1)}, u32[]{:S(2)}, u32[]{:S(2)}) collective-permute-start(bf16[128,1024]{1,0:T(8,128)(2,1)S(1)} %get-tuple-element.271), channel_id=1, source_target_pairs={{0,6},{1,7},{2,4},{3,5},{4,2},{5,3},{6,0},{7,1},{8,14},{9,15},{10,... | collective-permute-start | bytes 786440 | tf_op jit(solution)/shard_map/ppermute | solution.py:1097
  266.1 153.0 %reduce-scatter.5.cloned.1.call-start = ((), (), s32[]{:S(2)}) async-start(), calls=%async_computation.6 | async-start | bytes 655360 | tf_op jit(solution)/shard_map/reduce_scatter | solution.py:998
  328.3 41.4 %collective-permute-start.27 = (bf16[128,1024]{1,0:T(8,128)(2,1)}, bf16[128,1024]{1,0:T(8,128)(2,1)S(1)}, u32[]{:S(2)}, u32[]{:S(2)}) collective-permute-start(bf16[128,1024]{1,0:T(8,128)(2,1)} %get-tuple-element.267), channel_id=1, source_target_pairs={{0,2},{1,3},{2,0},{3,1},{4,6},{5,7},{6,4},{7,5},{8,10},{9,11},{10,... | collective-permute-start | bytes 786440 | tf_op jit(solution)/shard_map/ppermute | solution.py:1097
  328.3 41.4 %collective-permute-start.28 = (bf16[128,1024]{1,0:T(8,128)(2,1)}, bf16[128,1024]{1,0:T(8,128)(2,1)S(1)}, u32[]{:S(2)}, u32[]{:S(2)}) collective-permute-start(bf16[128,1024]{1,0:T(8,128)(2,1)} %get-tuple-element.266), channel_id=1, source_target_pairs={{0,4},{1,5},{2,6},{3,7},{4,0},{5,1},{6,2},{7,3},{8,12},{9,13},{10,... | collective-permute-start | bytes 786440 | tf_op jit(solution)/shard_map/ppermute | solution.py:1097
  340.3 28.3 %collective-permute-start.26 = (bf16[2,128,2176]{2,1,0:T(8,128)(2,1)S(1)}, bf16[2,128,2176]{2,1,0:T(8,128)(2,1)S(1)}, u32[]{:S(2)}, u32[]{:S(2)}) collective-permute-start(bf16[2,128,2176]{2,1,0:T(8,128)(2,1)S(1)} %dynamic-slice_bitcast_fusion.1), channel_id=1, source_target_pairs={{0,8},{8,0},{16,24},{24,16},{1,9},{9,1},{17,25},{25,17},{2,10},{10... | collective-permute-start | bytes 3342344 | tf_op jit(solution)/shard_map/ppermute | solution.py:1017
  341.2 35.6 %collective-permute-start.34 = (bf16[2,128,2176]{2,1,0:T(8,128)(2,1)S(1)}, bf16[2,128,2176]{2,1,0:T(8,128)(2,1)S(1)}, u32[]{:S(2)}, u32[]{:S(2)}) collective-permute-start(bf16[2,128,2176]{2,1,0:T(8,128)(2,1)S(1)} %dynamic-slice_bitcast_fusion), channel_id=1, source_target_pairs={{0,16},{8,24},{16,0},{24,8},{1,17},{9,25},{17,1},{25,9},{2,18},{10... | collective-permute-start | bytes 3342344 | tf_op jit(solution)/shard_map/ppermute | solution.py:1018
  412.6 30.4 %collective-permute-start.38 = (bf16[512,3072]{1,0:T(8,128)(2,1)}, bf16[512,3072]{1,0:T(8,128)(2,1)}, u32[]{:S(2)}, u32[]{:S(2)}) collective-permute-start(bf16[512,3072]{1,0:T(8,128)(2,1)} %get-tuple-element.166), channel_id=1, source_target_pairs={{0,1},{1,0},{2,3},{3,2},{4,5},{5,4},{6,7},{7,6},{8,9},{9,8},{10,11... | collective-permute-start | bytes 9437192 | tf_op jit(solution)/shard_map/ppermute | solution.py:1010
  416.7 24.5 %collective-permute-start.37 = (bf16[128,1024]{1,0:T(8,128)(2,1)S(1)}, bf16[128,1024]{1,0:T(8,128)(2,1)}, u32[]{:S(2)}, u32[]{:S(2)}) collective-permute-start(bf16[128,1024]{1,0:T(8,128)(2,1)S(1)} %get-tuple-element.265), channel_id=1, source_target_pairs={{0,6},{1,7},{2,4},{3,5},{4,2},{5,3},{6,0},{7,1},{8,14},{9,15},{10,... | collective-permute-start | bytes 786440 | tf_op jit(solution)/shard_map/ppermute | solution.py:1097
  (88 other events, 1023.8 us)
Sparse Core Ops, SparseCore 0:
  266.2 48.3 reduce-scatter.2
  331.4 24.1 reduce-scatter.4

commit v5 on v4

--- a/solution.py
+++ b/solution.py
@@ -1193,7 +1193,6 @@
     if halving:
         w_mid = gather_far(w_mid, mixed)
         w_out = gather_first(after(feed_out, mixed))
-        mixed = after(mixed, w_in[1])
         at_o, at_cq, at_co = (w_mid, 0), (w_mid, 1), (w_mid, 2)
         at_down, at_up = (w_mid, 6), (w_mid, 7)
     resid_one, first, first_low, cross_q = mix(
@@ -1201,6 +1200,7 @@
     )
     if halving:
         w_in = gather_near(gather_swap(w_in, cross_q), core, cross_q)
+        cross_q = after(cross_q, w_in[1])
     cross_mixed, cross_totals = attend_forward(
         cross_q, ckv_all, cross_keys, cross_rows, block, False
     )
@@ -1208,6 +1208,7 @@
         w_in = gather_far(w_in, cross_mixed)
         w_out = gather_far(gather_near(gather_swap(w_out, cross_mixed), core, cross_mixed))
         out_first, out_second = w_out[:2], w_out[2:]
+    cross_mixed = after(cross_mixed, grad_out)
     resid_two, second, second_low = mix(
         place, cross_mixed, view(first, width, 0), norm_two, *at_co, None, None, "mix_cross"
     )
@@ -1329,7 +1330,7 @@
             begun,
         )
         if halving and span[0] == 0:
-            d_mixed = after(d_mixed, begun[0], inner_sums.plane_one(), *grad_source[1:3])
+            d_mixed = after(d_mixed, begun[0], *grad_source[1:3])
     d_q, *d_kv = begun
     d_kv = collect(d_kv[0], d_kv[1:])
     at_self = at_q if halving else ((jnp.concatenate([at_q[0][0], at_kv[0][0]], axis=1),), 0)
@@ -1348,7 +1349,7 @@
         grad_source = set_down(grad_source)
         grad_target = set_down(grad_target)
     if halving:
-        d_q = after(d_q, inner_sums.plane_two())
+        d_q = after(d_q, inner_sums.plane_one())
         late = Scatter(
             *wgrad(
                 place,
@@ -1361,15 +1362,15 @@
             )
         )
         grad_source = set_down(grad_source, late.send)
-        late.keep = after(late.keep, inner_sums.z_one(), grad_source, grad_target[1])
+        late.keep = after(late.keep, inner_sums.plane_two(), grad_source, *grad_target[1:])
         late.core()
         late.plane_one()
         late.one, late.two, *_ = lax.optimization_barrier(
-            (late.one, late.two, inner_sums.z_two(), *grad_target)
+            (late.one, late.two, inner_sums.z_one(), *grad_target)
         )
         grad_target = set_down(grad_target, late.one)
         late.plane_two()
-        late.item = after(late.item, grad_target)
+        late.item = after(late.item, grad_target, inner_sums.z_two())
         late.z_one()
         late.z_two()
         grad_co, grad_down = early[:, :width], early[:, width : width + half]

time: 522 us -> 508 us (0.973)
  starting transfers between devices: 73.1 us -> 65.4 us
    ppermute x9, waiting for transfers between devices: 0.32 us -> 11.1 us  [send_back(): parts.append(lax.ppermute(take(item, which ^ bit, 0), 'seq', pairs))]
    ppermute x2, waiting for transfers between devices: 10.1 us -> 1.75 us  [plane_one(): from_x = lax.ppermute(take(self.one, 1 - x, 1), 'dp', swap_pairs(4, 1))]
    ppermute x2, waiting for transfers between devices: 9.63 us -> 2.79 us  [plane_two(): from_x = lax.ppermute(take(self.two, 1 - x, 0), 'dp', swap_pairs(4, 1))]
    ppermute x4, waiting for transfers between devices: 11.4 us -> 4.61 us  [gather_first(): return (own, lax.ppermute(own, ('dp', 'seq'), by_core(1, 2)))]
    ppermute x4, waiting for transfers between devices: 17 us -> 22.4 us  [gather_near(): return parts + (lax.ppermute(half_one, ('dp', 'seq'), by_core(2, 1)),)]
  transfers between devices with their start and end apart: 51 -> 51, of which waited for: 20 -> 22; matrix products, arithmetic and copies ran while one was open for 8% -> 9% of each run, Pallas kernels for 41% -> 42%
where the time goes in v5:
time: 508 us; the launch traced here: 502 us
  Pallas kernels  244 us (48%)
  waiting for transfers between devices  113 us (22%)
  starting transfers between devices  65.4 us (13%)
  local copies, waits for them, and re-layouts  47.8 us (9%)
  other arithmetic  16.9 us (3%)
  between operations  15.4 us (3%)
    pallas_call x17, Pallas kernels, run(): pl.pallas_call(kernel, grid_spec=pltpu.PrefetchScalarGridSpec(num_scalar_...  151 us
    pallas_call x3, Pallas kernels, attend_backward(): pl.pallas_call(functools.partial(backward_kernel, pieces, block, causal,...  51.8 us
    pallas_call x2, Pallas kernels, attend_forward(): pl.pallas_call(functools.partial(forward_kernel, pieces, block, causal),...  41.1 us
    unnamed x136, local copies, waits for them, and re-layouts  29.3 us
    ppermute x4, waiting for transfers between devices, gather_near(): return parts + (lax.ppermute(half_one, ('dp', 'seq'), by_core(2, 1)),)  22.4 us
    ppermute x3, waiting for transfers between devices, body(): lax.ppermute(vectors, 'dp', swap_pairs(4, bit))  17.4 us
    ppermute x2, waiting for transfers between devices, plane_two(): from_y = lax.ppermute(take(self.one, 1 - y, 0), 'dp', swap_pairs(4, 2))  16.5 us
    all_to_all x3, starting transfers between devices, to_sequence(): lax.all_to_all(item.swapaxes(0, 1), 'seq', 0, 0, axis_index_groups=apart,...  14.3 us
  transfers between devices with their start and end apart: 51, of which 22 were waited for; matrix products, arithmetic and copies ran while one was open for 9% of the time, Pallas kernels for 42%

profile of v5, /device:TPU:0, one launch (start us, length us, event | category | flops | bytes accessed | tf_op | source)
XLA Modules:
  0.0 502.0 jit_solution(13017470031485368446)
XLA Ops:
  31.0 15.9 %collective-permute-done.2 = bf16[6,256]{1,0:T(8,128)(2,1)S(1)} collective-permute-done((bf16[6,256]{1,0:T(8,128)(2,1)S(1)}, bf16[6,256]{1,0:T(8,128)(2,1)S(1)}, u32[]{:S(2)}, u32[]{:S(2)}) %collective-permute-start.2) | collective-permute-done | bytes 3104 | tf_op jit(solution)/shard_map/ppermute | solution.py:1139
  51.2 16.9 %collective-permute-done.5.refs_3_.refs_5_.refs_6_ = bf16[128,5120]{1,0:T(8,128)(2,1)S(1)} collective-permute-done((bf16[128,5120]{1,0:T(8,128)(2,1)S(1)}, bf16[128,5120]{1,0:T(8,128)(2,1)S(1)}, u32[]{:S(2)}, u32[]{:S(2)}) %collective-permute-start.5) | collective-permute-done | bytes 1310752 | tf_op jit(solution)/shard_map/ppermute | solution.py:904
  99.0 18.2 %attend_forward.2 = (bf16[512,1024]{1,0:T(8,128)(2,1)S(1)}, f32[8,2,512]{2,1,0:T(2,128)S(1)}) custom-call(bf16[512,1024]{1,0:T(8,128)(2,1)S(1)} %self_q.1.refs_0_, s32[2,512,1]{2,1,0:T(8,128)S(1)} %get-tuple-element.281.refs_1_.refs_4_, s32[1,512]{1,0:T(1,128)S(1)} %multiply_add_fusion.refs_2_.refs_5_, ...), custom_call_target="tpu_custom_call" | custom-call | flops 20700000256 | bytes 64800000 | tf_op jit(solution)/shard_map/attend_forward/pallas_call | solution.py:161
  132.4 9.5 %mix_self.1 = (f32[512,1024]{1,0:T(8,128)}, f32[512,1024]{1,0:T(8,128)}, bf16[512,1024]{1,0:T(8,128)(2,1)}, bf16[512,1024]{1,0:T(8,128)(2,1)S(1)}) custom-call(s32[16]{0:T(128)S(1)} %stack.123.place, bf16[512,1024]{1,0:T(8,128)(2,1)} %copy-done.17, bf16[512,1024]{1,0:T(8,128)(2,1)} %bitcast.150, f32[2,1024]{1,0:T(2,128)S(1)} %get-tuple-element.291.norm_ref, ...), custom_call_target="tpu_custom_call" | custom-call | flops 7245000192 | bytes 22680000 | tf_op jit(solution)/shard_map/mix_self/pallas_call | solution.py:332
  144.3 22.9 %attend_forward.3 = (bf16[512,1024]{1,0:T(8,128)(2,1)S(1)}, f32[8,2,512]{2,1,0:T(2,128)S(1)}) custom-call(bf16[512,1024]{1,0:T(8,128)(2,1)S(1)} %get-tuple-element.110.refs_0_, s32[2,512,1]{2,1,0:T(8,128)S(1)} %get-tuple-element.280.refs_1_.refs_4_, s32[1,512]{1,0:T(1,128)S(1)} %broadcast_in_dim.12.refs_2_.refs_5_, ...), custom_call_target="tpu_custom_call" | custom-call | flops 25300000768 | bytes 79200000 | tf_op jit(solution)/shard_map/attend_forward/pallas_call | solution.py:161
  172.9 7.4 %mix_cross.1 = (f32[512,1024]{1,0:T(8,128)}, f32[512,1024]{1,0:T(8,128)}, bf16[512,1024]{1,0:T(8,128)(2,1)}) custom-call(s32[16]{0:T(128)S(1)} %stack.123.place, bf16[512,1024]{1,0:T(8,128)(2,1)} %copy-done.13, f32[512,1024]{1,0:T(8,128)} %get-tuple-element.113.resid_ref, f32[2,1024]{1,0:T(2,128)S(1)} %get-tuple-element.290.norm_ref, ...), custom_call_target="tpu_custom_call" | custom-call | flops 4600000000 | bytes 14400000 | tf_op jit(solution)/shard_map/mix_cross/pallas_call | solution.py:332
  185.8 15.4 %feed_first.1 = (f32[512,1024]{1,0:T(8,128)S(1)}, bf16[512,2048]{1,0:T(8,128)(2,1)}, bf16[512,512]{1,0:T(8,128)(2,1)}, bf16[512,512]{1,0:T(8,128)(2,1)}) custom-call(s32[16]{0:T(128)S(1)} %stack.123.place, bf16[512,1024]{1,0:T(8,128)(2,1)} %get-tuple-element.114.low_ref.refs_2_, f32[512,1024]{1,0:T(8,128)} %get-tuple-element.115.second_ref, ...), custom_call_target="tpu_custom_call" | custom-call | flops 14949999616 | bytes 46800000 | tf_op jit(solution)/shard_map/feed_first/pallas_call | solution.py:332
  203.5 15.4 %feed_second.1 = (bf16[512,1024]{1,0:T(8,128)(2,1)}, f32[512,1024]{1,0:T(8,128)S(1)}, bf16[512,1024]{1,0:T(8,128)(2,1)S(1)}, f32[2,1024]{1,0:T(2,128)}, bf16[512,2048]{1,0:T(8,128)(2,1)}) custom-call(s32[16]{0:T(128)S(1)} %stack.123.place, bf16[512,1024]{1,0:T(8,128)(2,1)} %get-tuple-element.114.low_ref.refs_2_, f32[512,1024]{1,0:T(8,128)} %copy-done.21, ...), custom_call_target="tpu_custom_call" | custom-call | flops 15525000192 | bytes 48600000 | tf_op jit(solution)/shard_map/feed_second/pallas_call | solution.py:332
  226.3 29.1 %feed_backward.1 = (f32[512,1024]{1,0:T(8,128)}, bf16[512,1024]{1,0:T(8,128)(2,1)}, f32[2,1024]{1,0:T(2,128)}, bf16[512,512]{1,0:T(8,128)(2,1)}, bf16[512,1024]{1,0:T(8,128)(2,1)}) custom-call(s32[16]{0:T(128)} %copy-done.7, bf16[512,1024]{1,0:T(8,128)(2,1)} %copy-done.15, f32[512,1024]{1,0:T(8,128)} %copy-done.22, ...), custom_call_target="tpu_custom_call" | custom-call | flops 33350000640 | bytes 104400000 | tf_op jit(solution)/shard_map/feed_backward/pallas_call | solution.py:332
  256.8 7.7 %wgrad_early.1 = bf16[1024,2048]{1,0:T(8,128)(2,1)} custom-call(s32[16]{0:T(128)S(1)} %copy-done.8, bf16[512,1024]{1,0:T(8,128)(2,1)} %copy-done.13, bf16[512,1024]{1,0:T(8,128)(2,1)} %copy-done.13, bf16[512,1024]{1,0:T(8,128)(2,1)} %get-tuple-element.114.low_ref.refs_2_, bf16[512,512]{1,0:T(8,128)(2,1)} %get-tuple-element.129.refs_3_, ...), custom_call_target="tpu_custom_call" | custom-call | flops 3680000000 | bytes 11520000 | tf_op jit(solution)/shard_map/wgrad_early/pallas_call | solution.py:332
  268.3 27.4 %attend_backward.3 = (bf16[512,1024]{1,0:T(8,128)(2,1)}, f32[2,512,1024]{2,1,0:T(8,128)}, bf16[2,512,1024]{2,1,0:T(8,128)(2,1)}) custom-call(bf16[512,1024]{1,0:T(8,128)(2,1)S(1)} %copy-done.20, bf16[512,1024]{1,0:T(8,128)(2,1)S(1)} %copy-done.14, bf16[512,1024]{1,0:T(8,128)(2,1)S(1)} %copy-done.24, f32[8,2,512]{2,1,0:T(2,128)S(1)} %get-tuple-element.134.refs_3_, ...), custom_call_target="tpu_custom_call" | custom-call | flops 32199999488 | bytes 100800000 | tf_op jit(solution)/shard_map/attend_backward/pallas_call | solution.py:251
  295.7 10.1 %norm_step.1 = (f32[512,1024]{1,0:T(8,128)}, bf16[512,1024]{1,0:T(8,128)(2,1)S(1)}, f32[2,1024]{1,0:T(2,128)}, bf16[512,1024]{1,0:T(8,128)(2,1)S(1)}) custom-call(s32[16]{0:T(128)S(1)} %copy-done.8, bf16[512,1024]{1,0:T(8,128)(2,1)} %get-tuple-element.135.dquery_ref.refs_7_, f32[512,1024]{1,0:T(8,128)} %get-tuple-element.140.d_ref, ...), custom_call_target="tpu_custom_call" | custom-call | flops 7590000128 | bytes 23760000 | tf_op jit(solution)/shard_map/norm_step/pallas_call | solution.py:332
  307.9 6.1 %source_back.1 = bf16[512,1024]{1,0:T(8,128)(2,1)S(1)} custom-call(s32[16]{0:T(128)S(1)} %copy-done.8, bf16[2,512,1024]{2,1,0:T(8,128)(2,1)} %add_convert_fusion.3.refs_0_.refs_1_.refs_4_.refs_5_, bf16[2,512,1024]{2,1,0:T(8,128)(2,1)} %add_convert_fusion.3.refs_0_.refs_1_.refs_4_.refs_5_, ...), custom_call_target="tpu_custom_call" | custom-call | flops 6899999744 | bytes 21600000 | tf_op jit(solution)/shard_map/source_back/pallas_call | solution.py:332
  315.5 11.2 %wgrad_inner.1 = (bf16[512,4352]{1,0:T(8,128)(2,1)}, bf16[512,4352]{1,0:T(8,128)(2,1)}) custom-call(s32[16]{0:T(128)S(1)} %copy-done.8, bf16[512,1024]{1,0:T(8,128)(2,1)} %bitcast.23.left_ref.refs_0_.refs_1_, bf16[512,1024]{1,0:T(8,128)(2,1)} %bitcast.23.left_ref.refs_0_.refs_1_, bf16[512,1024]{1,0:T(8,128)(2,1)} %copy-done.17, ...), custom_call_target="tpu_custom_call" | custom-call | flops 7360000000 | bytes 23040000 | tf_op jit(solution)/shard_map/wgrad_inner/pallas_call | solution.py:332
  343.0 17.3 %attend_backward.4 = (bf16[512,1024]{1,0:T(8,128)(2,1)}, f32[2,512,1024]{2,1,0:T(8,128)}, bf16[2,512,1024]{2,1,0:T(8,128)(2,1)}) custom-call(bf16[512,1024]{1,0:T(8,128)(2,1)S(1)} %copy-done.1, bf16[512,1024]{1,0:T(8,128)(2,1)S(1)} %copy-done.18, bf16[512,1024]{1,0:T(8,128)(2,1)S(1)} %get-tuple-element.158.refs_2_, ...), custom_call_target="tpu_custom_call" | custom-call | flops 20700000256 | bytes 64800000 | tf_op jit(solution)/shard_map/attend_backward/pallas_call | solution.py:251
  360.4 7.1 %attend_backward.5 = (bf16[512,1024]{1,0:T(8,128)(2,1)}, f32[2,512,1024]{2,1,0:T(8,128)}, bf16[2,512,1024]{2,1,0:T(8,128)(2,1)}) custom-call(bf16[512,1024]{1,0:T(8,128)(2,1)S(1)} %copy-done.1, bf16[512,1024]{1,0:T(8,128)(2,1)S(1)} %copy-done.18, ...), custom_call_target="tpu_custom_call", output_to_operand_aliasing={{0}: (10, {}), {1}: (11, {}), {2}: (12, {})} | custom-call | flops 6899999744 | bytes 21600000 | tf_op jit(solution)/shard_map/attend_backward/pallas_call | solution.py:251
  373.0 10.6 %collective-permute-done.33 = bf16[128,2176]{1,0:T(8,128)(2,1)S(1)} collective-permute-done((bf16[128,2176]{1,0:T(8,128)(2,1)S(1)}, bf16[128,2176]{1,0:T(8,128)(2,1)S(1)}, u32[]{:S(2)}, u32[]{:S(2)}) %collective-permute-start.33) | collective-permute-done | bytes 557088 | tf_op jit(solution)/shard_map/ppermute | solution.py:1025
  387.9 8.6 %target_back.1 = bf16[512,1024]{1,0:T(8,128)(2,1)S(1)} custom-call(s32[16]{0:T(128)S(1)} %copy-done.8, bf16[512,1024]{1,0:T(8,128)(2,1)} %get-tuple-element.166.refs_0_.refs_3_, bf16[2,512,1024]{2,1,0:T(8,128)(2,1)} %add_convert_fusion.2.refs_1_.refs_2_.refs_4_.refs_5_, bf16[2,512,1024]{2,1,0:T(8,128)(2,1)} %add_convert_fusion.2.refs_1_.refs_2_.refs_4_.refs_5_, ...), custom_call_target="tpu_custom_call" | custom-call | flops 10350000128 | bytes 32400000 | tf_op jit(solution)/shard_map/target_back/pallas_call | solution.py:332
  396.5 9.2 %wgrad_self.1 = (bf16[512,3072]{1,0:T(8,128)(2,1)}, bf16[512,3072]{1,0:T(8,128)(2,1)}) custom-call(s32[16]{0:T(128)S(1)} %copy-done.8, bf16[512,1024]{1,0:T(8,128)(2,1)} %bitcast.151, bf16[512,1024]{1,0:T(8,128)(2,1)} %bitcast.152, bf16[512,1024]{1,0:T(8,128)(2,1)} %bitcast.153, bf16[512,1024]{1,0:T(8,128)(2,1)} %get-tuple-element.166.refs_0_.refs_3_, ...), custom_call_target="tpu_custom_call" | custom-call | flops 5520000000 | bytes 17280000 | tf_op jit(solution)/shard_map/wgrad_self/pallas_call | solution.py:332
  417.9 9.1 %collective-permute-done.40 = bf16[2,32,4352]{2,1,0:T(8,128)(2,1)S(1)} collective-permute-done((bf16[2,32,4352]{2,1,0:T(8,128)(2,1)S(1)}, bf16[2,32,4352]{2,1,0:T(8,128)(2,1)S(1)}, u32[]{:S(2)}, u32[]{:S(2)}) %collective-permute-start.40) | collective-permute-done | bytes 557088 | tf_op jit(solution)/shard_map/ppermute | solution.py:1034
  432.3 7.4 %collective-permute-done.31.refs_2_ = bf16[128,1024]{1,0:T(8,128)(2,1)S(1)} collective-permute-done((bf16[128,1024]{1,0:T(8,128)(2,1)S(1)}, bf16[128,1024]{1,0:T(8,128)(2,1)S(1)}, u32[]{:S(2)}, u32[]{:S(2)}) %collective-permute-start.31) | collective-permute-done | bytes 262176 | tf_op jit(solution)/shard_map/ppermute | solution.py:1097
  445.4 6.0 %collective-permute-done.43 = bf16[32,4352]{1,0:T(8,128)(2,1)S(1)} collective-permute-done((bf16[32,4352]{1,0:T(8,128)(2,1)S(1)}, bf16[32,4352]{1,0:T(8,128)(2,1)S(1)}, u32[]{:S(2)}, u32[]{:S(2)}) %collective-permute-start.43) | collective-permute-done | bytes 278560 | tf_op jit(solution)/shard_map/ppermute | solution.py:1039
  451.5 11.0 %collective-permute-done.39 = bf16[2,128,1536]{2,1,0:T(8,128)(2,1)S(1)} collective-permute-done((bf16[2,128,1536]{2,1,0:T(8,128)(2,1)S(1)}, bf16[2,128,1536]{2,1,0:T(8,128)(2,1)S(1)}, u32[]{:S(2)}, u32[]{:S(2)}) %collective-permute-start.39) | collective-permute-done | bytes 786464 | tf_op jit(solution)/shard_map/ppermute | solution.py:1018
  482.6 6.8 %collective-permute-start.45 = (bf16[32,3072]{1,0:T(8,128)(2,1)S(1)}, bf16[32,3072]{1,0:T(8,128)(2,1)S(1)}, u32[]{:S(2)}, u32[]{:S(2)}) collective-permute-start(bf16[32,3072]{1,0:T(8,128)(2,1)S(1)} %dynamic-slice_bitcast_fusion.20), channel_id=1, source_target_pairs={{0,4},{1,5},{2,6},{3,7},{4,0},{5,1},{6,2},{7,3},{8,12},{9,13},{10,... | collective-permute-start | bytes 589832 | tf_op jit(solution)/shard_map/ppermute | solution.py:1039
  (308 shorter events, 180.3 us)
Async XLA Ops:
  13.9 34.8 %collective-permute-start = (bf16[256,5120]{1,0:T(8,128)(2,1)}, bf16[256,5120]{1,0:T(8,128)(2,1)}, u32[]{:S(2)}, u32[]{:S(2)}) collective-permute-start(bf16[256,5120]{1,0:T(8,128)(2,1)} %constant_dynamic-update-slice_fusion.refs_0_.refs_2_.refs_3_), channel_id=1, source_target_pairs={{0,8},{1,17},{2,10},{3,19},{4,12},{5,21},{6,14},{7,23},{8,0},{9,25... | collective-permute-start | bytes 7864328 | tf_op jit(solution)/shard_map/ppermute | solution.py:893
  18.2 30.5 %all-to-all-start = ((bf16[4,128,1024]{2,1,0:T(8,128)(2,1)}), bf16[4,128,1024]{2,1,0:T(8,128)(2,1)S(1)}, u32[]{:S(2)}, u32[]{:S(2)}) async-start(bf16[4,128,1024]{2,1,0:T(8,128)(2,1)} %bitcast.136), calls=%async_computation | async-start | bytes 2097152 | tf_op jit(solution)/shard_map/all_to_all | solution.py:1086
  68.2 26.4 %collective-permute-start.7 = (bf16[256,4096]{1,0:T(8,128)(2,1)}, bf16[256,4096]{1,0:T(8,128)(2,1)}, u32[]{:S(2)}, u32[]{:S(2)}) collective-permute-start(bf16[256,4096]{1,0:T(8,128)(2,1)} %maximum_dynamic-update-slice_fusion.refs_0_.refs_5_.refs_7_.refs_12_.refs_10_.refs_15_.refs_20_), channel_id=1, source_target_pairs={{0,8},{1,17},{2,10},{3,19},{4,12},{5,21},{6,14},{7,23},{8,0},{9,25... | collective-permute-start | bytes 6291464 | tf_op jit(solution)/shard_map/ppermute | solution.py:893
  78.9 39.3 %all-to-all-start.1 = ((bf16[4,128,1024]{2,1,0:T(8,128)(2,1)}), bf16[4,128,1024]{2,1,0:T(8,128)(2,1)}, u32[]{:S(2)}, u32[]{:S(2)}) async-start(bf16[4,128,1024]{2,1,0:T(8,128)(2,1)} %bitcast.135), calls=%async_computation.1 | async-start | bytes 2097152 | tf_op jit(solution)/shard_map/all_to_all | solution.py:1086
  96.9 27.1 %collective-permute-start.10 = (bf16[128,4096]{1,0:T(8,128)(2,1)}, bf16[128,4096]{1,0:T(8,128)(2,1)}, u32[]{:S(2)}, u32[]{:S(2)}) collective-permute-start(bf16[128,4096]{1,0:T(8,128)(2,1)} %constant_dynamic-slice_fusion.2), channel_id=1, source_target_pairs={{0,16},{1,9},{2,18},{3,11},{4,20},{5,13},{6,22},{7,15},{8,24},{9,1... | collective-permute-start | bytes 3145736 | tf_op jit(solution)/shard_map/ppermute | solution.py:904
  97.5 34.9 %collective-permute-start.9 = (bf16[256,4096]{1,0:T(8,128)(2,1)}, bf16[256,4096]{1,0:T(8,128)(2,1)}, u32[]{:S(2)}, u32[]{:S(2)}) collective-permute-start(bf16[256,4096]{1,0:T(8,128)(2,1)} %collective-permute-done.7.refs_1_.refs_6_.refs_8_.refs_13_.refs_11_.refs_16_.refs_21_), channel_id=1, source_target_pairs={{0,1},{1,0},{2,3},{3,2},{4,5},{5,4},{6,7},{7,6},{8,9},{9,8},{10,11... | collective-permute-start | bytes 6291464 | tf_op jit(solution)/shard_map/ppermute | solution.py:897
  97.8 44.0 %collective-permute-start.12 = (bf16[256,4096]{1,0:T(8,128)(2,1)}, bf16[256,4096]{1,0:T(8,128)(2,1)}, u32[]{:S(2)}, u32[]{:S(2)}) collective-permute-start(bf16[256,4096]{1,0:T(8,128)(2,1)} %refs_0_.2), channel_id=1, source_target_pairs={{0,8},{1,17},{2,10},{3,19},{4,12},{5,21},{6,14},{7,23},{8,0},{9,25... | collective-permute-start | bytes 6291464 | tf_op jit(solution)/shard_map/ppermute | solution.py:893
  125.9 47.0 %all-to-all-start.2 = ((bf16[4,128,1024]{2,1,0:T(8,128)(2,1)}), bf16[4,128,1024]{2,1,0:T(8,128)(2,1)}, u32[]{:S(2)}, u32[]{:S(2)}) async-start(bf16[4,128,1024]{2,1,0:T(8,128)(2,1)} %bitcast.154), calls=%async_computation.2 | async-start | bytes 2097152 | tf_op jit(solution)/shard_map/all_to_all | solution.py:1086
  130.7 184.8 %reduce-scatter.3.cloned.1.call-start = ((), (), s32[]{:S(2)}) async-start(), calls=%async_computation.5 | async-start | bytes 4718592 | tf_op jit(solution)/shard_map/reduce_scatter | solution.py:998
  131.1 37.3 %collective-permute-start.17 = (bf16[1024,1024]{1,0:T(8,128)(2,1)}, bf16[1024,1024]{1,0:T(8,128)(2,1)}, u32[]{:S(2)}, u32[]{:S(2)}) collective-permute-start(bf16[1024,1024]{1,0:T(8,128)(2,1)} %refs_5_.1), channel_id=1, source_target_pairs={{0,8},{1,17},{2,10},{3,19},{4,12},{5,21},{6,14},{7,23},{8,0},{9,25... | collective-permute-start | bytes 6291464 | tf_op jit(solution)/shard_map/ppermute | solution.py:893
  141.8 44.0 %collective-permute-start.14 = (bf16[256,4096]{1,0:T(8,128)(2,1)}, bf16[256,4096]{1,0:T(8,128)(2,1)}, u32[]{:S(2)}, u32[]{:S(2)}) collective-permute-start(bf16[256,4096]{1,0:T(8,128)(2,1)} %collective-permute-done.12.refs_1_), channel_id=1, source_target_pairs={{0,1},{1,0},{2,3},{3,2},{4,5},{5,4},{6,7},{7,6},{8,9},{9,8},{10,11... | collective-permute-start | bytes 6291464 | tf_op jit(solution)/shard_map/ppermute | solution.py:897
  143.5 28.9 %collective-permute-start.15 = (bf16[128,4096]{1,0:T(8,128)(2,1)S(1)}, bf16[128,4096]{1,0:T(8,128)(2,1)}, u32[]{:S(2)}, u32[]{:S(2)}) collective-permute-start(bf16[128,4096]{1,0:T(8,128)(2,1)S(1)} %constant_dynamic-slice_fusion.1), channel_id=1, source_target_pairs={{0,16},{1,9},{2,18},{3,11},{4,20},{5,13},{6,22},{7,15},{8,24},{9,1... | collective-permute-start | bytes 3145736 | tf_op jit(solution)/shard_map/ppermute | solution.py:904
  172.4 30.1 %collective-permute-start.18 = (bf16[1024,1024]{1,0:T(8,128)(2,1)}, bf16[1024,1024]{1,0:T(8,128)(2,1)}, u32[]{:S(2)}, u32[]{:S(2)}) collective-permute-start(bf16[1024,1024]{1,0:T(8,128)(2,1)} %collective-permute-done.17.refs_6_), channel_id=1, source_target_pairs={{0,1},{1,0},{2,3},{3,2},{4,5},{5,4},{6,7},{7,6},{8,9},{9,8},{10,11... | collective-permute-start | bytes 6291464 | tf_op jit(solution)/shard_map/ppermute | solution.py:897
  221.8 33.7 %collective-permute-start.21 = (bf16[128,1024]{1,0:T(8,128)(2,1)S(1)}, bf16[128,1024]{1,0:T(8,128)(2,1)S(1)}, u32[]{:S(2)}, u32[]{:S(2)}) collective-permute-start(bf16[128,1024]{1,0:T(8,128)(2,1)S(1)} %get-tuple-element.275), channel_id=1, source_target_pairs={{0,2},{1,3},{2,0},{3,1},{4,6},{5,7},{6,4},{7,5},{8,10},{9,11},{10,... | collective-permute-start | bytes 786440 | tf_op jit(solution)/shard_map/ppermute | solution.py:1097
  223.8 31.6 %collective-permute-start.22 = (bf16[128,1024]{1,0:T(8,128)(2,1)S(1)}, bf16[128,1024]{1,0:T(8,128)(2,1)S(1)}, u32[]{:S(2)}, u32[]{:S(2)}) collective-permute-start(bf16[128,1024]{1,0:T(8,128)(2,1)S(1)} %get-tuple-element.274), channel_id=1, source_target_pairs={{0,4},{1,5},{2,6},{3,7},{4,0},{5,1},{6,2},{7,3},{8,12},{9,13},{10,... | collective-permute-start | bytes 786440 | tf_op jit(solution)/shard_map/ppermute | solution.py:1097
  226.2 29.3 %collective-permute-start.23 = (bf16[128,1024]{1,0:T(8,128)(2,1)S(1)}, bf16[128,1024]{1,0:T(8,128)(2,1)S(1)}, u32[]{:S(2)}, u32[]{:S(2)}) collective-permute-start(bf16[128,1024]{1,0:T(8,128)(2,1)S(1)} %get-tuple-element.273), channel_id=1, source_target_pairs={{0,6},{1,7},{2,4},{3,5},{4,2},{5,3},{6,0},{7,1},{8,14},{9,15},{10,... | collective-permute-start | bytes 786440 | tf_op jit(solution)/shard_map/ppermute | solution.py:1097
  264.6 145.9 %reduce-scatter.5.cloned.1.call-start = ((), (), s32[]{:S(2)}) async-start(), calls=%async_computation.6 | async-start | bytes 655360 | tf_op jit(solution)/shard_map/reduce_scatter | solution.py:998
  327.5 32.8 %collective-permute-start.26 = (bf16[128,1024]{1,0:T(8,128)(2,1)S(1)}, bf16[128,1024]{1,0:T(8,128)(2,1)S(1)}, u32[]{:S(2)}, u32[]{:S(2)}) collective-permute-start(bf16[128,1024]{1,0:T(8,128)(2,1)S(1)} %get-tuple-element.269), channel_id=1, source_target_pairs={{0,2},{1,3},{2,0},{3,1},{4,6},{5,7},{6,4},{7,5},{8,10},{9,11},{10,... | collective-permute-start | bytes 786440 | tf_op jit(solution)/shard_map/ppermute | solution.py:1097
  327.7 32.6 %collective-permute-start.27 = (bf16[128,1024]{1,0:T(8,128)(2,1)S(1)}, bf16[128,1024]{1,0:T(8,128)(2,1)S(1)}, u32[]{:S(2)}, u32[]{:S(2)}) collective-permute-start(bf16[128,1024]{1,0:T(8,128)(2,1)S(1)} %get-tuple-element.268), channel_id=1, source_target_pairs={{0,4},{1,5},{2,6},{3,7},{4,0},{5,1},{6,2},{7,3},{8,12},{9,13},{10,... | collective-permute-start | bytes 786440 | tf_op jit(solution)/shard_map/ppermute | solution.py:1097
  331.0 80.3 %collective-permute-start.36 = (bf16[128,1024]{1,0:T(8,128)(2,1)}, bf16[128,1024]{1,0:T(8,128)(2,1)}, u32[]{:S(2)}, u32[]{:S(2)}) collective-permute-start(bf16[128,1024]{1,0:T(8,128)(2,1)} %get-tuple-element.267), channel_id=1, source_target_pairs={{0,6},{1,7},{2,4},{3,5},{4,2},{5,3},{6,0},{7,1},{8,14},{9,15},{10,... | collective-permute-start | bytes 786440 | tf_op jit(solution)/shard_map/ppermute | solution.py:1097
  339.8 29.5 %collective-permute-start.32 = (bf16[2,128,2176]{2,1,0:T(8,128)(2,1)S(1)}, bf16[2,128,2176]{2,1,0:T(8,128)(2,1)S(1)}, u32[]{:S(2)}, u32[]{:S(2)}) collective-permute-start(bf16[2,128,2176]{2,1,0:T(8,128)(2,1)S(1)} %dynamic-slice_bitcast_fusion.1), channel_id=1, source_target_pairs={{0,8},{8,0},{16,24},{24,16},{1,9},{9,1},{17,25},{25,17},{2,10},{10... | collective-permute-start | bytes 3342344 | tf_op jit(solution)/shard_map/ppermute | solution.py:1017
  341.5 29.6 %collective-permute-start.34 = (bf16[2,128,2176]{2,1,0:T(8,128)(2,1)S(1)}, bf16[2,128,2176]{2,1,0:T(8,128)(2,1)S(1)}, u32[]{:S(2)}, u32[]{:S(2)}) collective-permute-start(bf16[2,128,2176]{2,1,0:T(8,128)(2,1)S(1)} %dynamic-slice_bitcast_fusion), channel_id=1, source_target_pairs={{0,16},{8,24},{16,0},{24,8},{1,17},{9,25},{17,1},{25,9},{2,18},{10... | collective-permute-start | bytes 3342344 | tf_op jit(solution)/shard_map/ppermute | solution.py:1018
  405.7 34.1 %collective-permute-start.37 = (bf16[512,3072]{1,0:T(8,128)(2,1)}, bf16[512,3072]{1,0:T(8,128)(2,1)}, u32[]{:S(2)}, u32[]{:S(2)}) collective-permute-start(bf16[512,3072]{1,0:T(8,128)(2,1)} %get-tuple-element.168), channel_id=1, source_target_pairs={{0,1},{1,0},{2,3},{3,2},{4,5},{5,4},{6,7},{7,6},{8,9},{9,8},{10,11... | collective-permute-start | bytes 9437192 | tf_op jit(solution)/shard_map/ppermute | solution.py:1010
  414.5 25.3 %collective-permute-start.31 = (bf16[128,1024]{1,0:T(8,128)(2,1)S(1)}, bf16[128,1024]{1,0:T(8,128)(2,1)S(1)}, u32[]{:S(2)}, u32[]{:S(2)}) collective-permute-start(bf16[128,1024]{1,0:T(8,128)(2,1)S(1)} %get-tuple-element.270), channel_id=1, source_target_pairs={{0,6},{1,7},{2,4},{3,5},{4,2},{5,3},{6,0},{7,1},{8,14},{9,15},{10,... | collective-permute-start | bytes 786440 | tf_op jit(solution)/shard_map/ppermute | solution.py:1097
  (88 other events, 1079.6 us)
Sparse Core Ops, SparseCore 0:
  264.7 50.6 reduce-scatter.2
  332.1 26.7 reduce-scatter.4

commit v6 on v5

--- a/solution.py
+++ b/solution.py
@@ -1018,7 +1018,7 @@
         from_y = lax.ppermute(take(self.two, 1 - y, 0), "dp", swap_pairs(4, 2))
         self.one = add(take(self.one, x, 1), from_x)
         self.two = add(take(self.two, y, 0), from_y)
-        return self.one
+        return self.one, self.two
 
     def plane_two(self):
         x, y = self.x, self.y
@@ -1314,7 +1314,7 @@
         d_mixed = after(d_mixed, grad_source[0])
 
     begun = ()
-    split = pairs * 3 // 4
+    split = pairs * 7 // 8
     for span in ((0, split), (split, pairs - split)):
         begun = attend_backward(
             queries,
@@ -1330,7 +1330,7 @@
             begun,
         )
         if halving and span[0] == 0:
-            d_mixed = after(d_mixed, begun[0], *grad_source[1:3])
+            d_mixed = after(d_mixed, begun[0], inner_sums.plane_one(), *grad_source[1:3])
     d_q, *d_kv = begun
     d_kv = collect(d_kv[0], d_kv[1:])
     at_self = at_q if halving else ((jnp.concatenate([at_q[0][0], at_kv[0][0]], axis=1),), 0)
@@ -1349,7 +1349,9 @@
         grad_source = set_down(grad_source)
         grad_target = set_down(grad_target)
     if halving:
-        d_q = after(d_q, inner_sums.plane_one())
+        inner_sums.one, inner_sums.two, _ = lax.optimization_barrier(
+            (inner_sums.one, inner_sums.two, grad_target[0])
+        )
         late = Scatter(
             *wgrad(
                 place,

time: 508 us -> 506 us (level)
    ppermute x2, waiting for transfers between devices: 16.5 us -> 7.82 us  [plane_two(): from_y = lax.ppermute(take(self.one, 1 - y, 0), 'dp', swap_pairs(4, 2))]
    ppermute x9, waiting for transfers between devices: 11.1 us -> 19.3 us  [send_back(): parts.append(lax.ppermute(take(item, which ^ bit, 0), 'seq', pairs))]
    ppermute x2, waiting for transfers between devices: 11.3 us -> 5.06 us  [z_one(): lax.ppermute(take(self.item, 1 - self.low, 1), 'seq', swap_pairs(8, 2))]
    unnamed x136 -> x132, local copies, waits for them, and re-layouts: 29.3 us -> 29.2 us
  transfers between devices with their start and end apart: 51 -> 51, of which waited for: 22 -> 24; matrix products, arithmetic and copies ran while one was open for 9% -> 9% of each run, Pallas kernels for 42% -> 41%
where the time goes in v6:
time: 506 us; the launch traced here: 499 us
  Pallas kernels  244 us (48%)
  waiting for transfers between devices  110 us (22%)
  starting transfers between devices  62.4 us (12%)
  local copies, waits for them, and re-layouts  47.3 us (9%)
  other arithmetic  20.3 us (4%)
  between operations  15.4 us (3%)
    pallas_call x17, Pallas kernels, run(): pl.pallas_call(kernel, grid_spec=pltpu.PrefetchScalarGridSpec(num_scalar_...  152 us
    pallas_call x3, Pallas kernels, attend_backward(): pl.pallas_call(functools.partial(backward_kernel, pieces, block, causal,...  51.2 us
    pallas_call x2, Pallas kernels, attend_forward(): pl.pallas_call(functools.partial(forward_kernel, pieces, block, causal),...  40.7 us
    unnamed x132, local copies, waits for them, and re-layouts  29.2 us
    ppermute x4, waiting for transfers between devices, gather_near(): return parts + (lax.ppermute(half_one, ('dp', 'seq'), by_core(2, 1)),)  22.4 us
    ppermute x9, waiting for transfers between devices, send_back(): parts.append(lax.ppermute(take(item, which ^ bit, 0), 'seq', pairs))  19.3 us
    ppermute x3, waiting for transfers between devices, body(): lax.ppermute(vectors, 'dp', swap_pairs(4, bit))  19 us
    ppermute x9, starting transfers between devices, send_back(): parts.append(lax.ppermute(take(item, which ^ bit, 0), 'seq', pairs))  16.7 us
  transfers between devices with their start and end apart: 51, of which 24 were waited for; matrix products, arithmetic and copies ran while one was open for 9% of the time, Pallas kernels for 41%

profile of v6, /device:TPU:0, one launch (start us, length us, event | category | flops | bytes accessed | tf_op | source)
XLA Modules:
  0.0 499.1 jit_solution(2194256084519250713)
XLA Ops:
  29.4 17.5 %collective-permute-done.2 = bf16[6,256]{1,0:T(8,128)(2,1)S(1)} collective-permute-done((bf16[6,256]{1,0:T(8,128)(2,1)S(1)}, bf16[6,256]{1,0:T(8,128)(2,1)S(1)}, u32[]{:S(2)}, u32[]{:S(2)}) %collective-permute-start.2) | collective-permute-done | bytes 3104 | tf_op jit(solution)/shard_map/ppermute | solution.py:1139
  49.4 17.1 %collective-permute-done.5.refs_3_.refs_5_.refs_6_ = bf16[128,5120]{1,0:T(8,128)(2,1)} collective-permute-done((bf16[128,5120]{1,0:T(8,128)(2,1)S(1)}, bf16[128,5120]{1,0:T(8,128)(2,1)}, u32[]{:S(2)}, u32[]{:S(2)}) %collective-permute-start.5) | collective-permute-done | bytes 1310752 | tf_op jit(solution)/shard_map/ppermute | solution.py:904
  69.9 5.9 %self_kv.1.refs_3_.refs_5_.refs_6_.refs_8_ = bf16[512,2048]{1,0:T(8,128)(2,1)S(1)} custom-call(s32[16]{0:T(128)S(1)} %stack.123.place, bf16[512,1024]{1,0:T(8,128)(2,1)} %bitcast.18.left_ref.resid_ref.refs_0_.refs_1_.refs_2_, bf16[256,5120]{1,0:T(8,128)(2,1)} %constant_dynamic-update-slice_fusion.refs_0_.refs_2_.refs_3_, bf16[256,5120]{1,0:T(8,128)(2,1)} %copy-done.25, ...), custom_call_target="tpu_custom_call" | custom-call | flops 5750000128 | bytes 18000000 | tf_op jit(solution)/shard_map/self_kv/pallas_call | solution.py:332
  97.3 18.2 %attend_forward.2 = (bf16[512,1024]{1,0:T(8,128)(2,1)S(1)}, f32[8,2,512]{2,1,0:T(2,128)S(1)}) custom-call(bf16[512,1024]{1,0:T(8,128)(2,1)S(1)} %self_q.1.refs_0_, s32[2,512,1]{2,1,0:T(8,128)S(1)} %get-tuple-element.283.refs_1_.refs_4_, s32[1,512]{1,0:T(1,128)S(1)} %multiply_add_fusion.refs_2_.refs_5_, ...), custom_call_target="tpu_custom_call" | custom-call | flops 20700000256 | bytes 64800000 | tf_op jit(solution)/shard_map/attend_forward/pallas_call | solution.py:161
  116.6 6.8 %cross_kv.1.refs_3_.refs_5_.refs_6_.refs_8_ = bf16[512,2048]{1,0:T(8,128)(2,1)} custom-call(s32[16]{0:T(128)S(1)} %stack.123.place, bf16[512,1024]{1,0:T(8,128)(2,1)} %bitcast.23.left_ref.refs_0_.refs_1_, bf16[256,5120]{1,0:T(8,128)(2,1)} %constant_dynamic-update-slice_fusion.refs_0_.refs_2_.refs_3_, bf16[256,5120]{1,0:T(8,128)(2,1)} %copy-done.25, ...), custom_call_target="tpu_custom_call" | custom-call | flops 5750000128 | bytes 18000000 | tf_op jit(solution)/shard_map/cross_kv/pallas_call | solution.py:332
  131.9 9.5 %mix_self.1 = (f32[512,1024]{1,0:T(8,128)}, f32[512,1024]{1,0:T(8,128)}, bf16[512,1024]{1,0:T(8,128)(2,1)}, bf16[512,1024]{1,0:T(8,128)(2,1)S(1)}) custom-call(s32[16]{0:T(128)S(1)} %stack.123.place, bf16[512,1024]{1,0:T(8,128)(2,1)} %copy-done.4, bf16[512,1024]{1,0:T(8,128)(2,1)} %bitcast.18.left_ref.resid_ref.refs_0_.refs_1_.refs_2_, ...), custom_call_target="tpu_custom_call" | custom-call | flops 7245000192 | bytes 22680000 | tf_op jit(solution)/shard_map/mix_self/pallas_call | solution.py:332
  143.8 22.4 %attend_forward.3 = (bf16[512,1024]{1,0:T(8,128)(2,1)S(1)}, f32[8,2,512]{2,1,0:T(2,128)S(1)}) custom-call(bf16[512,1024]{1,0:T(8,128)(2,1)S(1)} %get-tuple-element.111.refs_0_, s32[2,512,1]{2,1,0:T(8,128)S(1)} %get-tuple-element.282.refs_1_.refs_4_, s32[1,512]{1,0:T(1,128)S(1)} %broadcast_in_dim.12.refs_2_.refs_5_, ...), custom_call_target="tpu_custom_call" | custom-call | flops 25300000768 | bytes 79200000 | tf_op jit(solution)/shard_map/attend_forward/pallas_call | solution.py:161
  172.4 7.5 %mix_cross.1 = (f32[512,1024]{1,0:T(8,128)}, f32[512,1024]{1,0:T(8,128)}, bf16[512,1024]{1,0:T(8,128)(2,1)}) custom-call(s32[16]{0:T(128)S(1)} %stack.123.place, bf16[512,1024]{1,0:T(8,128)(2,1)} %copy-done.13, f32[512,1024]{1,0:T(8,128)} %get-tuple-element.114.resid_ref, f32[2,1024]{1,0:T(2,128)S(1)} %get-tuple-element.292.norm_ref, ...), custom_call_target="tpu_custom_call" | custom-call | flops 4600000000 | bytes 14400000 | tf_op jit(solution)/shard_map/mix_cross/pallas_call | solution.py:332
  179.9 5.3 %collective-permute-done.19.refs_6_.refs_8_ = bf16[512,1024]{1,0:T(8,128)(2,1)} collective-permute-done((bf16[512,1024]{1,0:T(8,128)(2,1)}, bf16[512,1024]{1,0:T(8,128)(2,1)}, u32[]{:S(2)}, u32[]{:S(2)}) %collective-permute-start.19) | collective-permute-done | bytes 1048608 | tf_op jit(solution)/shard_map/ppermute | solution.py:904
  185.2 15.5 %feed_first.1 = (f32[512,1024]{1,0:T(8,128)S(1)}, bf16[512,2048]{1,0:T(8,128)(2,1)}, bf16[512,512]{1,0:T(8,128)(2,1)}, bf16[512,512]{1,0:T(8,128)(2,1)}) custom-call(s32[16]{0:T(128)S(1)} %stack.123.place, bf16[512,1024]{1,0:T(8,128)(2,1)} %get-tuple-element.115.low_ref.refs_2_, f32[512,1024]{1,0:T(8,128)} %get-tuple-element.116.second_ref, ...), custom_call_target="tpu_custom_call" | custom-call | flops 14949999616 | bytes 46800000 | tf_op jit(solution)/shard_map/feed_first/pallas_call | solution.py:332
  203.0 15.1 %feed_second.1 = (bf16[512,1024]{1,0:T(8,128)(2,1)}, f32[512,1024]{1,0:T(8,128)S(1)}, bf16[512,1024]{1,0:T(8,128)(2,1)S(1)}, f32[2,1024]{1,0:T(2,128)}, bf16[512,2048]{1,0:T(8,128)(2,1)}) custom-call(s32[16]{0:T(128)S(1)} %stack.123.place, bf16[512,1024]{1,0:T(8,128)(2,1)} %get-tuple-element.115.low_ref.refs_2_, f32[512,1024]{1,0:T(8,128)} %copy-done.19, ...), custom_call_target="tpu_custom_call" | custom-call | flops 15525000192 | bytes 48600000 | tf_op jit(solution)/shard_map/feed_second/pallas_call | solution.py:332
  225.5 29.2 %feed_backward.1 = (f32[512,1024]{1,0:T(8,128)}, bf16[512,1024]{1,0:T(8,128)(2,1)}, f32[2,1024]{1,0:T(2,128)}, bf16[512,512]{1,0:T(8,128)(2,1)}, bf16[512,1024]{1,0:T(8,128)(2,1)}) custom-call(s32[16]{0:T(128)} %copy-done.11, bf16[512,1024]{1,0:T(8,128)(2,1)} %copy-done.15, f32[512,1024]{1,0:T(8,128)} %copy-done.20, ...), custom_call_target="tpu_custom_call" | custom-call | flops 33350000640 | bytes 104400000 | tf_op jit(solution)/shard_map/feed_backward/pallas_call | solution.py:332
  256.1 7.8 %wgrad_early.1 = bf16[1024,2048]{1,0:T(8,128)(2,1)} custom-call(s32[16]{0:T(128)S(1)} %copy-done.12, bf16[512,1024]{1,0:T(8,128)(2,1)} %copy-done.13, bf16[512,1024]{1,0:T(8,128)(2,1)} %copy-done.13, bf16[512,1024]{1,0:T(8,128)(2,1)} %get-tuple-element.115.low_ref.refs_2_, bf16[512,512]{1,0:T(8,128)(2,1)} %get-tuple-element.130.refs_3_, ...), custom_call_target="tpu_custom_call" | custom-call | flops 3680000000 | bytes 11520000 | tf_op jit(solution)/shard_map/wgrad_early/pallas_call | solution.py:332
  267.6 26.9 %attend_backward.3 = (bf16[512,1024]{1,0:T(8,128)(2,1)}, f32[2,512,1024]{2,1,0:T(8,128)}, bf16[2,512,1024]{2,1,0:T(8,128)(2,1)}) custom-call(bf16[512,1024]{1,0:T(8,128)(2,1)S(1)} %copy-done.18, bf16[512,1024]{1,0:T(8,128)(2,1)S(1)} %copy-done.14, bf16[512,1024]{1,0:T(8,128)(2,1)S(1)} %copy-done.22, f32[8,2,512]{2,1,0:T(2,128)S(1)} %get-tuple-element.135.refs_3_, ...), custom_call_target="tpu_custom_call" | custom-call | flops 32199999488 | bytes 100800000 | tf_op jit(solution)/shard_map/attend_backward/pallas_call | solution.py:251
  294.5 10.1 %norm_step.1 = (f32[512,1024]{1,0:T(8,128)}, bf16[512,1024]{1,0:T(8,128)(2,1)S(1)}, f32[2,1024]{1,0:T(2,128)}, bf16[512,1024]{1,0:T(8,128)(2,1)S(1)}) custom-call(s32[16]{0:T(128)S(1)} %copy-done.12, bf16[512,1024]{1,0:T(8,128)(2,1)} %get-tuple-element.136.dquery_ref.refs_7_, f32[512,1024]{1,0:T(8,128)} %get-tuple-element.141.d_ref, ...), custom_call_target="tpu_custom_call" | custom-call | flops 7590000128 | bytes 23760000 | tf_op jit(solution)/shard_map/norm_step/pallas_call | solution.py:332
  306.8 6.2 %source_back.1 = bf16[512,1024]{1,0:T(8,128)(2,1)S(1)} custom-call(s32[16]{0:T(128)S(1)} %copy-done.12, bf16[2,512,1024]{2,1,0:T(8,128)(2,1)} %add_convert_fusion.3.refs_0_.refs_1_.refs_4_.refs_5_, bf16[2,512,1024]{2,1,0:T(8,128)(2,1)} %add_convert_fusion.3.refs_0_.refs_1_.refs_4_.refs_5_, ...), custom_call_target="tpu_custom_call" | custom-call | flops 6899999744 | bytes 21600000 | tf_op jit(solution)/shard_map/source_back/pallas_call | solution.py:332
  314.8 11.4 %wgrad_inner.1 = (bf16[512,4352]{1,0:T(8,128)(2,1)}, bf16[512,4352]{1,0:T(8,128)(2,1)}) custom-call(s32[16]{0:T(128)S(1)} %copy-done.12, bf16[512,1024]{1,0:T(8,128)(2,1)} %bitcast.23.left_ref.refs_0_.refs_1_, bf16[512,1024]{1,0:T(8,128)(2,1)} %bitcast.23.left_ref.refs_0_.refs_1_, bf16[512,1024]{1,0:T(8,128)(2,1)} %copy-done.4, ...), custom_call_target="tpu_custom_call" | custom-call | flops 7360000000 | bytes 23040000 | tf_op jit(solution)/shard_map/wgrad_inner/pallas_call | solution.py:332
  342.6 20.1 %attend_backward.4 = (bf16[512,1024]{1,0:T(8,128)(2,1)}, f32[2,512,1024]{2,1,0:T(8,128)}, bf16[2,512,1024]{2,1,0:T(8,128)(2,1)}) custom-call(bf16[512,1024]{1,0:T(8,128)(2,1)S(1)} %copy-done.1, bf16[512,1024]{1,0:T(8,128)(2,1)S(1)} %copy-done.5, bf16[512,1024]{1,0:T(8,128)(2,1)S(1)} %get-tuple-element.159.refs_2_, ...), custom_call_target="tpu_custom_call" | custom-call | flops 24149999616 | bytes 75600000 | tf_op jit(solution)/shard_map/attend_backward/pallas_call | solution.py:251
  381.8 8.8 %target_back.1 = bf16[512,1024]{1,0:T(8,128)(2,1)S(1)} custom-call(s32[16]{0:T(128)S(1)} %copy-done.12, bf16[512,1024]{1,0:T(8,128)(2,1)} %get-tuple-element.166.refs_0_.refs_3_, bf16[2,512,1024]{2,1,0:T(8,128)(2,1)} %add_convert_fusion.2.refs_1_.refs_2_.refs_4_.refs_5_, bf16[2,512,1024]{2,1,0:T(8,128)(2,1)} %add_convert_fusion.2.refs_1_.refs_2_.refs_4_.refs_5_, ...), custom_call_target="tpu_custom_call" | custom-call | flops 10350000128 | bytes 32400000 | tf_op jit(solution)/shard_map/target_back/pallas_call | solution.py:332
  393.8 9.1 %wgrad_self.1 = (bf16[512,3072]{1,0:T(8,128)(2,1)}, bf16[512,3072]{1,0:T(8,128)(2,1)}) custom-call(s32[16]{0:T(128)S(1)} %copy-done.12, bf16[512,1024]{1,0:T(8,128)(2,1)} %bitcast.18.left_ref.resid_ref.refs_0_.refs_1_.refs_2_, bf16[512,1024]{1,0:T(8,128)(2,1)} %bitcast.18.left_ref.resid_ref.refs_0_.refs_1_.refs_2_, ...), custom_call_target="tpu_custom_call" | custom-call | flops 5520000000 | bytes 17280000 | tf_op jit(solution)/shard_map/wgrad_self/pallas_call | solution.py:332
  421.3 12.0 %collective-permute-done.31.refs_0_ = bf16[128,1024]{1,0:T(8,128)(2,1)S(1)} collective-permute-done((bf16[128,1024]{1,0:T(8,128)(2,1)}, bf16[128,1024]{1,0:T(8,128)(2,1)S(1)}, u32[]{:S(2)}, u32[]{:S(2)}) %collective-permute-start.31) | collective-permute-done | bytes 262176 | tf_op jit(solution)/shard_map/ppermute | solution.py:1097
  433.7 6.9 %collective-permute-done.33.refs_2_ = bf16[128,1024]{1,0:T(8,128)(2,1)S(1)} collective-permute-done((bf16[128,1024]{1,0:T(8,128)(2,1)}, bf16[128,1024]{1,0:T(8,128)(2,1)S(1)}, u32[]{:S(2)}, u32[]{:S(2)}) %collective-permute-start.33) | collective-permute-done | bytes 262176 | tf_op jit(solution)/shard_map/ppermute | solution.py:1097
  452.7 10.4 %collective-permute-done.39 = bf16[2,128,1536]{2,1,0:T(8,128)(2,1)S(1)} collective-permute-done((bf16[2,128,1536]{2,1,0:T(8,128)(2,1)S(1)}, bf16[2,128,1536]{2,1,0:T(8,128)(2,1)S(1)}, u32[]{:S(2)}, u32[]{:S(2)}) %collective-permute-start.39) | collective-permute-done | bytes 786464 | tf_op jit(solution)/shard_map/ppermute | solution.py:1018
  478.3 5.1 %collective-permute-done.44 = bf16[2,32,3072]{2,1,0:T(8,128)(2,1)S(1)} collective-permute-done((bf16[2,32,3072]{2,1,0:T(8,128)(2,1)S(1)}, bf16[2,32,3072]{2,1,0:T(8,128)(2,1)S(1)}, u32[]{:S(2)}, u32[]{:S(2)}) %collective-permute-start.44) | collective-permute-done | bytes 393248 | tf_op jit(solution)/shard_map/ppermute | solution.py:1034
  (304 shorter events, 179.2 us)
Async XLA Ops:
  13.9 34.7 %collective-permute-start = (bf16[256,5120]{1,0:T(8,128)(2,1)}, bf16[256,5120]{1,0:T(8,128)(2,1)S(1)}, u32[]{:S(2)}, u32[]{:S(2)}) collective-permute-start(bf16[256,5120]{1,0:T(8,128)(2,1)} %constant_dynamic-update-slice_fusion.refs_0_.refs_2_.refs_3_), channel_id=1, source_target_pairs={{0,8},{1,17},{2,10},{3,19},{4,12},{5,21},{6,14},{7,23},{8,0},{9,25... | collective-permute-start | bytes 7864328 | tf_op jit(solution)/shard_map/ppermute | solution.py:893
  18.2 30.4 %all-to-all-start = ((bf16[4,128,1024]{2,1,0:T(8,128)(2,1)}), bf16[4,128,1024]{2,1,0:T(8,128)(2,1)}, u32[]{:S(2)}, u32[]{:S(2)}) async-start(bf16[4,128,1024]{2,1,0:T(8,128)(2,1)} %bitcast.149), calls=%async_computation | async-start | bytes 2097152 | tf_op jit(solution)/shard_map/all_to_all | solution.py:1086
  66.6 26.4 %collective-permute-start.7 = (bf16[256,4096]{1,0:T(8,128)(2,1)}, bf16[256,4096]{1,0:T(8,128)(2,1)}, u32[]{:S(2)}, u32[]{:S(2)}) collective-permute-start(bf16[256,4096]{1,0:T(8,128)(2,1)} %copy-done.41), channel_id=1, source_target_pairs={{0,8},{1,17},{2,10},{3,19},{4,12},{5,21},{6,14},{7,23},{8,0},{9,25... | collective-permute-start | bytes 6291464 | tf_op jit(solution)/shard_map/ppermute | solution.py:893
  77.2 39.3 %all-to-all-start.1 = ((bf16[4,128,1024]{2,1,0:T(8,128)(2,1)}), bf16[4,128,1024]{2,1,0:T(8,128)(2,1)}, u32[]{:S(2)}, u32[]{:S(2)}) async-start(bf16[4,128,1024]{2,1,0:T(8,128)(2,1)} %bitcast.135), calls=%async_computation.1 | async-start | bytes 2097152 | tf_op jit(solution)/shard_map/all_to_all | solution.py:1086
  95.3 28.0 %collective-permute-start.10 = (bf16[128,4096]{1,0:T(8,128)(2,1)}, bf16[128,4096]{1,0:T(8,128)(2,1)}, u32[]{:S(2)}, u32[]{:S(2)}) collective-permute-start(bf16[128,4096]{1,0:T(8,128)(2,1)} %constant_dynamic-slice_fusion.2), channel_id=1, source_target_pairs={{0,16},{1,9},{2,18},{3,11},{4,20},{5,13},{6,22},{7,15},{8,24},{9,1... | collective-permute-start | bytes 3145736 | tf_op jit(solution)/shard_map/ppermute | solution.py:904
  95.8 36.0 %collective-permute-start.9 = (bf16[256,4096]{1,0:T(8,128)(2,1)}, bf16[256,4096]{1,0:T(8,128)(2,1)}, u32[]{:S(2)}, u32[]{:S(2)}) collective-permute-start(bf16[256,4096]{1,0:T(8,128)(2,1)} %collective-permute-done.7.refs_1_.refs_6_.refs_8_.refs_13_.refs_11_.refs_16_.refs_21_), channel_id=1, source_target_pairs={{0,1},{1,0},{2,3},{3,2},{4,5},{5,4},{6,7},{7,6},{8,9},{9,8},{10,11... | collective-permute-start | bytes 6291464 | tf_op jit(solution)/shard_map/ppermute | solution.py:897
  96.2 45.2 %collective-permute-start.12 = (bf16[256,4096]{1,0:T(8,128)(2,1)}, bf16[256,4096]{1,0:T(8,128)(2,1)}, u32[]{:S(2)}, u32[]{:S(2)}) collective-permute-start(bf16[256,4096]{1,0:T(8,128)(2,1)} %refs_0_.2), channel_id=1, source_target_pairs={{0,8},{1,17},{2,10},{3,19},{4,12},{5,21},{6,14},{7,23},{8,0},{9,25... | collective-permute-start | bytes 6291464 | tf_op jit(solution)/shard_map/ppermute | solution.py:893
  125.2 47.2 %all-to-all-start.2 = ((bf16[4,128,1024]{2,1,0:T(8,128)(2,1)}), bf16[4,128,1024]{2,1,0:T(8,128)(2,1)}, u32[]{:S(2)}, u32[]{:S(2)}) async-start(bf16[4,128,1024]{2,1,0:T(8,128)(2,1)} %bitcast.148), calls=%async_computation.2 | async-start | bytes 2097152 | tf_op jit(solution)/shard_map/all_to_all | solution.py:1086
  129.9 185.0 %reduce-scatter.3.cloned.1.call-start = ((), (), s32[]{:S(2)}) async-start(), calls=%async_computation.5 | async-start | bytes 4718592 | tf_op jit(solution)/shard_map/reduce_scatter | solution.py:998
  130.5 37.3 %collective-permute-start.17 = (bf16[1024,1024]{1,0:T(8,128)(2,1)}, bf16[1024,1024]{1,0:T(8,128)(2,1)}, u32[]{:S(2)}, u32[]{:S(2)}) collective-permute-start(bf16[1024,1024]{1,0:T(8,128)(2,1)} %refs_5_.1), channel_id=1, source_target_pairs={{0,8},{1,17},{2,10},{3,19},{4,12},{5,21},{6,14},{7,23},{8,0},{9,25... | collective-permute-start | bytes 6291464 | tf_op jit(solution)/shard_map/ppermute | solution.py:893
  141.3 43.9 %collective-permute-start.14 = (bf16[256,4096]{1,0:T(8,128)(2,1)}, bf16[256,4096]{1,0:T(8,128)(2,1)}, u32[]{:S(2)}, u32[]{:S(2)}) collective-permute-start(bf16[256,4096]{1,0:T(8,128)(2,1)} %collective-permute-done.12.refs_1_), channel_id=1, source_target_pairs={{0,1},{1,0},{2,3},{3,2},{4,5},{5,4},{6,7},{7,6},{8,9},{9,8},{10,11... | collective-permute-start | bytes 6291464 | tf_op jit(solution)/shard_map/ppermute | solution.py:897
  143.0 28.9 %collective-permute-start.15 = (bf16[128,4096]{1,0:T(8,128)(2,1)S(1)}, bf16[128,4096]{1,0:T(8,128)(2,1)}, u32[]{:S(2)}, u32[]{:S(2)}) collective-permute-start(bf16[128,4096]{1,0:T(8,128)(2,1)S(1)} %constant_dynamic-slice_fusion.1), channel_id=1, source_target_pairs={{0,16},{1,9},{2,18},{3,11},{4,20},{5,13},{6,22},{7,15},{8,24},{9,1... | collective-permute-start | bytes 3145736 | tf_op jit(solution)/shard_map/ppermute | solution.py:904
  171.9 30.1 %collective-permute-start.18 = (bf16[1024,1024]{1,0:T(8,128)(2,1)}, bf16[1024,1024]{1,0:T(8,128)(2,1)}, u32[]{:S(2)}, u32[]{:S(2)}) collective-permute-start(bf16[1024,1024]{1,0:T(8,128)(2,1)} %collective-permute-done.17.refs_6_), channel_id=1, source_target_pairs={{0,1},{1,0},{2,3},{3,2},{4,5},{5,4},{6,7},{7,6},{8,9},{9,8},{10,11... | collective-permute-start | bytes 6291464 | tf_op jit(solution)/shard_map/ppermute | solution.py:897
  221.0 33.7 %collective-permute-start.21 = (bf16[128,1024]{1,0:T(8,128)(2,1)S(1)}, bf16[128,1024]{1,0:T(8,128)(2,1)S(1)}, u32[]{:S(2)}, u32[]{:S(2)}) collective-permute-start(bf16[128,1024]{1,0:T(8,128)(2,1)S(1)} %get-tuple-element.277), channel_id=1, source_target_pairs={{0,2},{1,3},{2,0},{3,1},{4,6},{5,7},{6,4},{7,5},{8,10},{9,11},{10,... | collective-permute-start | bytes 786440 | tf_op jit(solution)/shard_map/ppermute | solution.py:1097
  223.0 31.6 %collective-permute-start.22 = (bf16[128,1024]{1,0:T(8,128)(2,1)S(1)}, bf16[128,1024]{1,0:T(8,128)(2,1)S(1)}, u32[]{:S(2)}, u32[]{:S(2)}) collective-permute-start(bf16[128,1024]{1,0:T(8,128)(2,1)S(1)} %get-tuple-element.276), channel_id=1, source_target_pairs={{0,4},{1,5},{2,6},{3,7},{4,0},{5,1},{6,2},{7,3},{8,12},{9,13},{10,... | collective-permute-start | bytes 786440 | tf_op jit(solution)/shard_map/ppermute | solution.py:1097
  225.4 29.3 %collective-permute-start.23 = (bf16[128,1024]{1,0:T(8,128)(2,1)S(1)}, bf16[128,1024]{1,0:T(8,128)(2,1)S(1)}, u32[]{:S(2)}, u32[]{:S(2)}) collective-permute-start(bf16[128,1024]{1,0:T(8,128)(2,1)S(1)} %get-tuple-element.275), channel_id=1, source_target_pairs={{0,6},{1,7},{2,4},{3,5},{4,2},{5,3},{6,0},{7,1},{8,14},{9,15},{10,... | collective-permute-start | bytes 786440 | tf_op jit(solution)/shard_map/ppermute | solution.py:1097
  263.9 154.5 %reduce-scatter.5.cloned.1.call-start = ((), (), s32[]{:S(2)}) async-start(), calls=%async_computation.6 | async-start | bytes 655360 | tf_op jit(solution)/shard_map/reduce_scatter | solution.py:998
  327.4 41.3 %collective-permute-start.28 = (bf16[128,1024]{1,0:T(8,128)(2,1)S(1)}, bf16[128,1024]{1,0:T(8,128)(2,1)S(1)}, u32[]{:S(2)}, u32[]{:S(2)}) collective-permute-start(bf16[128,1024]{1,0:T(8,128)(2,1)S(1)} %get-tuple-element.271), channel_id=1, source_target_pairs={{0,2},{1,3},{2,0},{3,1},{4,6},{5,7},{6,4},{7,5},{8,10},{9,11},{10,... | collective-permute-start | bytes 786440 | tf_op jit(solution)/shard_map/ppermute | solution.py:1097
  328.1 40.7 %collective-permute-start.29 = (bf16[128,1024]{1,0:T(8,128)(2,1)S(1)}, bf16[128,1024]{1,0:T(8,128)(2,1)S(1)}, u32[]{:S(2)}, u32[]{:S(2)}) collective-permute-start(bf16[128,1024]{1,0:T(8,128)(2,1)S(1)} %get-tuple-element.270), channel_id=1, source_target_pairs={{0,4},{1,5},{2,6},{3,7},{4,0},{5,1},{6,2},{7,3},{8,12},{9,13},{10,... | collective-permute-start | bytes 786440 | tf_op jit(solution)/shard_map/ppermute | solution.py:1097
  339.4 26.7 %collective-permute-start.27 = (bf16[2,128,2176]{2,1,0:T(8,128)(2,1)S(1)}, bf16[2,128,2176]{2,1,0:T(8,128)(2,1)S(1)}, u32[]{:S(2)}, u32[]{:S(2)}) collective-permute-start(bf16[2,128,2176]{2,1,0:T(8,128)(2,1)S(1)} %dynamic-slice_bitcast_fusion), channel_id=1, source_target_pairs={{0,16},{8,24},{16,0},{24,8},{1,17},{9,25},{17,1},{25,9},{2,18},{10... | collective-permute-start | bytes 3342344 | tf_op jit(solution)/shard_map/ppermute | solution.py:1018
  341.0 26.4 %collective-permute-start.26 = (bf16[2,128,2176]{2,1,0:T(8,128)(2,1)S(1)}, bf16[2,128,2176]{2,1,0:T(8,128)(2,1)S(1)}, u32[]{:S(2)}, u32[]{:S(2)}) collective-permute-start(bf16[2,128,2176]{2,1,0:T(8,128)(2,1)S(1)} %dynamic-slice_bitcast_fusion.1), channel_id=1, source_target_pairs={{0,8},{8,0},{16,24},{24,16},{1,9},{9,1},{17,25},{25,17},{2,10},{10... | collective-permute-start | bytes 3342344 | tf_op jit(solution)/shard_map/ppermute | solution.py:1017
  373.2 43.8 %collective-permute-start.36 = (bf16[128,1024]{1,0:T(8,128)(2,1)S(1)}, bf16[128,1024]{1,0:T(8,128)(2,1)}, u32[]{:S(2)}, u32[]{:S(2)}) collective-permute-start(bf16[128,1024]{1,0:T(8,128)(2,1)S(1)} %get-tuple-element.269), channel_id=1, source_target_pairs={{0,6},{1,7},{2,4},{3,5},{4,2},{5,3},{6,0},{7,1},{8,14},{9,15},{10,... | collective-permute-start | bytes 786440 | tf_op jit(solution)/shard_map/ppermute | solution.py:1097
  402.9 39.5 %collective-permute-start.37 = (bf16[512,3072]{1,0:T(8,128)(2,1)}, bf16[512,3072]{1,0:T(8,128)(2,1)}, u32[]{:S(2)}, u32[]{:S(2)}) collective-permute-start(bf16[512,3072]{1,0:T(8,128)(2,1)} %get-tuple-element.170), channel_id=1, source_target_pairs={{0,1},{1,0},{2,3},{3,2},{4,5},{5,4},{6,7},{7,6},{8,9},{9,8},{10,11... | collective-permute-start | bytes 9437192 | tf_op jit(solution)/shard_map/ppermute | solution.py:1010
  408.4 32.2 %collective-permute-start.40 = (bf16[2,32,4352]{2,1,0:T(8,128)(2,1)S(1)}, bf16[2,32,4352]{2,1,0:T(8,128)(2,1)S(1)}, u32[]{:S(2)}, u32[]{:S(2)}) collective-permute-start(bf16[2,32,4352]{2,1,0:T(8,128)(2,1)S(1)} %dynamic-slice_bitcast_fusion.4), channel_id=1, source_target_pairs={{0,2},{1,3},{2,0},{3,1},{4,6},{5,7},{6,4},{7,5},{8,10},{9,11},{10,... | collective-permute-start | bytes 1671176 | tf_op jit(solution)/shard_map/ppermute | solution.py:1034
  (86 other events, 1001.6 us)
Sparse Core Ops, SparseCore 0:
  264.0 50.7 reduce-scatter.2
  376.8 23.9 reduce-scatter.4

commit v7 on v6

--- a/solution.py
+++ b/solution.py
@@ -1364,7 +1364,7 @@
             )
         )
         grad_source = set_down(grad_source, late.send)
-        late.keep = after(late.keep, inner_sums.plane_two(), grad_source, *grad_target[1:])
+        late.keep = after(late.keep, inner_sums.plane_two(), grad_source, grad_target[1])
         late.core()
         late.plane_one()
         late.one, late.two, *_ = lax.optimization_barrier(

time: 506 us -> 508 us (level)
  waiting for transfers between devices: 110 us -> 117 us
  starting transfers between devices: 62.4 us -> 57 us
    ppermute x2, waiting for transfers between devices: 8.21 us -> 27.7 us  [z_two(): lax.ppermute(take(self.item, 1 - self.high, 0), 'seq', swap_pairs(8, 4))]
    ppermute x2, waiting for transfers between devices: 13.8 us -> 3.38 us  [plane_one(): from_y = lax.ppermute(take(self.two, 1 - y, 0), 'dp', swap_pairs(4, 2))]
  transfers between devices with their start and end apart: 51 -> 51, of which waited for: 24 -> 21; matrix products, arithmetic and copies ran while one was open for 9% -> 9% of each run, Pallas kernels for 41% -> 41%
where the time goes in v7:
time: 508 us; the launch traced here: 501 us
  Pallas kernels  244 us (48%)
  waiting for transfers between devices  117 us (23%)
  starting transfers between devices  57 us (11%)
  local copies, waits for them, and re-layouts  47.3 us (9%)
  other arithmetic  20.3 us (4%)
  between operations  15.4 us (3%)
    pallas_call x17, Pallas kernels, run(): pl.pallas_call(kernel, grid_spec=pltpu.PrefetchScalarGridSpec(num_scalar_...  152 us
    pallas_call x3, Pallas kernels, attend_backward(): pl.pallas_call(functools.partial(backward_kernel, pieces, block, causal,...  51.2 us
    pallas_call x2, Pallas kernels, attend_forward(): pl.pallas_call(functools.partial(forward_kernel, pieces, block, causal),...  40.7 us
    unnamed x132, local copies, waits for them, and re-layouts  29.2 us
    ppermute x2, waiting for transfers between devices, z_two(): lax.ppermute(take(self.item, 1 - self.high, 0), 'seq', swap_pairs(8, 4))  27.7 us
    ppermute x4, waiting for transfers between devices, gather_near(): return parts + (lax.ppermute(half_one, ('dp', 'seq'), by_core(2, 1)),)  22.4 us
    ppermute x3, waiting for transfers between devices, body(): lax.ppermute(vectors, 'dp', swap_pairs(4, bit))  19 us
    ppermute x9, waiting for transfers between devices, send_back(): parts.append(lax.ppermute(take(item, which ^ bit, 0), 'seq', pairs))  14.7 us
  transfers between devices with their start and end apart: 51, of which 21 were waited for; matrix products, arithmetic and copies ran while one was open for 9% of the time, Pallas kernels for 41%

profile of v7, /device:TPU:0, one launch (start us, length us, event | category | flops | bytes accessed | tf_op | source)
XLA Modules:
  0.0 501.2 jit_solution(9495443517778256338)
XLA Ops:
  29.4 17.5 %collective-permute-done.2 = bf16[6,256]{1,0:T(8,128)(2,1)S(1)} collective-permute-done((bf16[6,256]{1,0:T(8,128)(2,1)S(1)}, bf16[6,256]{1,0:T(8,128)(2,1)S(1)}, u32[]{:S(2)}, u32[]{:S(2)}) %collective-permute-start.2) | collective-permute-done | bytes 3104 | tf_op jit(solution)/shard_map/ppermute | solution.py:1139
  49.4 17.1 %collective-permute-done.5.refs_3_.refs_5_.refs_6_ = bf16[128,5120]{1,0:T(8,128)(2,1)} collective-permute-done((bf16[128,5120]{1,0:T(8,128)(2,1)S(1)}, bf16[128,5120]{1,0:T(8,128)(2,1)}, u32[]{:S(2)}, u32[]{:S(2)}) %collective-permute-start.5) | collective-permute-done | bytes 1310752 | tf_op jit(solution)/shard_map/ppermute | solution.py:904
  69.9 5.9 %self_kv.1.refs_3_.refs_5_.refs_6_.refs_8_ = bf16[512,2048]{1,0:T(8,128)(2,1)S(1)} custom-call(s32[16]{0:T(128)S(1)} %stack.123.place, bf16[512,1024]{1,0:T(8,128)(2,1)} %bitcast.18.left_ref.resid_ref.refs_0_.refs_1_.refs_2_, bf16[256,5120]{1,0:T(8,128)(2,1)} %constant_dynamic-update-slice_fusion.refs_0_.refs_2_.refs_3_, bf16[256,5120]{1,0:T(8,128)(2,1)} %copy-done.25, ...), custom_call_target="tpu_custom_call" | custom-call | flops 5750000128 | bytes 18000000 | tf_op jit(solution)/shard_map/self_kv/pallas_call | solution.py:332
  97.3 18.2 %attend_forward.2 = (bf16[512,1024]{1,0:T(8,128)(2,1)S(1)}, f32[8,2,512]{2,1,0:T(2,128)S(1)}) custom-call(bf16[512,1024]{1,0:T(8,128)(2,1)S(1)} %self_q.1.refs_0_, s32[2,512,1]{2,1,0:T(8,128)S(1)} %get-tuple-element.283.refs_1_.refs_4_, s32[1,512]{1,0:T(1,128)S(1)} %multiply_add_fusion.refs_2_.refs_5_, ...), custom_call_target="tpu_custom_call" | custom-call | flops 20700000256 | bytes 64800000 | tf_op jit(solution)/shard_map/attend_forward/pallas_call | solution.py:161
  116.6 6.8 %cross_kv.1.refs_3_.refs_5_.refs_6_.refs_8_ = bf16[512,2048]{1,0:T(8,128)(2,1)} custom-call(s32[16]{0:T(128)S(1)} %stack.123.place, bf16[512,1024]{1,0:T(8,128)(2,1)} %bitcast.23.left_ref.refs_0_.refs_1_, bf16[256,5120]{1,0:T(8,128)(2,1)} %constant_dynamic-update-slice_fusion.refs_0_.refs_2_.refs_3_, bf16[256,5120]{1,0:T(8,128)(2,1)} %copy-done.25, ...), custom_call_target="tpu_custom_call" | custom-call | flops 5750000128 | bytes 18000000 | tf_op jit(solution)/shard_map/cross_kv/pallas_call | solution.py:332
  131.9 9.5 %mix_self.1 = (f32[512,1024]{1,0:T(8,128)}, f32[512,1024]{1,0:T(8,128)}, bf16[512,1024]{1,0:T(8,128)(2,1)}, bf16[512,1024]{1,0:T(8,128)(2,1)S(1)}) custom-call(s32[16]{0:T(128)S(1)} %stack.123.place, bf16[512,1024]{1,0:T(8,128)(2,1)} %copy-done.4, bf16[512,1024]{1,0:T(8,128)(2,1)} %bitcast.18.left_ref.resid_ref.refs_0_.refs_1_.refs_2_, ...), custom_call_target="tpu_custom_call" | custom-call | flops 7245000192 | bytes 22680000 | tf_op jit(solution)/shard_map/mix_self/pallas_call | solution.py:332
  143.8 22.4 %attend_forward.3 = (bf16[512,1024]{1,0:T(8,128)(2,1)S(1)}, f32[8,2,512]{2,1,0:T(2,128)S(1)}) custom-call(bf16[512,1024]{1,0:T(8,128)(2,1)S(1)} %get-tuple-element.111.refs_0_, s32[2,512,1]{2,1,0:T(8,128)S(1)} %get-tuple-element.282.refs_1_.refs_4_, s32[1,512]{1,0:T(1,128)S(1)} %broadcast_in_dim.12.refs_2_.refs_5_, ...), custom_call_target="tpu_custom_call" | custom-call | flops 25300000768 | bytes 79200000 | tf_op jit(solution)/shard_map/attend_forward/pallas_call | solution.py:161
  172.4 7.5 %mix_cross.1 = (f32[512,1024]{1,0:T(8,128)}, f32[512,1024]{1,0:T(8,128)}, bf16[512,1024]{1,0:T(8,128)(2,1)}) custom-call(s32[16]{0:T(128)S(1)} %stack.123.place, bf16[512,1024]{1,0:T(8,128)(2,1)} %copy-done.13, f32[512,1024]{1,0:T(8,128)} %get-tuple-element.114.resid_ref, f32[2,1024]{1,0:T(2,128)S(1)} %get-tuple-element.292.norm_ref, ...), custom_call_target="tpu_custom_call" | custom-call | flops 4600000000 | bytes 14400000 | tf_op jit(solution)/shard_map/mix_cross/pallas_call | solution.py:332
  179.9 5.3 %collective-permute-done.19.refs_6_.refs_8_ = bf16[512,1024]{1,0:T(8,128)(2,1)} collective-permute-done((bf16[512,1024]{1,0:T(8,128)(2,1)}, bf16[512,1024]{1,0:T(8,128)(2,1)}, u32[]{:S(2)}, u32[]{:S(2)}) %collective-permute-start.19) | collective-permute-done | bytes 1048608 | tf_op jit(solution)/shard_map/ppermute | solution.py:904
  185.2 15.5 %feed_first.1 = (f32[512,1024]{1,0:T(8,128)S(1)}, bf16[512,2048]{1,0:T(8,128)(2,1)}, bf16[512,512]{1,0:T(8,128)(2,1)}, bf16[512,512]{1,0:T(8,128)(2,1)}) custom-call(s32[16]{0:T(128)S(1)} %stack.123.place, bf16[512,1024]{1,0:T(8,128)(2,1)} %get-tuple-element.115.low_ref.refs_2_, f32[512,1024]{1,0:T(8,128)} %get-tuple-element.116.second_ref, ...), custom_call_target="tpu_custom_call" | custom-call | flops 14949999616 | bytes 46800000 | tf_op jit(solution)/shard_map/feed_first/pallas_call | solution.py:332
  203.0 15.1 %feed_second.1 = (bf16[512,1024]{1,0:T(8,128)(2,1)}, f32[512,1024]{1,0:T(8,128)S(1)}, bf16[512,1024]{1,0:T(8,128)(2,1)S(1)}, f32[2,1024]{1,0:T(2,128)}, bf16[512,2048]{1,0:T(8,128)(2,1)}) custom-call(s32[16]{0:T(128)S(1)} %stack.123.place, bf16[512,1024]{1,0:T(8,128)(2,1)} %get-tuple-element.115.low_ref.refs_2_, f32[512,1024]{1,0:T(8,128)} %copy-done.19, ...), custom_call_target="tpu_custom_call" | custom-call | flops 15525000192 | bytes 48600000 | tf_op jit(solution)/shard_map/feed_second/pallas_call | solution.py:332
  225.5 29.2 %feed_backward.1 = (f32[512,1024]{1,0:T(8,128)}, bf16[512,1024]{1,0:T(8,128)(2,1)}, f32[2,1024]{1,0:T(2,128)}, bf16[512,512]{1,0:T(8,128)(2,1)}, bf16[512,1024]{1,0:T(8,128)(2,1)}) custom-call(s32[16]{0:T(128)} %copy-done.11, bf16[512,1024]{1,0:T(8,128)(2,1)} %copy-done.15, f32[512,1024]{1,0:T(8,128)} %copy-done.20, ...), custom_call_target="tpu_custom_call" | custom-call | flops 33350000640 | bytes 104400000 | tf_op jit(solution)/shard_map/feed_backward/pallas_call | solution.py:332
  256.1 7.8 %wgrad_early.1 = bf16[1024,2048]{1,0:T(8,128)(2,1)} custom-call(s32[16]{0:T(128)S(1)} %copy-done.12, bf16[512,1024]{1,0:T(8,128)(2,1)} %copy-done.13, bf16[512,1024]{1,0:T(8,128)(2,1)} %copy-done.13, bf16[512,1024]{1,0:T(8,128)(2,1)} %get-tuple-element.115.low_ref.refs_2_, bf16[512,512]{1,0:T(8,128)(2,1)} %get-tuple-element.130.refs_3_, ...), custom_call_target="tpu_custom_call" | custom-call | flops 3680000000 | bytes 11520000 | tf_op jit(solution)/shard_map/wgrad_early/pallas_call | solution.py:332
  267.6 26.9 %attend_backward.3 = (bf16[512,1024]{1,0:T(8,128)(2,1)}, f32[2,512,1024]{2,1,0:T(8,128)}, bf16[2,512,1024]{2,1,0:T(8,128)(2,1)}) custom-call(bf16[512,1024]{1,0:T(8,128)(2,1)S(1)} %copy-done.18, bf16[512,1024]{1,0:T(8,128)(2,1)S(1)} %copy-done.14, bf16[512,1024]{1,0:T(8,128)(2,1)S(1)} %copy-done.22, f32[8,2,512]{2,1,0:T(2,128)S(1)} %get-tuple-element.135.refs_3_, ...), custom_call_target="tpu_custom_call" | custom-call | flops 32199999488 | bytes 100800000 | tf_op jit(solution)/shard_map/attend_backward/pallas_call | solution.py:251
  294.5 10.1 %norm_step.1 = (f32[512,1024]{1,0:T(8,128)}, bf16[512,1024]{1,0:T(8,128)(2,1)S(1)}, f32[2,1024]{1,0:T(2,128)}, bf16[512,1024]{1,0:T(8,128)(2,1)S(1)}) custom-call(s32[16]{0:T(128)S(1)} %copy-done.12, bf16[512,1024]{1,0:T(8,128)(2,1)} %get-tuple-element.136.dquery_ref.refs_7_, f32[512,1024]{1,0:T(8,128)} %get-tuple-element.141.d_ref, ...), custom_call_target="tpu_custom_call" | custom-call | flops 7590000128 | bytes 23760000 | tf_op jit(solution)/shard_map/norm_step/pallas_call | solution.py:332
  306.8 6.2 %source_back.1 = bf16[512,1024]{1,0:T(8,128)(2,1)S(1)} custom-call(s32[16]{0:T(128)S(1)} %copy-done.12, bf16[2,512,1024]{2,1,0:T(8,128)(2,1)} %add_convert_fusion.3.refs_0_.refs_1_.refs_4_.refs_5_, bf16[2,512,1024]{2,1,0:T(8,128)(2,1)} %add_convert_fusion.3.refs_0_.refs_1_.refs_4_.refs_5_, ...), custom_call_target="tpu_custom_call" | custom-call | flops 6899999744 | bytes 21600000 | tf_op jit(solution)/shard_map/source_back/pallas_call | solution.py:332
  314.8 11.4 %wgrad_inner.1 = (bf16[512,4352]{1,0:T(8,128)(2,1)}, bf16[512,4352]{1,0:T(8,128)(2,1)}) custom-call(s32[16]{0:T(128)S(1)} %copy-done.12, bf16[512,1024]{1,0:T(8,128)(2,1)} %bitcast.23.left_ref.refs_0_.refs_1_, bf16[512,1024]{1,0:T(8,128)(2,1)} %bitcast.23.left_ref.refs_0_.refs_1_, bf16[512,1024]{1,0:T(8,128)(2,1)} %copy-done.4, ...), custom_call_target="tpu_custom_call" | custom-call | flops 7360000000 | bytes 23040000 | tf_op jit(solution)/shard_map/wgrad_inner/pallas_call | solution.py:332
  342.6 20.1 %attend_backward.4 = (bf16[512,1024]{1,0:T(8,128)(2,1)}, f32[2,512,1024]{2,1,0:T(8,128)}, bf16[2,512,1024]{2,1,0:T(8,128)(2,1)}) custom-call(bf16[512,1024]{1,0:T(8,128)(2,1)S(1)} %copy-done.1, bf16[512,1024]{1,0:T(8,128)(2,1)S(1)} %copy-done.5, bf16[512,1024]{1,0:T(8,128)(2,1)S(1)} %get-tuple-element.159.refs_2_, ...), custom_call_target="tpu_custom_call" | custom-call | flops 24149999616 | bytes 75600000 | tf_op jit(solution)/shard_map/attend_backward/pallas_call | solution.py:251
  381.8 8.9 %target_back.1 = bf16[512,1024]{1,0:T(8,128)(2,1)S(1)} custom-call(s32[16]{0:T(128)S(1)} %copy-done.12, bf16[512,1024]{1,0:T(8,128)(2,1)} %get-tuple-element.166.refs_0_.refs_3_, bf16[2,512,1024]{2,1,0:T(8,128)(2,1)} %add_convert_fusion.2.refs_1_.refs_2_.refs_4_.refs_5_, bf16[2,512,1024]{2,1,0:T(8,128)(2,1)} %add_convert_fusion.2.refs_1_.refs_2_.refs_4_.refs_5_, ...), custom_call_target="tpu_custom_call" | custom-call | flops 10350000128 | bytes 32400000 | tf_op jit(solution)/shard_map/target_back/pallas_call | solution.py:332
  393.8 9.1 %wgrad_self.1 = (bf16[512,3072]{1,0:T(8,128)(2,1)}, bf16[512,3072]{1,0:T(8,128)(2,1)}) custom-call(s32[16]{0:T(128)S(1)} %copy-done.12, bf16[512,1024]{1,0:T(8,128)(2,1)} %bitcast.18.left_ref.resid_ref.refs_0_.refs_1_.refs_2_, bf16[512,1024]{1,0:T(8,128)(2,1)} %bitcast.18.left_ref.resid_ref.refs_0_.refs_1_.refs_2_, ...), custom_call_target="tpu_custom_call" | custom-call | flops 5520000000 | bytes 17280000 | tf_op jit(solution)/shard_map/wgrad_self/pallas_call | solution.py:332
  418.3 12.9 %collective-permute-done.36.refs_2_ = bf16[128,1024]{1,0:T(8,128)(2,1)} collective-permute-done((bf16[128,1024]{1,0:T(8,128)(2,1)S(1)}, bf16[128,1024]{1,0:T(8,128)(2,1)}, u32[]{:S(2)}, u32[]{:S(2)}) %collective-permute-start.36) | collective-permute-done | bytes 262176 | tf_op jit(solution)/shard_map/ppermute | solution.py:1097
  443.8 22.8 %collective-permute-done.43 = bf16[32,4352]{1,0:T(8,128)(2,1)S(1)} collective-permute-done((bf16[32,4352]{1,0:T(8,128)(2,1)S(1)}, bf16[32,4352]{1,0:T(8,128)(2,1)S(1)}, u32[]{:S(2)}, u32[]{:S(2)}) %collective-permute-start.43) | collective-permute-done | bytes 278560 | tf_op jit(solution)/shard_map/ppermute | solution.py:1039
  470.4 5.1 %collective-permute-done.41 = bf16[128,1536]{1,0:T(8,128)(2,1)S(1)} collective-permute-done((bf16[128,1536]{1,0:T(8,128)(2,1)S(1)}, bf16[128,1536]{1,0:T(8,128)(2,1)S(1)}, u32[]{:S(2)}, u32[]{:S(2)}) %collective-permute-start.41) | collective-permute-done | bytes 393248 | tf_op jit(solution)/shard_map/ppermute | solution.py:1025
  480.5 5.0 collective-permute-done.44
  (304 shorter events, 169.9 us)
Async XLA Ops:
  13.9 34.7 %collective-permute-start = (bf16[256,5120]{1,0:T(8,128)(2,1)}, bf16[256,5120]{1,0:T(8,128)(2,1)S(1)}, u32[]{:S(2)}, u32[]{:S(2)}) collective-permute-start(bf16[256,5120]{1,0:T(8,128)(2,1)} %constant_dynamic-update-slice_fusion.refs_0_.refs_2_.refs_3_), channel_id=1, source_target_pairs={{0,8},{1,17},{2,10},{3,19},{4,12},{5,21},{6,14},{7,23},{8,0},{9,25... | collective-permute-start | bytes 7864328 | tf_op jit(solution)/shard_map/ppermute | solution.py:893
  18.2 30.4 %all-to-all-start = ((bf16[4,128,1024]{2,1,0:T(8,128)(2,1)}), bf16[4,128,1024]{2,1,0:T(8,128)(2,1)}, u32[]{:S(2)}, u32[]{:S(2)}) async-start(bf16[4,128,1024]{2,1,0:T(8,128)(2,1)} %bitcast.149), calls=%async_computation | async-start | bytes 2097152 | tf_op jit(solution)/shard_map/all_to_all | solution.py:1086
  77.2 39.3 %all-to-all-start.1 = ((bf16[4,128,1024]{2,1,0:T(8,128)(2,1)}), bf16[4,128,1024]{2,1,0:T(8,128)(2,1)}, u32[]{:S(2)}, u32[]{:S(2)}) async-start(bf16[4,128,1024]{2,1,0:T(8,128)(2,1)} %bitcast.135), calls=%async_computation.1 | async-start | bytes 2097152 | tf_op jit(solution)/shard_map/all_to_all | solution.py:1086
  95.3 28.0 %collective-permute-start.10 = (bf16[128,4096]{1,0:T(8,128)(2,1)}, bf16[128,4096]{1,0:T(8,128)(2,1)}, u32[]{:S(2)}, u32[]{:S(2)}) collective-permute-start(bf16[128,4096]{1,0:T(8,128)(2,1)} %constant_dynamic-slice_fusion.2), channel_id=1, source_target_pairs={{0,16},{1,9},{2,18},{3,11},{4,20},{5,13},{6,22},{7,15},{8,24},{9,1... | collective-permute-start | bytes 3145736 | tf_op jit(solution)/shard_map/ppermute | solution.py:904
  95.8 36.0 %collective-permute-start.9 = (bf16[256,4096]{1,0:T(8,128)(2,1)}, bf16[256,4096]{1,0:T(8,128)(2,1)}, u32[]{:S(2)}, u32[]{:S(2)}) collective-permute-start(bf16[256,4096]{1,0:T(8,128)(2,1)} %collective-permute-done.7.refs_1_.refs_6_.refs_8_.refs_13_.refs_11_.refs_16_.refs_21_), channel_id=1, source_target_pairs={{0,1},{1,0},{2,3},{3,2},{4,5},{5,4},{6,7},{7,6},{8,9},{9,8},{10,11... | collective-permute-start | bytes 6291464 | tf_op jit(solution)/shard_map/ppermute | solution.py:897
  96.2 45.2 %collective-permute-start.12 = (bf16[256,4096]{1,0:T(8,128)(2,1)}, bf16[256,4096]{1,0:T(8,128)(2,1)}, u32[]{:S(2)}, u32[]{:S(2)}) collective-permute-start(bf16[256,4096]{1,0:T(8,128)(2,1)} %refs_0_.2), channel_id=1, source_target_pairs={{0,8},{1,17},{2,10},{3,19},{4,12},{5,21},{6,14},{7,23},{8,0},{9,25... | collective-permute-start | bytes 6291464 | tf_op jit(solution)/shard_map/ppermute | solution.py:893
  125.2 47.2 %all-to-all-start.2 = ((bf16[4,128,1024]{2,1,0:T(8,128)(2,1)}), bf16[4,128,1024]{2,1,0:T(8,128)(2,1)}, u32[]{:S(2)}, u32[]{:S(2)}) async-start(bf16[4,128,1024]{2,1,0:T(8,128)(2,1)} %bitcast.148), calls=%async_computation.2 | async-start | bytes 2097152 | tf_op jit(solution)/shard_map/all_to_all | solution.py:1086
  129.9 185.0 %reduce-scatter.3.cloned.1.call-start = ((), (), s32[]{:S(2)}) async-start(), calls=%async_computation.5 | async-start | bytes 4718592 | tf_op jit(solution)/shard_map/reduce_scatter | solution.py:998
  130.5 37.3 %collective-permute-start.17 = (bf16[1024,1024]{1,0:T(8,128)(2,1)}, bf16[1024,1024]{1,0:T(8,128)(2,1)}, u32[]{:S(2)}, u32[]{:S(2)}) collective-permute-start(bf16[1024,1024]{1,0:T(8,128)(2,1)} %refs_5_.1), channel_id=1, source_target_pairs={{0,8},{1,17},{2,10},{3,19},{4,12},{5,21},{6,14},{7,23},{8,0},{9,25... | collective-permute-start | bytes 6291464 | tf_op jit(solution)/shard_map/ppermute | solution.py:893
  141.3 43.9 %collective-permute-start.14 = (bf16[256,4096]{1,0:T(8,128)(2,1)}, bf16[256,4096]{1,0:T(8,128)(2,1)}, u32[]{:S(2)}, u32[]{:S(2)}) collective-permute-start(bf16[256,4096]{1,0:T(8,128)(2,1)} %collective-permute-done.12.refs_1_), channel_id=1, source_target_pairs={{0,1},{1,0},{2,3},{3,2},{4,5},{5,4},{6,7},{7,6},{8,9},{9,8},{10,11... | collective-permute-start | bytes 6291464 | tf_op jit(solution)/shard_map/ppermute | solution.py:897
  143.0 28.9 %collective-permute-start.15 = (bf16[128,4096]{1,0:T(8,128)(2,1)S(1)}, bf16[128,4096]{1,0:T(8,128)(2,1)}, u32[]{:S(2)}, u32[]{:S(2)}) collective-permute-start(bf16[128,4096]{1,0:T(8,128)(2,1)S(1)} %constant_dynamic-slice_fusion.1), channel_id=1, source_target_pairs={{0,16},{1,9},{2,18},{3,11},{4,20},{5,13},{6,22},{7,15},{8,24},{9,1... | collective-permute-start | bytes 3145736 | tf_op jit(solution)/shard_map/ppermute | solution.py:904
  171.9 30.1 %collective-permute-start.18 = (bf16[1024,1024]{1,0:T(8,128)(2,1)}, bf16[1024,1024]{1,0:T(8,128)(2,1)}, u32[]{:S(2)}, u32[]{:S(2)}) collective-permute-start(bf16[1024,1024]{1,0:T(8,128)(2,1)} %collective-permute-done.17.refs_6_), channel_id=1, source_target_pairs={{0,1},{1,0},{2,3},{3,2},{4,5},{5,4},{6,7},{7,6},{8,9},{9,8},{10,11... | collective-permute-start | bytes 6291464 | tf_op jit(solution)/shard_map/ppermute | solution.py:897
  221.0 33.7 %collective-permute-start.21 = (bf16[128,1024]{1,0:T(8,128)(2,1)S(1)}, bf16[128,1024]{1,0:T(8,128)(2,1)S(1)}, u32[]{:S(2)}, u32[]{:S(2)}) collective-permute-start(bf16[128,1024]{1,0:T(8,128)(2,1)S(1)} %get-tuple-element.277), channel_id=1, source_target_pairs={{0,2},{1,3},{2,0},{3,1},{4,6},{5,7},{6,4},{7,5},{8,10},{9,11},{10,... | collective-permute-start | bytes 786440 | tf_op jit(solution)/shard_map/ppermute | solution.py:1097
  223.0 31.6 %collective-permute-start.22 = (bf16[128,1024]{1,0:T(8,128)(2,1)S(1)}, bf16[128,1024]{1,0:T(8,128)(2,1)S(1)}, u32[]{:S(2)}, u32[]{:S(2)}) collective-permute-start(bf16[128,1024]{1,0:T(8,128)(2,1)S(1)} %get-tuple-element.276), channel_id=1, source_target_pairs={{0,4},{1,5},{2,6},{3,7},{4,0},{5,1},{6,2},{7,3},{8,12},{9,13},{10,... | collective-permute-start | bytes 786440 | tf_op jit(solution)/shard_map/ppermute | solution.py:1097
  225.4 29.3 %collective-permute-start.23 = (bf16[128,1024]{1,0:T(8,128)(2,1)S(1)}, bf16[128,1024]{1,0:T(8,128)(2,1)S(1)}, u32[]{:S(2)}, u32[]{:S(2)}) collective-permute-start(bf16[128,1024]{1,0:T(8,128)(2,1)S(1)} %get-tuple-element.275), channel_id=1, source_target_pairs={{0,6},{1,7},{2,4},{3,5},{4,2},{5,3},{6,0},{7,1},{8,14},{9,15},{10,... | collective-permute-start | bytes 786440 | tf_op jit(solution)/shard_map/ppermute | solution.py:1097
  263.9 153.7 %reduce-scatter.5.cloned.1.call-start = ((), (), s32[]{:S(2)}) async-start(), calls=%async_computation.6 | async-start | bytes 655360 | tf_op jit(solution)/shard_map/reduce_scatter | solution.py:998
  327.4 41.3 %collective-permute-start.28 = (bf16[128,1024]{1,0:T(8,128)(2,1)S(1)}, bf16[128,1024]{1,0:T(8,128)(2,1)S(1)}, u32[]{:S(2)}, u32[]{:S(2)}) collective-permute-start(bf16[128,1024]{1,0:T(8,128)(2,1)S(1)} %get-tuple-element.271), channel_id=1, source_target_pairs={{0,2},{1,3},{2,0},{3,1},{4,6},{5,7},{6,4},{7,5},{8,10},{9,11},{10,... | collective-permute-start | bytes 786440 | tf_op jit(solution)/shard_map/ppermute | solution.py:1097
  328.1 40.7 %collective-permute-start.29 = (bf16[128,1024]{1,0:T(8,128)(2,1)S(1)}, bf16[128,1024]{1,0:T(8,128)(2,1)S(1)}, u32[]{:S(2)}, u32[]{:S(2)}) collective-permute-start(bf16[128,1024]{1,0:T(8,128)(2,1)S(1)} %get-tuple-element.270), channel_id=1, source_target_pairs={{0,4},{1,5},{2,6},{3,7},{4,0},{5,1},{6,2},{7,3},{8,12},{9,13},{10,... | collective-permute-start | bytes 786440 | tf_op jit(solution)/shard_map/ppermute | solution.py:1097
  339.4 26.7 %collective-permute-start.27 = (bf16[2,128,2176]{2,1,0:T(8,128)(2,1)S(1)}, bf16[2,128,2176]{2,1,0:T(8,128)(2,1)S(1)}, u32[]{:S(2)}, u32[]{:S(2)}) collective-permute-start(bf16[2,128,2176]{2,1,0:T(8,128)(2,1)S(1)} %dynamic-slice_bitcast_fusion), channel_id=1, source_target_pairs={{0,16},{8,24},{16,0},{24,8},{1,17},{9,25},{17,1},{25,9},{2,18},{10... | collective-permute-start | bytes 3342344 | tf_op jit(solution)/shard_map/ppermute | solution.py:1018
  402.9 36.0 %collective-permute-start.37 = (bf16[512,3072]{1,0:T(8,128)(2,1)}, bf16[512,3072]{1,0:T(8,128)(2,1)}, u32[]{:S(2)}, u32[]{:S(2)}) collective-permute-start(bf16[512,3072]{1,0:T(8,128)(2,1)} %get-tuple-element.170), channel_id=1, source_target_pairs={{0,1},{1,0},{2,3},{3,2},{4,5},{5,4},{6,7},{7,6},{8,9},{9,8},{10,11... | collective-permute-start | bytes 9437192 | tf_op jit(solution)/shard_map/ppermute | solution.py:1010
  408.4 27.8 %collective-permute-start.40 = (bf16[2,32,4352]{2,1,0:T(8,128)(2,1)S(1)}, bf16[2,32,4352]{2,1,0:T(8,128)(2,1)S(1)}, u32[]{:S(2)}, u32[]{:S(2)}) collective-permute-start(bf16[2,32,4352]{2,1,0:T(8,128)(2,1)S(1)} %dynamic-slice_bitcast_fusion.4), channel_id=1, source_target_pairs={{0,2},{1,3},{2,0},{3,1},{4,6},{5,7},{6,4},{7,5},{8,10},{9,11},{10,... | collective-permute-start | bytes 1671176 | tf_op jit(solution)/shard_map/ppermute | solution.py:1034
  431.2 35.8 %collective-permute-start.32 = (bf16[128,1024]{1,0:T(8,128)(2,1)}, bf16[128,1024]{1,0:T(8,128)(2,1)S(1)}, u32[]{:S(2)}, u32[]{:S(2)}) collective-permute-start(bf16[128,1024]{1,0:T(8,128)(2,1)} %get-tuple-element.273), channel_id=1, source_target_pairs={{0,4},{1,5},{2,6},{3,7},{4,0},{5,1},{6,2},{7,3},{8,12},{9,13},{10,... | collective-permute-start | bytes 786440 | tf_op jit(solution)/shard_map/ppermute | solution.py:1097
  431.2 35.9 %collective-permute-start.33 = (bf16[128,1024]{1,0:T(8,128)(2,1)}, bf16[128,1024]{1,0:T(8,128)(2,1)S(1)}, u32[]{:S(2)}, u32[]{:S(2)}) collective-permute-start(bf16[128,1024]{1,0:T(8,128)(2,1)} %get-tuple-element.272), channel_id=1, source_target_pairs={{0,6},{1,7},{2,4},{3,5},{4,2},{5,3},{6,0},{7,1},{8,14},{9,15},{10,... | collective-permute-start | bytes 786440 | tf_op jit(solution)/shard_map/ppermute | solution.py:1097
  436.4 30.2 %collective-permute-start.43 = (bf16[32,4352]{1,0:T(8,128)(2,1)S(1)}, bf16[32,4352]{1,0:T(8,128)(2,1)S(1)}, u32[]{:S(2)}, u32[]{:S(2)}) collective-permute-start(bf16[32,4352]{1,0:T(8,128)(2,1)S(1)} %dynamic-slice_bitcast_fusion.10), channel_id=1, source_target_pairs={{0,4},{1,5},{2,6},{3,7},{4,0},{5,1},{6,2},{7,3},{8,12},{9,13},{10,... | collective-permute-start | bytes 835592 | tf_op jit(solution)/shard_map/ppermute | solution.py:1039
  (86 other events, 998.1 us)
Sparse Core Ops, SparseCore 0:
  264.0 50.7 reduce-scatter.2
  373.3 26.3 reduce-scatter.4
